TPU v7x, 32 devices: a whole 2x2x4 slice. The times are simulated.
32 devices in a mesh: batch: 8 (over y, x, core), seq: 4 (over z).
Axes of the slice: x: 2, y: 2, z: 4, core: 2. Of those that a mesh axis runs over, the one named last changes fastest.
Arguments:
- patches: bfloat16 [16, 1024, 1152], P('batch', 'seq'), may hold values from -6 to 6
- timesteps: int32 [16], P('batch'), may hold values from 0 to 999
- labels: int32 [16], P('batch'), may hold values from 0 to 1000
- next_grad: bfloat16 [16, 1024, 1152], P('batch', 'seq'), may hold values from -6 to 6
- skip_grad: bfloat16 [16, 1024, 1152], P('batch', 'seq'), may hold values from -6 to 6
- next_extra: bfloat16 [16, 2, 1152], P('batch'), may hold values from -6 to 6
- skip_extra: bfloat16 [16, 2, 1152], P('batch'), may hold values from -6 to 6
- w_qkv: float32 [1152, 3456], P(None, ('batch', 'seq')), may hold values from -0.1875 to 0.1875
- w_proj: float32 [1152, 1152], P(None, ('batch', 'seq')), may hold values from -1.25 to 1.25
- w_up: float32 [1152, 4608], P(None, ('batch', 'seq')), may hold values from -0.1875 to 0.1875
- w_down: float32 [4608, 1152], P(('batch', 'seq')), may hold values from -0.09375 to 0.09375
- mom_qkv: float32 [1152, 3456], P(None, ('batch', 'seq'))
- mom_proj: float32 [1152, 1152], P(None, ('batch', 'seq'))
- mom_up: float32 [1152, 4608], P(None, ('batch', 'seq'))
- mom_down: float32 [4608, 1152], P(('batch', 'seq'))
- vectors: float32 [10, 1152], P(None, ('batch', 'seq'))
- vec_first: float32 [10, 1152], P(None, ('batch', 'seq')), may hold values from -64 to 64
- vec_second: float32 [10, 1152], P(None, ('batch', 'seq')), may hold values from 19.6992 to 73.872
- table: float32 [1001, 1152], P(None, ('batch', 'seq')), may hold values from -6 to 6
- table_first: float32 [1001, 1152], P(None, ('batch', 'seq')), may hold values from -2.5 to 2.5
- table_second: float32 [1001, 1152], P(None, ('batch', 'seq')), may hold values from 0.0022 to 0.009
Outputs:
- y_patches: bfloat16 [16, 1024, 1152], P('batch', 'seq')
- y_extras: bfloat16 [16, 2, 1152], P('batch')
- dx_patches: bfloat16 [16, 1024, 1152], P('batch', 'seq')
- w_qkv_new: float32 [1152, 3456], P(None, ('batch', 'seq'))
- w_proj_new: float32 [1152, 1152], P(None, ('batch', 'seq'))
- w_up_new: float32 [1152, 4608], P(None, ('batch', 'seq'))
- w_down_new: float32 [4608, 1152], P(('batch', 'seq'))
- mom_qkv_new: float32 [1152, 3456], P(None, ('batch', 'seq'))
- mom_proj_new: float32 [1152, 1152], P(None, ('batch', 'seq'))
- mom_up_new: float32 [1152, 4608], P(None, ('batch', 'seq'))
- mom_down_new: float32 [4608, 1152], P(('batch', 'seq'))
- vec_first_new: float32 [10, 1152], P(None, ('batch', 'seq'))
- vec_second_new: float32 [10, 1152], P(None, ('batch', 'seq'))
- vectors_new: float32 [10, 1152], P(None, ('batch', 'seq'))
- table_first_new: float32 [1001, 1152], P(None, ('batch', 'seq'))
- table_second_new: float32 [1001, 1152], P(None, ('batch', 'seq'))
- table_new: float32 [1001, 1152], P(None, ('batch', 'seq'))
All inputs are finite; a program needn't handle non-finite values.
Results may differ from a plain program's by a relative error of at most 0.02.
Values may be sent and summed in bfloat16 or wider, within the bound.
No kernel may reach another device: no remote copies, remote signals or barrier semaphores. Data moves between devices by JAX's collectives and lax.ppermute only.
A program may use at most 384 MiB of HBM per device.

v0:
```python
import math

import jax
import jax.numpy as jnp
from jax import lax
from jax.sharding import PartitionSpec as P

HEADS = 16
NS_STEPS = 5
STEP = 10


norm_eps = 1e-05
poly_first = 3.4445
poly_second = -4.775
poly_third = 2.0315
muon_momentum = 0.95
muon_rate = 1.5
muon_decay = 0.01
beta_one = 0.9
beta_two = 0.999
adam_rate = 1.0
adam_eps = 1e-08
highest = lax.Precision.HIGHEST


def broadcast(block, axis, owner):
    block = jnp.where(lax.axis_index(axis) == owner, block, jnp.zeros_like(block))
    return lax.psum(block, axis)


def matmul(former, latter):
    return jnp.dot(former, latter, preferred_element_type=jnp.float32)


def matmul_last(former, latter, precision=None):
    return lax.dot_general(
        former,
        latter,
        (((1,), (1,)), ((), ())),
        precision=precision,
        preferred_element_type=jnp.float32,
    )


def matmul_first(former, latter, precision=None):
    return lax.dot_general(
        former,
        latter,
        (((0,), (0,)), ((), ())),
        precision=precision,
        preferred_element_type=jnp.float32,
    )


def standardize(values):
    average = jnp.mean(values, axis=-1, keepdims=True)
    centred = values - average
    variance = jnp.mean(centred * centred, axis=-1, keepdims=True)
    return centred * lax.rsqrt(variance + norm_eps)


def gelu_exact(inputs):
    return jax.nn.gelu(inputs, approximate=False)


def time_tokens(step_values, model_width):
    half_width = model_width // 2
    frequency = jnp.exp(-math.log(10000.0) * jnp.arange(half_width, dtype=jnp.float32) / half_width)
    angles = step_values.astype(jnp.float32)[:, None] * frequency[None, :]
    return jnp.concatenate([jnp.cos(angles), jnp.sin(angles)], axis=-1)


def adam_step(parameter, first_state, second, gradient):
    first_new = beta_one * first_state + (1.0 - beta_one) * gradient
    second_new = beta_two * second + (1.0 - beta_two) * gradient * gradient
    first_hat = first_new / (1.0 - beta_one**STEP)
    second_hat = second_new / (1.0 - beta_two**STEP)
    return (
        first_new,
        second_new,
        parameter - adam_rate * first_hat / (jnp.sqrt(second_hat) + adam_eps),
    )


def body(
    patches,
    timesteps,
    labels,
    next_grad,
    skip_grad,
    next_extra,
    skip_extra,
    w_qkv,
    w_proj,
    w_up,
    w_down,
    mom_qkv,
    mom_proj,
    mom_up,
    mom_down,
    vectors,
    vec_first,
    vec_second,
    table,
    table_first,
    table_second,
):
    images, patch_rows, model_width = patches.shape
    token_count = patch_rows + 2
    row_count = images * token_count
    batch_count = lax.axis_size("batch")
    seq_count = lax.axis_size("seq")
    shards = batch_count * seq_count
    seq_rank = lax.axis_index("seq")
    batch_rank = lax.axis_index("batch")
    owner_ranks = [position * (batch_count - 1) // 3 for position in range(4)]
    full_qkv, full_proj, full_up, full_down, full_vec, full_table = (
        lax.all_gather(w_qkv.astype(jnp.bfloat16), ("batch", "seq"), axis=1, tiled=True),
        lax.all_gather(w_proj.astype(jnp.bfloat16), ("batch", "seq"), axis=1, tiled=True),
        lax.all_gather(w_up.astype(jnp.bfloat16), ("batch", "seq"), axis=1, tiled=True),
        lax.all_gather(w_down.astype(jnp.bfloat16), ("batch", "seq"), axis=0, tiled=True),
        lax.all_gather(vectors.astype(jnp.bfloat16), ("batch", "seq"), axis=1, tiled=True),
        lax.all_gather(table.astype(jnp.bfloat16), ("batch", "seq"), axis=1, tiled=True),
    )
    up_width = full_up.shape[1]
    vec_values = full_vec.astype(jnp.float32)
    up_bias = vec_values[6:].reshape(-1)
    counted = (seq_rank == 0).astype(jnp.float32)
    extra_weight = jnp.full((images, 2, 1), 1.0, jnp.float32) * counted
    row_weight = jnp.concatenate(
        [extra_weight, jnp.ones((images, patch_rows, 1), jnp.float32)], axis=1
    ).reshape(row_count, 1)
    row_low = row_weight.astype(jnp.bfloat16)
    class_count = full_table.shape[0]
    selector = (labels[:, None] == jnp.arange(class_count, dtype=jnp.int32)[None, :]).astype(
        jnp.float32
    )
    class_rows = matmul(selector.astype(jnp.bfloat16), full_table)
    extras = jnp.stack([time_tokens(timesteps, model_width), class_rows], axis=1)
    tokens = jnp.concatenate([extras, patches.astype(jnp.float32)], axis=1).reshape(
        row_count, model_width
    )
    standard_one = standardize(tokens)
    normed = (standard_one * vec_values[0] + vec_values[1]).astype(jnp.bfloat16)
    packed = matmul(normed, full_qkv).astype(jnp.bfloat16)
    packed_view = packed.reshape(images, token_count, 3, model_width)
    queries = packed_view[:, :, 0]
    keys_own = packed_view[:, :, 1]
    values_own = packed_view[:, :, 2]
    far_keys, far_values = (
        lax.all_gather(keys_own[:, 2:], "seq", axis=1, tiled=True),
        lax.all_gather(values_own[:, 2:], "seq", axis=1, tiled=True),
    )
    keys_all = jnp.concatenate([keys_own[:, :2], far_keys], axis=1)
    values_all = jnp.concatenate([values_own[:, :2], far_values], axis=1)
    key_count = keys_all.shape[1]
    head_count = HEADS
    head_size = model_width // head_count
    score_scale = head_size ** (-0.5)
    query_heads = queries.reshape(images, token_count, head_count, head_size)
    key_heads = keys_all.reshape(images, key_count, head_count, head_size)
    value_heads = values_all.reshape(images, key_count, head_count, head_size)
    scores = (
        jnp.einsum("gqhe,gkhe->ghqk", query_heads, key_heads, preferred_element_type=jnp.float32)
        * score_scale
    )
    largest = jnp.max(scores, axis=-1, keepdims=True)
    powers = jnp.exp(scores - largest)
    totals = jnp.sum(powers, axis=-1, keepdims=True)
    attention = powers / totals
    log_total = largest + jnp.log(totals)
    attended = jnp.einsum(
        "ghqk,gkhe->gqhe", attention, value_heads.astype(jnp.float32), precision=highest
    ).reshape(row_count, model_width)
    attended_low = attended.astype(jnp.bfloat16)
    branch = matmul(attended_low, full_proj) + vec_values[4]
    middle = tokens + branch
    standard_two = standardize(middle)
    normed_two = (standard_two * vec_values[2] + vec_values[3]).astype(jnp.bfloat16)
    hidden = matmul(normed_two, full_up) + up_bias
    activated = gelu_exact(hidden).astype(jnp.bfloat16)
    output = middle + (matmul(activated, full_down) + vec_values[5])
    output_view = output.reshape(images, token_count, model_width)
    y_extras = output_view[:, :2].astype(jnp.bfloat16)
    y_patches = output_view[:, 2:].astype(jnp.bfloat16)
    incoming = jnp.concatenate(
        [
            next_extra.astype(jnp.float32) + skip_extra.astype(jnp.float32),
            next_grad.astype(jnp.float32) + skip_grad.astype(jnp.float32),
        ],
        axis=1,
    ).reshape(row_count, model_width)
    incoming_low = incoming.astype(jnp.bfloat16)
    act_grad = matmul_last(incoming_low, full_down)
    gelu_pull = jax.vjp(gelu_exact, hidden)[1]
    hidden_grad = gelu_pull(act_grad)[0].astype(jnp.bfloat16)
    normed_two_grad = matmul_last(hidden_grad, full_up)
    middle_grad = incoming + jax.vjp(standardize, middle)[1](normed_two_grad * vec_values[2])[0]
    middle_low = middle_grad.astype(jnp.bfloat16)
    attended_grad = matmul_last(middle_low, full_proj).astype(jnp.bfloat16)
    grad_heads = attended_grad.reshape(images, token_count, head_count, head_size)
    grad_wide = grad_heads.astype(jnp.float32)
    attended_heads = attended.reshape(images, token_count, head_count, head_size)
    row_delta = jnp.transpose(jnp.sum(grad_wide * attended_heads, axis=-1), (0, 2, 1))[..., None]
    scores_again = (
        jnp.einsum("gqhe,gkhe->ghqk", query_heads, key_heads, preferred_element_type=jnp.float32)
        * score_scale
    )
    attention_again = jnp.exp(scores_again - log_total)
    prob_grad = jnp.einsum(
        "gqhe,gkhe->ghqk", grad_heads, value_heads, preferred_element_type=jnp.float32
    )
    score_grad = (attention_again * (prob_grad - row_delta)).astype(jnp.bfloat16)
    query_grad = (
        jnp.einsum("ghqk,gkhe->gqhe", score_grad, key_heads, preferred_element_type=jnp.float32)
        * score_scale
    )
    query_mask = row_weight.reshape(images, 1, token_count, 1)
    score_kept = score_grad * query_mask.astype(jnp.bfloat16)
    attention_kept = attention_again * query_mask

    def key_block(first_key, key_total):
        score_part = lax.dynamic_slice_in_dim(score_kept, first_key, key_total, 3)
        prob_part = lax.dynamic_slice_in_dim(attention_kept, first_key, key_total, 3)
        key_part = (
            jnp.einsum(
                "ghqk,gqhe->kghe", score_part, query_heads, preferred_element_type=jnp.float32
            )
            * score_scale
        )
        value_part = jnp.einsum("ghqk,gqhe->kghe", prob_part, grad_wide, precision=highest)
        return jnp.concatenate(
            [
                key_part.reshape(key_total, images, model_width),
                value_part.reshape(key_total, images, model_width),
            ],
            axis=-1,
        )

    first_block = jnp.int32(0) // token_count
    pieces = []
    for block_offset in range(token_count * lax.axis_size("seq") // token_count):
        block_index = first_block + block_offset
        lead = (block_index == 0).astype(jnp.float32)
        pieces.append(key_block(0, 2) * lead)
        pieces.append(key_block(2 + block_index * patch_rows, patch_rows))
    token_sums = lax.psum_scatter(
        jnp.concatenate(pieces, axis=0).astype(jnp.bfloat16), "seq", scatter_dimension=0, tiled=True
    ).astype(jnp.float32)
    key_grad = jnp.transpose(token_sums, (1, 0, 2))
    packed_grad = (
        jnp.concatenate([query_grad.reshape(images, token_count, model_width), key_grad], axis=-1)
        .reshape(row_count, 3 * model_width)
        .astype(jnp.bfloat16)
    )
    normed_grad = matmul_last(packed_grad, full_qkv)
    token_grad = middle_grad + jax.vjp(standardize, tokens)[1](normed_grad * vec_values[0])[0]
    token_view = token_grad.reshape(images, token_count, model_width)
    dx_patches = token_view[:, 2:].astype(jnp.bfloat16)
    class_grad = token_view[:, 1] * counted
    table_grad = matmul_first(selector, class_grad, highest)
    vec_grad = jnp.concatenate(
        [
            jnp.sum(row_weight * normed_grad * standard_one, axis=0)[None],
            jnp.sum(row_weight * normed_grad, axis=0)[None],
            jnp.sum(row_weight * normed_two_grad * standard_two, axis=0)[None],
            jnp.sum(row_weight * normed_two_grad, axis=0)[None],
            jnp.sum(row_weight * middle_low.astype(jnp.float32), axis=0)[None],
            jnp.sum(row_weight * incoming_low.astype(jnp.float32), axis=0)[None],
            jnp.sum(row_weight * hidden_grad.astype(jnp.float32), axis=0).reshape(4, model_width),
        ],
        axis=0,
    )
    vec_sum, table_sum = (
        lax.psum_scatter(vec_grad, ("batch", "seq"), scatter_dimension=1, tiled=True),
        lax.psum_scatter(table_grad, ("batch", "seq"), scatter_dimension=1, tiled=True),
    )
    long_sides = [packed_grad, middle_low, hidden_grad, activated]
    other_sides = [
        normed * row_low,
        attended_low * row_low,
        normed_two * row_low,
        incoming_low * row_low,
    ]
    piece_widths = [
        3 * model_width // shards,
        model_width // shards,
        up_width // shards,
        up_width // shards,
    ]
    slice_rows = sum(piece_widths)
    slice_total = slice_rows * lax.axis_size(("batch", "seq")) // slice_rows
    blocks = []
    for long_side, other_side, piece_width in zip(long_sides, other_sides, piece_widths):
        blocks.append(
            matmul_first(long_side, other_side).reshape(slice_total, piece_width, model_width)
        )
    grad_share = lax.psum_scatter(
        jnp.concatenate(blocks, axis=1).reshape(
            slice_rows * lax.axis_size(("batch", "seq")), model_width
        ),
        ("batch", "seq"),
        scatter_dimension=0,
        tiled=True,
    )
    offset_one = piece_widths[0]
    offset_two = offset_one + piece_widths[1]
    offset_three = offset_two + piece_widths[2]
    grad_qkv = grad_share[:offset_one].T
    grad_proj = grad_share[offset_one:offset_two].T
    grad_up = grad_share[offset_two:offset_three].T
    grad_down = grad_share[offset_three:]
    mom_qkv_new = muon_momentum * mom_qkv + grad_qkv
    mom_proj_new = muon_momentum * mom_proj + grad_proj
    mom_up_new = muon_momentum * mom_up + grad_up
    mom_down_new = muon_momentum * mom_down + grad_down
    group_qkv, group_proj, group_up, group_down = (
        lax.all_gather(mom_qkv_new.astype(jnp.bfloat16), "batch", axis=1, tiled=True).astype(
            mom_qkv_new.dtype
        ),
        lax.all_gather(mom_proj_new.astype(jnp.bfloat16), "batch", axis=1, tiled=True).astype(
            mom_proj_new.dtype
        ),
        lax.all_gather(mom_up_new.astype(jnp.bfloat16), "batch", axis=1, tiled=True).astype(
            mom_up_new.dtype
        ),
        lax.all_gather(mom_down_new.astype(jnp.bfloat16), "batch", axis=0, tiled=True).astype(
            mom_down_new.dtype
        ),
    )
    slab_width = up_width // seq_count
    candidates = (group_qkv, group_proj, group_up, group_down.T)
    owned_slab = jnp.zeros((model_width, slab_width), jnp.float32)
    for position, candidate in enumerate(candidates):
        padded = jnp.pad(candidate, ((0, 0), (0, slab_width - candidate.shape[1])))
        owned_slab = owned_slab + (batch_rank == owner_ranks[position]).astype(jnp.float32) * padded
    square_sum = lax.psum(jnp.sum(owned_slab * owned_slab), "seq")
    current = owned_slab / (jnp.sqrt(square_sum) + 1e-07)
    for sweep in range(NS_STEPS):
        gram_matrix = lax.psum(
            matmul_last(current, current, highest).astype(jnp.bfloat16), "seq"
        ).astype(jnp.float32)
        square = jnp.dot(gram_matrix, gram_matrix, precision=highest)
        mixing = poly_second * gram_matrix + poly_third * square
        current = poly_first * current + jnp.dot(mixing, current, precision=highest)
    masters = (w_qkv, w_proj, w_up, w_down)
    ratios = (3.0, 1.0, up_width / model_width, model_width / up_width)
    updated = []
    for position in range(4):
        received = broadcast(current.astype(jnp.bfloat16), "batch", owner_ranks[position]).astype(
            current.dtype
        )
        own_part = lax.dynamic_slice_in_dim(
            received, batch_rank * piece_widths[position], piece_widths[position], 1
        )
        if position == 3:
            own_part = own_part.T
        factor = math.sqrt(max(1.0, ratios[position]))
        updated.append(
            masters[position] * (1.0 - muon_rate * muon_decay) - muon_rate * factor * own_part
        )
    vec_first_new, vec_second_new, vectors_new = adam_step(vectors, vec_first, vec_second, vec_sum)
    table_first_new, table_second_new, table_new = adam_step(
        table, table_first, table_second, table_sum
    )
    return (
        y_patches,
        y_extras,
        dx_patches,
        updated[0],
        updated[1],
        updated[2],
        updated[3],
        mom_qkv_new,
        mom_proj_new,
        mom_up_new,
        mom_down_new,
        vec_first_new,
        vec_second_new,
        vectors_new,
        table_first_new,
        table_second_new,
        table_new,
    )


def solution(mesh):
    placed = (
        P("batch", "seq", None),
        P("batch"),
        P("batch"),
        P("batch", "seq", None),
        P("batch", "seq", None),
        P("batch", None, None),
        P("batch", None, None),
        P(None, ("batch", "seq")),
        P(None, ("batch", "seq")),
        P(None, ("batch", "seq")),
        P(("batch", "seq"), None),
        P(None, ("batch", "seq")),
        P(None, ("batch", "seq")),
        P(None, ("batch", "seq")),
        P(("batch", "seq"), None),
        P(None, ("batch", "seq")),
        P(None, ("batch", "seq")),
        P(None, ("batch", "seq")),
        P(None, ("batch", "seq")),
        P(None, ("batch", "seq")),
        P(None, ("batch", "seq")),
    )
    return jax.shard_map(
        body,
        mesh=mesh,
        in_specs=placed,
        out_specs=(
            P("batch", "seq", None),
            P("batch", None, None),
            P("batch", "seq", None),
            P(None, ("batch", "seq")),
            P(None, ("batch", "seq")),
            P(None, ("batch", "seq")),
            P(("batch", "seq"), None),
            P(None, ("batch", "seq")),
            P(None, ("batch", "seq")),
            P(None, ("batch", "seq")),
            P(("batch", "seq"), None),
            P(None, ("batch", "seq")),
            P(None, ("batch", "seq")),
            P(None, ("batch", "seq")),
            P(None, ("batch", "seq")),
            P(None, ("batch", "seq")),
            P(None, ("batch", "seq")),
        ),
        check_vma=False,
    )
```

profile of v0, /device:TPU:9, one launch (start us, length us, event | category | flops | bytes accessed | tf_op | source)
XLA Modules:
  0.0 3381.2 jit_solution(14502588134225451922)
XLA Ops:
  14.1 59.6 %all-gather.1 = bf16[32,36,10]{1,2,0:T(8,128)(2,1)S(1)} all-gather(bf16[1,36,10]{1,2,0:T(8,128)(2,1)S(1)} %convert_bitcast_fusion.5), channel_id=1, replica_groups=mesh['batch'=8,'seq'=4] {'batch','seq'}, dimensions={0}, use_global_device_ids=true | all-gather | bytes 23760 | tf_op jit(solution)/shard_map/all_gather | solution.py:123
  87.1 63.4 %all-gather.31.cloned.1.call-done = bf16[32,108,1152]{2,1,0:T(8,128)(2,1)} async-done(((bf16[1,108,1152]{2,1,0:T(8,128)(2,1)}), bf16[32,108,1152]{2,1,0:T(8,128)(2,1)}) %all-gather.31.cloned.1.call-update) | async-done | bytes 7962640 | tf_op jit(solution)/shard_map/all_gather | solution.py:119
  150.5 9.2 reshape.415
  159.7 11.2 convolution_convert_fusion.5
  170.8 9.6 reshape.389
  180.4 11.1 fusion.132
  234.2 64.3 %all-gather.17.cloned.1.call-done = bf16[2,1024,1152]{2,1,0:T(8,128)(2,1)} async-done(((bf16[2,256,1152]{2,1,0:T(8,128)(2,1)}), bf16[2,1024,1152]{2,1,0:T(8,128)(2,1)}) %all-gather.17.cloned.1.call-update) | async-done | bytes 4718608 | tf_op jit(solution)/shard_map/all_gather | solution.py:153
  304.3 8.5 copy.181
  312.8 75.7 %all-gather.19.cloned.1.call-done = bf16[2,1024,1152]{2,1,0:T(8,128)(2,1)} async-done(((bf16[2,256,1152]{2,1,0:T(8,128)(2,1)}), bf16[2,1024,1152]{2,1,0:T(8,128)(2,1)}) %all-gather.19.cloned.1.call-update) | async-done | bytes 4718608 | tf_op jit(solution)/shard_map/all_gather | solution.py:152
  394.2 8.4 copy.183
  402.6 17.2 fusion.133
  419.8 15.5 fusion.3
  435.3 33.0 broadcast_multiply_fusion.1
  483.7 32.0 fusion.12
  515.7 53.9 %all-gather.23.cloned.1.call-done = bf16[4608,1152]{1,0:T(8,128)(2,1)} async-done(((bf16[144,1152]{1,0:T(8,128)(2,1)}), bf16[4608,1152]{1,0:T(8,128)(2,1)}) %all-gather.23.cloned.1.call-update) | async-done | bytes 10616848 | tf_op jit(solution)/shard_map/all_gather | solution.py:122
  569.6 18.3 multiply_reduce_fusion
  587.9 13.5 multiply_reduce_fusion.5
  615.3 29.5 fusion.4
  651.2 10.9 fusion.75
  663.3 28.6 broadcast_multiply_fusion
  700.6 11.5 fusion.78
  715.0 11.1 fusion.81
  728.9 11.0 fusion.84
  742.8 11.6 fusion.66
  806.1 23.2 fusion.15
  829.3 8.0 copy.211
  848.4 7.8 fusion.135
  856.3 12.4 fusion.136
  868.8 13.5 fusion.88
  882.3 247.1 %all-reduce.28.cloned.1.call-done = bf16[1032,2,2304]{2,1,0:T(2,128)(2,1)} async-done(((bf16[1032,2,2304]{2,1,0:T(2,128)(2,1)}), bf16[1032,2,2304]{2,1,0:T(2,128)(2,1)}) %all-reduce.28.cloned.1.call-update) | async-done | bytes 9510928
  1138.1 18.7 dot_general.170
  1156.9 12.7 fusion.57
  1169.6 43.1 %pad_maximum_fusion = f32[32,432,1152]{2,1,0:T(8,128)} fusion(f32[32,144,1152]{2,1,0:T(8,128)} %fusion.136, f32[32,144,1152]{2,1,0:T(8,128)} %bitcast.269, f32[32,36,1152]{2,1,0:T(8,128)} %fusion.135, f32[32,108,1152]{2,1,0:T(8,128)} %fusion.57), kind=kLoop, calls=%fused_computation | loop fusion | flops 47775744 | bytes 127401984 | tf_op jit(solution)/shard_map/concatenate | solution.py:300
  1212.7 63.4 %copy.212 = f32[13824,1152]{0,1:T(8,128)} copy(f32[13824,1152]{1,0:T(8,128)} %bitcast.258) | data formatting | bytes 127401984 | tf_op jit(solution)/shard_map/reshape | solution.py:300
  1277.4 917.8 %all-reduce.30.cloned.1.call-done = f32[13824,1152]{0,1:T(8,128)} async-done(((f32[13824,1152]{0,1:T(8,128)}), f32[13824,1152]{0,1:T(8,128)}) %all-reduce.30.cloned.1.call-update) | async-done | bytes 63701008
  2209.9 13.4 all-gather.5
  2232.1 28.0 all-gather.27.cloned.1.call-done
  2264.2 28.6 all-gather.25.cloned.1.call-done
  2302.2 7.5 psum.70
  2310.4 32.4 convolution_convert_fusion.4
  2342.8 105.1 %all-reduce.18.cloned.1.call-done = bf16[1152,1152]{1,0:T(8,128)(2,1)} async-done(((bf16[1152,1152]{1,0:T(8,128)(2,1)}), bf16[1152,1152]{1,0:T(8,128)(2,1)}) %all-reduce.18.cloned.1.call-update) | async-done | bytes 2654224 | tf_op jit(solution)/shard_map/psum | solution.py:341
  2447.9 7.5 fusion.7
  2455.4 26.4 convolution_add_fusion.4
  2484.2 24.7 convolution_convert_fusion.3
  2508.9 104.3 %all-reduce.20.cloned.1.call-done = bf16[1152,1152]{1,0:T(8,128)(2,1)} async-done(((bf16[1152,1152]{1,0:T(8,128)(2,1)}), bf16[1152,1152]{1,0:T(8,128)(2,1)}) %all-reduce.20.cloned.1.call-update) | async-done | bytes 2654224 | tf_op jit(solution)/shard_map/psum | solution.py:341
  2613.2 7.4 fusion.8
  2620.6 27.7 convolution_add_fusion.3
  2650.7 24.8 convolution_convert_fusion.2
  2675.6 104.3 %all-reduce.22.cloned.1.call-done = bf16[1152,1152]{1,0:T(8,128)(2,1)} async-done(((bf16[1152,1152]{1,0:T(8,128)(2,1)}), bf16[1152,1152]{1,0:T(8,128)(2,1)}) %all-reduce.22.cloned.1.call-update) | async-done | bytes 2654224 | tf_op jit(solution)/shard_map/psum | solution.py:341
  2779.9 7.4 fusion.9
  2787.3 27.7 convolution_add_fusion.2
  2817.3 24.8 convolution_convert_fusion.1
  2842.3 104.3 %all-reduce.24.cloned.1.call-done = bf16[1152,1152]{1,0:T(8,128)(2,1)} async-done(((bf16[1152,1152]{1,0:T(8,128)(2,1)}), bf16[1152,1152]{1,0:T(8,128)(2,1)}) %all-reduce.24.cloned.1.call-update) | async-done | bytes 2654224 | tf_op jit(solution)/shard_map/psum | solution.py:341
  2946.6 7.4 fusion.10
  2954.0 27.7 convolution_add_fusion.1
  2984.0 24.8 convolution_convert_fusion
  3016.2 14.5 fusion.63
  3036.0 77.3 %all-reduce.26.cloned.1.call-done = bf16[1152,1152]{1,0:T(8,128)(2,1)} async-done(((bf16[1152,1152]{1,0:T(8,128)(2,1)}), bf16[1152,1152]{1,0:T(8,128)(2,1)}) %all-reduce.26.cloned.1.call-update) | async-done | bytes 2654224 | tf_op jit(solution)/shard_map/psum | solution.py:341
  3113.3 7.4 fusion.11
  3120.7 27.9 broadcast_select_fusion
  3150.3 10.6 multiply_reduce_fusion.6
  3170.9 117.2 %fusion = f32[1001,40]{0,1:T(8,128)S(1)} fusion(f32[1001,1152]{0,1:T(8,128)} %fusion.113), kind=kCustom, calls=%all-reduce-scatter | all-reduce-scatter fusion | flops 1281281 | bytes 4772768
  3305.5 39.4 %all-reduce.5 = f32[10,1152]{1,0:T(8,128)} all-reduce(f32[10,1152]{1,0:T(8,128)S(1)} %concatenate.81), channel_id=4, replica_groups=mesh['batch'=8,'seq'=4] {'batch','seq'}, use_global_device_ids=true, to_apply=%region_31.32.clone | all-reduce | flops 11520 | bytes 92160
  3349.2 7.7 concatenate.82
  (414 shorter events, 309.6 us)
Async XLA Ops:
  7.2 67.4 %all-gather.29.cloned.1.call-start = ((), (), s32[]{:S(2)}) async-start(), calls=%async_computation.11 | async-start | bytes 2703360 | tf_op jit(solution)/shard_map/all_gather | solution.py:124
  8.8 141.6 %all-gather.31.cloned.1.call-start = ((), (), s32[]{:S(2)}) async-start(), calls=%async_computation.12 | async-start | bytes 8515584 | tf_op jit(solution)/shard_map/all_gather | solution.py:119
  10.7 68.3 %copy-start.87 = (s32[2]{0:T(128)S(1)}, s32[2]{0:T(128)}, u32[]{:S(2)}) copy-start(s32[2]{0:T(128)} %param.23) | copy-start | bytes 28
  10.7 210.9 %all-gather.33.cloned.1.call-start = ((), (), s32[]{:S(2)}) async-start(), calls=%async_computation.13 | async-start | bytes 3041280 | tf_op jit(solution)/shard_map/all_gather | solution.py:120
  12.3 286.2 %all-gather.17.cloned.1.call-start = ((), (), s32[]{:S(2)}) async-start(), calls=%async_computation | async-start | bytes 5898240 | tf_op jit(solution)/shard_map/all_gather | solution.py:153
  74.6 138.4 %copy-start.52 = (f32[1152]{0:T(1024)}, f32[1152]{0:T(1024)S(1)}, u32[]{:S(2)}) copy-start(f32[1152]{0:T(1024)S(1)} %get-tuple-element.96) | copy-start | bytes 13828
  81.8 77.9 %copy-start.68 = (f32[516]{0:T(1024)}, f32[516]{0:T(1024)S(1)}, u32[]{:S(2)}) copy-start(f32[516]{0:T(1024)S(1)} %div.97) | copy-start | bytes 6196
  87.1 72.5 %copy-start.58 = (f32[516]{0:T(1024)}, f32[516]{0:T(1024)S(1)}, u32[]{:S(2)}) copy-start(f32[516]{0:T(1024)S(1)} %add.262) | copy-start | bytes 6196
  87.1 72.5 %copy-start.70 = (f32[516]{0:T(1024)}, f32[516]{0:T(1024)S(1)}, u32[]{:S(2)}) copy-start(f32[516]{0:T(1024)S(1)} %rsqrt.25) | copy-start | bytes 6196
  194.2 194.3 %all-gather.19.cloned.1.call-start = ((), (), s32[]{:S(2)}) async-start(), calls=%async_computation.1 | async-start | bytes 5898240 | tf_op jit(solution)/shard_map/all_gather | solution.py:152
  198.8 284.8 %all-gather.21.cloned.1.call-start = ((), (), s32[]{:S(2)}) async-start(), calls=%async_computation.2 | async-start | bytes 10948608 | tf_op jit(solution)/shard_map/all_gather | solution.py:121
  199.7 369.9 %all-gather.23.cloned.1.call-start = ((), (), s32[]{:S(2)}) async-start(), calls=%async_computation.3 | async-start | bytes 10948608 | tf_op jit(solution)/shard_map/all_gather | solution.py:122
  201.6 927.8 %all-reduce.28.cloned.1.call-start = ((), (), s32[]{:S(2)}) async-start(), calls=%async_computation.15 | async-start | bytes 19021824
  201.9 367.6 %copy-start.48 = (f32[4608]{0:T(1024)}, f32[4608]{0:T(1024)S(1)}, u32[]{:S(2)}) copy-start(f32[4608]{0:T(1024)S(1)} %add.274) | copy-start | bytes 55300
  234.2 168.4 %copy-start.1 = (bf16[2,258,1,1152]{1,3,0,2:T(8,128)(2,1)}, bf16[2,258,1,1152]{1,3,0,2:T(8,128)(2,1)S(1)}, u32[]{:S(2)}) copy-start(bf16[2,258,1,1152]{1,3,0,2:T(8,128)(2,1)S(1)} %copy.182) | copy-start | bytes 3566596
  481.8 119.6 %copy-start.56 = (f32[516]{0:T(1024)}, f32[516]{0:T(1024)S(1)}, u32[]{:S(2)}) copy-start(f32[516]{0:T(1024)S(1)} %broadcast_multiply_fusion.2) | copy-start | bytes 6196
  483.6 117.8 %copy-start.72 = (f32[516]{0:T(1024)}, f32[516]{0:T(1024)S(1)}, u32[]{:S(2)}) copy-start(f32[516]{0:T(1024)S(1)} %fusion.118) | copy-start | bytes 6196
  483.6 131.6 %copy-start.36 = (f32[2,16,258]{2,1,0:T(8,128)}, f32[2,16,258]{2,1,0:T(8,128)S(1)}, u32[]{:S(2)}) copy-start(f32[2,16,258]{2,1,0:T(8,128)S(1)} %log_add_fusion) | copy-start | bytes 99076
  483.7 85.9 %copy-start.5 = (f32[516,1152]{1,0:T(8,128)S(1)}, f32[516,1152]{1,0:T(8,128)}, u32[]{:S(2)}) copy-start(f32[516,1152]{1,0:T(8,128)} %reshape.393) | copy-start | bytes 7133188
  483.7 85.9 %copy-start.75 = (f32[516]{0:T(1024)S(1)}, f32[516]{0:T(1024)}, u32[]{:S(2)}) copy-start(f32[516]{0:T(1024)} %copy-done.74) | copy-start | bytes 6196
  587.9 13.6 copy-start.10
  651.1 10.9 copy-start.30
  663.3 28.6 copy-start.2
  694.8 17.2 copy-start
  762.6 12.5 copy-start.29
  762.6 12.4 copy-start.38
  774.4 11.2 copy-start.27
  784.1 12.0 copy-start.26
  805.4 1389.8 %all-reduce.30.cloned.1.call-start = ((), (), s32[]{:S(2)}) async-start(), calls=%async_computation.16 | async-start | bytes 127401984
  848.4 20.4 slice-start.2
  856.3 12.5 copy-start.11
  856.3 12.5 copy-start.57
  856.3 12.5 copy-start.61
  856.3 12.5 copy-start.73
  856.3 12.5 copy-start.81
  856.3 12.5 copy-start.89
  856.3 12.5 slice-start.3
  1138.1 18.8 copy-start.16
  1276.1 922.4 %copy-start.40 = (f32[144,1152]{1,0:T(8,128)S(1)}, f32[144,1152]{1,0:T(8,128)}, u32[]{:S(2)}) copy-start(f32[144,1152]{1,0:T(8,128)} %param.35) | copy-start | bytes 1990660
  1276.1 951.8 %all-gather.35.cloned.1.call-start = ((), (), s32[]{:S(2)}) async-start(), calls=%async_computation.14 | async-start | bytes 2322432 | tf_op jit(solution)/shard_map/all_gather | solution.py:319
  1277.4 925.4 %copy-start.41 = (f32[1152,144]{0,1:T(8,128)S(1)}, f32[1152,144]{0,1:T(8,128)}, u32[]{:S(2)}) copy-start(f32[1152,144]{0,1:T(8,128)} %param.34) | copy-start | bytes 1990660
  2198.4 61.6 %all-gather.27.cloned.1.call-start = ((), (), s32[]{:S(2)}) async-start(), calls=%async_computation.5 | async-start | bytes 2985984 | tf_op jit(solution)/shard_map/all_gather | solution.py:328
  2202.8 90.0 %all-gather.25.cloned.1.call-start = ((), (), s32[]{:S(2)}) async-start(), calls=%async_computation.4 | async-start | bytes 2985984 | tf_op jit(solution)/shard_map/all_gather | solution.py:325
  2207.1 240.8 %all-reduce.18.cloned.1.call-start = ((), (), s32[]{:S(2)}) async-start(), calls=%async_computation.6 | async-start | bytes 5308416 | tf_op jit(solution)/shard_map/psum | solution.py:341
  2342.8 270.5 %all-reduce.20.cloned.1.call-start = ((), (), s32[]{:S(2)}) async-start(), calls=%async_computation.7 | async-start | bytes 5308416 | tf_op jit(solution)/shard_map/psum | solution.py:341
  2508.9 271.0 %all-reduce.22.cloned.1.call-start = ((), (), s32[]{:S(2)}) async-start(), calls=%async_computation.8 | async-start | bytes 5308416 | tf_op jit(solution)/shard_map/psum | solution.py:341
  2675.5 271.0 %all-reduce.24.cloned.1.call-start = ((), (), s32[]{:S(2)}) async-start(), calls=%async_computation.9 | async-start | bytes 5308416 | tf_op jit(solution)/shard_map/psum | solution.py:341
  2842.2 271.1 %all-reduce.26.cloned.1.call-start = ((), (), s32[]{:S(2)}) async-start(), calls=%async_computation.10 | async-start | bytes 5308416 | tf_op jit(solution)/shard_map/psum | solution.py:341
  2984.0 27.2 copy-start.39
  3009.0 355.3 %all-reduce.32.cloned.1.call-start = ((), (), s32[]{:S(2)}) async-start(), calls=%async_computation.17 | async-start | bytes 21233664 | tf_op jit(solution)/shard_map/psum | solution.py:29
  3166.6 133.1 %copy-start.86 = (f32[1152]{0:T(1024)S(1)}, f32[1152]{0:T(1024)}, u32[]{:S(2)}) copy-start(f32[1152]{0:T(1024)} %get-tuple-element.87) | copy-start | bytes 13828
  3166.6 133.7 %copy-start.85 = (f32[1152]{0:T(1024)S(1)}, f32[1152]{0:T(1024)}, u32[]{:S(2)}) copy-start(f32[1152]{0:T(1024)} %get-tuple-element.90) | copy-start | bytes 13828
  3166.6 134.3 %copy-start.84 = (f32[1152]{0:T(1024)S(1)}, f32[1152]{0:T(1024)}, u32[]{:S(2)}) copy-start(f32[1152]{0:T(1024)} %get-tuple-element.97) | copy-start | bytes 13828
  3166.6 137.9 %copy-start.51 = (f32[4,1152]{1,0:T(4,128)S(1)}, f32[4,1152]{1,0:T(4,128)}, u32[]{:S(2)}) copy-start(f32[4,1152]{1,0:T(4,128)} %reshape.408) | copy-start | bytes 55300
  3166.6 178.2 %copy-start.66 = (f32[10,36]{1,0:T(8,128)S(1)}, f32[10,36]{1,0:T(8,128)}, u32[]{:S(2)}) copy-start(f32[10,36]{1,0:T(8,128)} %param.36) | copy-start | bytes 4324
  3170.9 186.0 %copy-start.42 = (f32[1001,36]{0,1:T(8,128)S(1)}, f32[1001,36]{0,1:T(8,128)}, u32[]{:S(2)}) copy-start(f32[1001,36]{0,1:T(8,128)} %param.39) | copy-start | bytes 432436
  3170.9 186.0 %copy-start.45 = (f32[1001,36]{0,1:T(8,128)S(1)}, f32[1001,36]{0,1:T(8,128)}, u32[]{:S(2)}) copy-start(f32[1001,36]{0,1:T(8,128)} %param.41) | copy-start | bytes 432436
  3170.9 187.9 %copy-start.34 = (f32[1152,108]{1,0:T(8,128)S(1)}, f32[1152,108]{1,0:T(8,128)}, u32[]{:S(2)}) copy-start(f32[1152,108]{1,0:T(8,128)} %get-tuple-element.109) | copy-start | bytes 1492996
  3288.1 73.8 %copy-start.25 = (f32[1152,144]{1,0:T(8,128)S(1)}, f32[1152,144]{1,0:T(8,128)}, u32[]{:S(2)}) copy-start(f32[1152,144]{1,0:T(8,128)} %get-tuple-element.113) | copy-start | bytes 1990660
  3288.1 75.0 %copy-start.24 = (f32[144,1152]{0,1:T(8,128)S(1)}, f32[144,1152]{0,1:T(8,128)}, u32[]{:S(2)}) copy-start(f32[144,1152]{0,1:T(8,128)} %get-tuple-element.115) | copy-start | bytes 1990660
  3288.7 60.5 %collective-permute-start.2 = (f32[1001,40]{0,1:T(8,128)S(1)}, f32[1001,40]{0,1:T(8,128)}, u32[]{:S(2)}, u32[]{:S(2)}) collective-permute-start(f32[1001,40]{0,1:T(8,128)S(1)} %fusion), channel_id=1, source_target_pairs={{0,3},{1,4},{2,5},{3,6},{4,7},{5,8},{6,9},{7,10},{8,11},{9,12},{10... | collective-permute-start | bytes 480488
  3294.6 54.6 %collective-permute-start.1 = (f32[1001,40]{0,1:T(8,128)S(1)}, f32[1001,40]{0,1:T(8,128)}, u32[]{:S(2)}, u32[]{:S(2)}) collective-permute-start(f32[1001,40]{0,1:T(8,128)S(1)} %fusion), channel_id=1, source_target_pairs={{0,2},{1,3},{2,4},{3,5},{4,6},{5,7},{6,8},{7,9},{8,10},{9,11},{10,... | collective-permute-start | bytes 480488
  3296.6 52.6 %collective-permute-start = (f32[1001,40]{0,1:T(8,128)S(1)}, f32[1001,40]{0,1:T(8,128)}, u32[]{:S(2)}, u32[]{:S(2)}) collective-permute-start(f32[1001,40]{0,1:T(8,128)S(1)} %fusion), channel_id=1, source_target_pairs={{0,1},{1,2},{2,3},{3,4},{4,5},{5,6},{6,7},{7,8},{8,9},{9,10},{10,1... | collective-permute-start | bytes 480488
  3301.5 47.7 %collective-permute-start.3 = (f32[1001,4]{0,1:T(4,128)}, f32[1001,4]{0,1:T(4,128)}, u32[]{:S(2)}, u32[]{:S(2)}) collective-permute-start(f32[1001,4]{0,1:T(4,128)} %slice.119), channel_id=1, source_target_pairs={{0,4},{1,5},{2,6},{3,7},{4,8},{5,9},{6,10},{7,11},{8,12},{9,13},{1... | collective-permute-start | bytes 48056
  (58 other events, 284.2 us)
Sparse Core Ops, SparseCore 0:
  11.5 58.6 all-gather.28
  73.5 76.9 all-gather.30
  153.9 56.2 all-gather.32
  212.2 86.2 all-gather.16
  300.5 87.8 all-gather.18
  391.7 88.6 all-gather.20
  483.7 85.7 all-gather.22
  805.5 323.8 all-reduce.27
  1276.2 918.9 all-reduce.29
  2198.6 29.2 all-gather.34
  2230.5 29.4 all-gather.26
  2262.5 30.2 all-gather.24
  2342.9 104.9 all-reduce.17
  2509.0 104.1 all-reduce.19
  2675.7 104.1 all-reduce.21
  2842.3 104.1 all-reduce.23
  3009.1 104.1 all-reduce.25
  3148.8 172.9 all-reduce.31
where the time goes:
time: 3400 us; the launch traced here: 3380 us
  waiting for transfers between devices  1980 us (58%)
  matrix products  624 us (18%)
  local copies, waits for them, and re-layouts  319 us (9%)
  blocking collectives  237 us (7%)
  other arithmetic  190 us (6%)
    unnamed x24, waiting for transfers between devices  1170 us
    psum x5, waiting for transfers between devices, body(): lax.psum(matmul_last(current, current, highest).astype(jnp.bfloat16), 'seq')  495 us
    dot_general x9, matrix products, matmul_last(): lax.dot_general(former, latter, (((1,), (1,)), ((), ())), precision=preci...  176 us
    unnamed x2, blocking collectives  157 us
    dot_general x5, matrix products, body(): current = poly_first * current + jnp.dot(mixing, current, precision=highest)  137 us
    unnamed x232, local copies, waits for them, and re-layouts  77.3 us
    all_gather x1, waiting for transfers between devices, body(): lax.all_gather(keys_own[:, 2:], 'seq', axis=1, tiled=True)  75.7 us
  transfers between devices with their start and end apart: 22, of which 14 were waited for; matrix products, arithmetic and copies ran while one was open for 15% of the time, Pallas kernels for 0%

commit v1 on v0

v1 whole, which is shorter than its diff:
```python
import functools
import math

import jax
import jax.numpy as jnp
from jax import lax
from jax.experimental import pallas as pl
from jax.experimental.pallas import tpu as pltpu
from jax.sharding import PartitionSpec as P

HEADS = 16
STEP = 10
FIRST_STEPS = 3
LAST_STEPS = 2

norm_eps = 1e-05
poly_first = 3.4445
poly_second = -4.775
poly_third = 2.0315
muon_momentum = 0.95
muon_rate = 1.5
muon_decay = 0.01
beta_one = 0.9
beta_two = 0.999
adam_rate = 1.0
adam_eps = 1e-08
highest = lax.Precision.HIGHEST
BF = jnp.bfloat16
F32 = jnp.float32
LOG2E = math.log2(math.e)
MIB = 1024 * 1024


def dot_nt(former, latter):
    return lax.dot_general(former, latter, (((1,), (1,)), ((), ())), preferred_element_type=F32)


def dot_nn(former, latter):
    return lax.dot_general(former, latter, (((1,), (0,)), ((), ())), preferred_element_type=F32)


def dot_tn(former, latter):
    return lax.dot_general(former, latter, (((0,), (0,)), ((), ())), preferred_element_type=F32)


def in_vmem(count):
    return [pl.BlockSpec(memory_space=pltpu.VMEM)] * count


def shape_of(shape, dtype):
    return jax.ShapeDtypeStruct(shape, dtype)


def head_window(head, size, width):
    start = jnp.minimum((head * size) // 128, (width - 256) // 128) * 128
    return pl.multiple_of(start, 128), head * size - start


def attention_forward_kernel(groups, valid_ref, own_ref, *refs):
    others, (o_ref, lse_ref, lsex_ref, acc) = refs[: groups - 1], refs[groups - 1 :]
    rows = own_ref.shape[0] - 16
    width = own_ref.shape[1] // 3
    size = width // HEADS
    factor = size**-0.5 * LOG2E
    tables = [(own_ref, width, 2 * width)] + [(ref, 0, width) for ref in others]
    parts = []
    for group, (ref, key_at, value_at) in enumerate(tables):
        parts.append((ref, pl.ds(0, rows), key_at, value_at, None))
        parts.append((ref, pl.ds(rows, 16), key_at, value_at, valid_ref[group]))
    acc[...] = jnp.zeros_like(acc)
    tile_row = lax.broadcasted_iota(jnp.int32, (16, rows), 0)

    def one_head(head, carry):
        start, offset = head_window(head, size, width)
        lane = lax.broadcasted_iota(jnp.int32, (rows, 256), 1)
        mask = (lane >= offset) & (lane < offset + size)
        query = jnp.where(mask, own_ref[:rows, pl.ds(start, 256)], jnp.zeros((), BF))
        scores = []
        for ref, span, key_at, value_at, valid in parts:
            score = dot_nt(ref[span, pl.ds(pl.multiple_of(key_at + start, 128), 256)], query)
            if valid is not None:
                score = jnp.where(tile_row < valid, score, -1e30)
            scores.append(score)
        largest = functools.reduce(
            jnp.maximum, [jnp.max(score, axis=0, keepdims=True) for score in scores]
        )
        largest = largest * factor
        total = jnp.zeros((1, rows), F32)
        out = jnp.zeros((256, rows), F32)
        for score, (ref, span, key_at, value_at, valid) in zip(scores, parts):
            power = jnp.exp2(score * factor - largest)
            total = total + jnp.sum(power, axis=0, keepdims=True)
            values = ref[span, pl.ds(pl.multiple_of(value_at + start, 128), 256)]
            out = out + dot_tn(values, power.astype(BF))
        out = (out * (1.0 / total)).T
        acc[:, pl.ds(start, 256)] += jnp.where(mask, out, 0.0)
        lse_ref[pl.ds(head, 1), :] = largest + jnp.log2(total)
        return carry

    lax.fori_loop(0, HEADS, one_head, 0)
    o_ref[:rows, :] = acc[...].astype(BF)
    head_row = lax.broadcasted_iota(jnp.int32, (HEADS, width), 0)
    lane = lax.broadcasted_iota(jnp.int32, (HEADS, width), 1)
    diagonal = (lane >= head_row * size) & (lane < head_row * size + size)
    extra = jnp.broadcast_to(own_ref[rows : rows + 16, :width].astype(F32)[0:1], (HEADS, width))
    extra = jnp.where(diagonal, extra, 0.0).astype(BF)
    tile_lane = lax.broadcasted_iota(jnp.int32, (HEADS, 16), 1)
    scores = []
    for ref, span, key_at, value_at, valid in parts:
        score = dot_nt(extra, ref[span, key_at : key_at + width])
        if valid is not None:
            score = jnp.where(tile_lane < valid, score, -1e30)
        scores.append(score)
    largest = functools.reduce(
        jnp.maximum, [jnp.max(score, axis=1, keepdims=True) for score in scores]
    )
    largest = largest * factor
    total = jnp.zeros((HEADS, 1), F32)
    out = jnp.zeros((HEADS, width), F32)
    for score, (ref, span, key_at, value_at, valid) in zip(scores, parts):
        power = jnp.exp2(score * factor - largest)
        total = total + jnp.sum(power, axis=1, keepdims=True)
        out = out + dot_nn(power.astype(BF), ref[span, value_at : value_at + width])
    out = jnp.sum(jnp.where(diagonal, out * (1.0 / total), 0.0), axis=0, keepdims=True)
    first = lax.broadcasted_iota(jnp.int32, (16, width), 0) < valid_ref[0]
    o_ref[rows:, :] = jnp.where(first, jnp.broadcast_to(out, (16, width)), 0.0).astype(BF)
    lsex_ref[...] = jnp.broadcast_to(largest + jnp.log2(total), (HEADS, 128))


def attention_forward(valid, own, others):
    padded, wide = own.shape
    rows, width, groups = padded - 16, wide // 3, 1 + len(others)
    pairs = rows * groups * rows
    return pl.pallas_call(
        functools.partial(attention_forward_kernel, groups),
        out_shape=[
            shape_of((padded, width), BF),
            shape_of((HEADS, rows), F32),
            shape_of((HEADS, 128), F32),
        ],
        in_specs=[pl.BlockSpec(memory_space=pltpu.SMEM)] + in_vmem(groups),
        out_specs=in_vmem(3),
        scratch_shapes=[pltpu.VMEM((rows, width), F32)],
        compiler_params=pltpu.CompilerParams(vmem_limit_bytes=60 * MIB),
        cost_estimate=pl.CostEstimate(
            flops=16 * pairs * width,
            bytes_accessed=groups * padded * wide * 2,
            transcendentals=HEADS * pairs,
        ),
        name="attention_forward",
    )(valid, own, *others)


def attention_backward_kernel(groups, valid_ref, own_ref, *refs):
    others, refs = refs[: groups - 1], refs[groups - 1 :]
    o_ref, do_ref, lse_ref, lsex_ref = refs[:4]
    dq_ref, dkv_refs, refs = refs[4], refs[5 : 5 + groups], refs[5 + groups :]
    dq_acc, dk_acc, dv_acc, delta = refs
    rows = own_ref.shape[0] - 16
    padded = rows + 16
    width = own_ref.shape[1] // 3
    size = width // HEADS
    scale = size**-0.5
    factor = scale * LOG2E
    tables = [(own_ref, width, 2 * width)] + [(ref, 0, width) for ref in others]
    parts = []
    for group, (ref, key_at, value_at) in enumerate(tables):
        parts.append((ref, 0, rows, key_at, value_at, group, None))
        parts.append((ref, rows, 16, key_at, value_at, group, valid_ref[group]))
    head_row = lax.broadcasted_iota(jnp.int32, (HEADS, width), 0)
    lane = lax.broadcasted_iota(jnp.int32, (HEADS, width), 1)
    diagonal = (lane >= head_row * size) & (lane < head_row * size + size)
    ones = jnp.where(diagonal, 1.0, 0.0).astype(BF)
    product = do_ref[:rows, :].astype(F32) * o_ref[:rows, :].astype(F32)
    upper = product.astype(BF)
    lower = (product - upper.astype(F32)).astype(BF)
    delta[...] = dot_nt(ones, upper) + dot_nt(ones, lower)
    extra = jnp.broadcast_to(own_ref[rows:padded, :width].astype(F32)[0:1], (HEADS, width))
    extra = jnp.where(diagonal, extra, 0.0).astype(BF)
    extra_do = jnp.broadcast_to(do_ref[rows:padded, :].astype(F32)[0:1], (HEADS, width))
    extra_do = jnp.where(diagonal, extra_do, 0.0)
    extra_o = o_ref[rows:padded, :].astype(F32)[0:1]
    extra_delta = jnp.sum(extra_do * extra_o, axis=1, keepdims=True)
    extra_do = extra_do.astype(BF)
    extra_lse = lsex_ref[:, 0:1]
    tile_lane = lax.broadcasted_iota(jnp.int32, (HEADS, 16), 1)
    extra_dq = jnp.zeros((HEADS, width), F32)
    for ref, at, count, key_at, value_at, group, valid in parts:
        keys = ref[at : at + count, key_at : key_at + width]
        values = ref[at : at + count, value_at : value_at + width]
        prob = jnp.exp2(dot_nt(extra, keys) * factor - extra_lse)
        if valid is not None:
            prob = jnp.where(tile_lane < valid, prob, 0.0)
        score_grad = (prob * (dot_nt(extra_do, values) - extra_delta)).astype(BF)
        extra_dq = extra_dq + dot_nn(score_grad, keys)
        dk_acc[group, at : at + count, :] = dot_tn(score_grad, extra)
        dv_acc[group, at : at + count, :] = dot_tn(prob.astype(BF), extra_do)
    extra_dq = jnp.sum(jnp.where(diagonal, extra_dq, 0.0), axis=0, keepdims=True) * scale
    first = lax.broadcasted_iota(jnp.int32, (16, width), 0) < valid_ref[0]
    dq_ref[rows:, :] = jnp.where(first, jnp.broadcast_to(extra_dq, (16, width)), 0.0).astype(BF)
    dq_acc[...] = jnp.zeros_like(dq_acc)
    tile_row = lax.broadcasted_iota(jnp.int32, (16, rows), 0)

    def one_head(head, carry):
        start, offset = head_window(head, size, width)
        window = pl.ds(start, 256)
        lanes = lax.broadcasted_iota(jnp.int32, (rows, 256), 1)
        mask = (lanes >= offset) & (lanes < offset + size)
        zero = jnp.zeros((), BF)
        query = jnp.where(mask, own_ref[:rows, window], zero)
        out_grad = jnp.where(mask, do_ref[:rows, window], zero)
        lse = lse_ref[pl.ds(head, 1), :]
        row_delta = delta[pl.ds(head, 1), :]
        query_grad = jnp.zeros((256, rows), F32)
        for ref, at, count, key_at, value_at, group, valid in parts:
            keys = ref[at : at + count, pl.ds(pl.multiple_of(key_at + start, 128), 256)]
            values = ref[at : at + count, pl.ds(pl.multiple_of(value_at + start, 128), 256)]
            prob = jnp.exp2(dot_nt(keys, query) * factor - lse)
            if valid is not None:
                prob = jnp.where(tile_row < valid, prob, 0.0)
            score_grad = (prob * (dot_nt(values, out_grad) - row_delta)).astype(BF)
            dv_acc[group, at : at + count, window] += dot_nn(prob.astype(BF), out_grad)
            dk_acc[group, at : at + count, window] += dot_nn(score_grad, query)
            query_grad = query_grad + dot_tn(keys, score_grad)
        dq_acc[:, window] += jnp.where(mask, query_grad.T, 0.0)
        return carry

    lax.fori_loop(0, HEADS, one_head, 0)
    dq_ref[:rows, :] = (dq_acc[...] * scale).astype(BF)
    for group, dkv_ref in enumerate(dkv_refs):
        dkv_ref[:, :width] = (dk_acc[group] * scale).astype(dkv_ref.dtype)
        dkv_ref[:, width:] = dv_acc[group].astype(dkv_ref.dtype)


def attention_backward(valid, own, others, attended, attended_grad, lse, lse_extra):
    padded, wide = own.shape
    rows, width, groups = padded - 16, wide // 3, 1 + len(others)
    pairs = rows * groups * rows
    return pl.pallas_call(
        functools.partial(attention_backward_kernel, groups),
        out_shape=[shape_of((padded, width), BF)]
        + [shape_of((padded, 2 * width), BF) for _ in range(groups)],
        in_specs=[pl.BlockSpec(memory_space=pltpu.SMEM)] + in_vmem(groups + 4),
        out_specs=in_vmem(1 + groups),
        scratch_shapes=[
            pltpu.VMEM((rows, width), F32),
            pltpu.VMEM((groups, padded, width), F32),
            pltpu.VMEM((groups, padded, width), F32),
            pltpu.VMEM((HEADS, rows), F32),
        ],
        compiler_params=pltpu.CompilerParams(vmem_limit_bytes=60 * MIB),
        cost_estimate=pl.CostEstimate(
            flops=36 * pairs * width,
            bytes_accessed=2 * groups * padded * wide * 2,
            transcendentals=HEADS * pairs,
        ),
        name="attention_backward",
    )(valid, own, *others, attended, attended_grad, lse, lse_extra)


def mlp_kernel(
    units, unit, block, first_ref, bias_ref, rows_ref, n_own, n_other, dm_own, dm_other,
    out_own, out_other, dn_own, dn_other, gup_ref, gdown_ref, gbias_ref,
    out_acc, dn_acc, up_all, down_all, n_ref, dm_ref, sems,
):
    step = pl.program_id(0)

    @pl.when(step == 0)
    def _():
        copies = []
        for index in range(units):
            start = pl.multiple_of(first_ref[index], 16)
            for which, joined in enumerate((up_all, down_all)):
                copy = pltpu.make_async_copy(
                    rows_ref.at[pl.ds(start + which * unit, unit)],
                    joined.at[pl.ds(index * unit, unit)],
                    sems.at[2 * index + which],
                )
                copy.start()
                copies.append(copy)
        half = out_own.shape[0]
        for index, (source, joined, at) in enumerate(
            ((n_own, n_ref, 0), (n_other, n_ref, half), (dm_own, dm_ref, 0), (dm_other, dm_ref, half))
        ):
            copy = pltpu.make_async_copy(
                source, joined.at[pl.ds(at, half)], sems.at[2 * units + index]
            )
            copy.start()
            copies.append(copy)
        out_acc[...] = jnp.zeros_like(out_acc)
        dn_acc[...] = jnp.zeros_like(dn_acc)
        for copy in copies:
            copy.wait()

    span = pl.ds(pl.multiple_of(step * block, block), block)
    normed, dm, up, down = n_ref[...], dm_ref[...], up_all[span, :], down_all[span, :]
    hidden = dot_nt(normed, up) + bias_ref[...]
    below = 0.5 * (1.0 + lax.erf(hidden * (2.0**-0.5)))
    activated = (hidden * below).astype(BF)
    out_acc[...] += dot_nn(activated, down)
    gdown_ref[...] = dot_tn(activated, dm).astype(BF)
    slope = below + hidden * (jnp.exp(-0.5 * hidden * hidden) * (1.0 / math.sqrt(2 * math.pi)))
    hidden_grad = (dot_nt(dm, down) * slope).astype(BF)
    dn_acc[...] += dot_nn(hidden_grad, up)
    gup_ref[...] = dot_tn(hidden_grad, normed).astype(BF)
    gbias_ref[...] = jnp.sum(hidden_grad.astype(F32), axis=0, keepdims=True)
    half = out_own.shape[0]

    @pl.when(step == pl.num_programs(0) - 1)
    def _():
        out_own[...] = out_acc[:half, :]
        out_other[...] = out_acc[half:, :].astype(BF)
        dn_own[...] = dn_acc[:half, :]
        dn_other[...] = dn_acc[half:, :].astype(BF)


def mlp(normed, dm, bias, gathered, first_rows, block=384):
    half, width = normed[0].shape
    hidden = bias.shape[1]
    rows = 2 * half
    units = first_rows.shape[0]
    unit = hidden // units
    if unit % 16:
        wide = -(-unit // 16) * 16
        fill = ((0, 0), (0, wide - unit), (0, 0))
        gathered = jnp.pad(gathered.reshape(2 * units, unit, width), fill).reshape(-1, width)
        bias = jnp.pad(bias.reshape(units, unit), fill[:2]).reshape(1, -1)
        *outs, grad_up, grad_down, grad_bias = mlp(
            normed, dm, bias, gathered, first_rows // unit * wide, block
        )
        grads = [
            grad.reshape(units, wide, width)[:, :unit].reshape(hidden, width)
            for grad in (grad_up, grad_down)
        ]
        return *outs, *grads, grad_bias.reshape(units, wide)[:, :unit].reshape(1, hidden)
    whole = lambda step: (0, 0)
    part = lambda step: (step, 0)
    return pl.pallas_call(
        functools.partial(mlp_kernel, units, unit, block),
        grid=(hidden // block,),
        out_shape=[shape_of((half, width), dtype) for dtype in (F32, BF, F32, BF)]
        + [shape_of((hidden, width), BF)] * 2
        + [shape_of((1, hidden), F32)],
        in_specs=[
            pl.BlockSpec(memory_space=pltpu.SMEM),
            pl.BlockSpec((1, block), lambda step: (0, step)),
        ]
        + [pl.BlockSpec(memory_space=pl.ANY)] * 5,
        out_specs=[pl.BlockSpec((half, width), whole)] * 4
        + [pl.BlockSpec((block, width), part)] * 2
        + [pl.BlockSpec((1, block), lambda step: (0, step))],
        scratch_shapes=[pltpu.VMEM((rows, width), F32)] * 2
        + [pltpu.VMEM((hidden, width), BF)] * 2
        + [pltpu.VMEM((rows, width), BF)] * 2
        + [pltpu.SemaphoreType.DMA((2 * units + 4,))],
        compiler_params=pltpu.CompilerParams(vmem_limit_bytes=62 * MIB),
        cost_estimate=pl.CostEstimate(
            flops=12 * rows * width * hidden,
            bytes_accessed=8 * hidden * width + 16 * rows * width,
            transcendentals=2 * rows * hidden,
        ),
        name="mlp",
    )(first_rows.astype(jnp.int32), bias, gathered, *normed, *dm)


def column_blocks(width):
    return [(at, min(256, width - at)) for at in range(0, width, 256)]


def packed_rows(width, units):
    rows = sum((at + w) * w // 256 for at, w in column_blocks(width))
    return -(-rows // (16 * units)) * (16 * units)


def gram_into(slab, slab_t, out_ref):
    row = 0
    for at, w in column_blocks(slab.shape[1]):
        high = at + w
        value = dot_nn(slab_t[0:high, :], slab[:, at:high]).astype(BF)
        if w == 256:
            out_ref[row : row + high, :] = value
            row += high
        else:
            half = high // 2
            out_ref[row : row + half, 0:128] = value[:half]
            out_ref[row : row + half, 128:256] = value[half:]
            row += half
    out_ref[row:, :] = jnp.zeros((out_ref.shape[0] - row, 256), BF)


def unpack(packed, width, store):
    row = 0
    for at, w in column_blocks(width):
        high = at + w
        if w == 256:
            value = packed[row : row + high, :]
            row += high
        else:
            half = high // 2
            value = jnp.concatenate(
                [packed[row : row + half, 0:128], packed[row : row + half, 128:256]], axis=0
            )
            row += half
        store(at, w, value.astype(F32))


def store_both(ref, at, w, value):
    ref[0 : at + w, at : at + w] = value.astype(BF)
    if at:
        ref[at : at + w, 0:at] = value[0:at].T.astype(BF)


def on_diagonal(at, w):
    rows = lax.broadcasted_iota(jnp.int32, (at + w, w), 0)
    return rows == lax.broadcasted_iota(jnp.int32, (at + w, w), 1) + at


def symmetric_product(former, latter, width, done):
    for at, w in column_blocks(width):
        done(at, w, dot_nn(former[0 : at + w, :], latter[:, at : at + w]))


def deal(packed, offset_ref, kept, sent, sems):
    copies = []
    count, unit = kept.shape[0], kept.shape[1]
    for index in range(2 * count):
        start = pl.multiple_of(offset_ref[index], 16)
        out = kept if index < count else sent
        copy = pltpu.make_async_copy(
            packed.at[pl.ds(start, unit)], out.at[index % count], sems.at[index]
        )
        copy.start()
        copies.append(copy)
    for copy in copies:
        copy.wait()


def collect(pairs, offset_ref, packed, sems):
    copies = []
    unit = pairs[0].shape[1]
    for index, pair in enumerate(pairs):
        for side in (0, 1):
            at = side * len(pairs) + index
            start = pl.multiple_of(offset_ref[at], 16)
            copy = pltpu.make_async_copy(pair.at[side], packed.at[pl.ds(start, unit)], sems.at[at])
            copy.start()
            copies.append(copy)
    for copy in copies:
        copy.wait()


def gram_kernel(offset_ref, slab_ref, kept, sent, slab_t, packed, sems):
    slab_t[...] = slab_ref[...].T
    gram_into(slab_ref, slab_t, packed)
    deal(packed, offset_ref, kept, sent, sems)


SMEM = pl.BlockSpec(memory_space=pltpu.SMEM)
ANYWHERE = pl.BlockSpec(memory_space=pl.ANY)


def gram(slab, offsets):
    rows, width = slab.shape
    units = offsets.shape[0]
    size = packed_rows(width, units)
    part = shape_of((units // 2, size // units, 256), BF)
    return pl.pallas_call(
        gram_kernel,
        out_shape=[part, part],
        in_specs=[SMEM] + in_vmem(1),
        out_specs=[ANYWHERE] * 2,
        scratch_shapes=[
            pltpu.VMEM((width, rows), BF),
            pltpu.VMEM((size, 256), BF),
            pltpu.SemaphoreType.DMA((units,)),
        ],
        compiler_params=pltpu.CompilerParams(vmem_limit_bytes=50 * MIB),
        cost_estimate=pl.CostEstimate(
            flops=2 * rows * width * width,
            bytes_accessed=2 * rows * width + 2 * width * width,
            transcendentals=0,
        ),
        name="gram",
    )(offsets, slab)


def first_steps_kernel(count, offset_ref, slab_ref, *refs):
    pairs, refs = refs[:count], refs[count:]
    slab_out, kept, sent = refs[:3]
    gram_f, mix_f, prod_f, poly_f, gram_b, mix_b, prod_b, poly_b, slab_t, packed, sems = refs[3:]
    width = slab_ref.shape[1]
    collect(pairs, offset_ref, packed, sems)
    square = [jnp.zeros((1, 1), F32)]

    def add_diagonal(at, w, value):
        here = jnp.where(on_diagonal(at, w), value, 0.0)
        square[0] = square[0] + jnp.sum(here, keepdims=True).reshape(1, 1)

    unpack(packed, width, add_diagonal)
    inverse = 1.0 / (jnp.sqrt(square[0]) + 1e-07)

    def start(at, w, value):
        value = value * inverse * inverse
        gram_f[0 : at + w, at : at + w] = value
        store_both(gram_b, at, w, value)

    unpack(packed, width, start)
    lead = 1.0
    for step in range(FIRST_STEPS):
        def make_mix(at, w, value):
            span = (slice(0, at + w), slice(at, at + w))
            mix = poly_second * gram_f[span] + poly_third * value
            mix_f[span] = mix
            store_both(mix_b, at, w, mix)
            if step == 0:
                poly_f[span] = mix
                store_both(poly_b, at, w, mix)

        symmetric_product(gram_b, gram_b, width, make_mix)
        if step > 0:

            def join(at, w, value):
                span = (slice(0, at + w), slice(at, at + w))
                poly = poly_first * poly_f[span] + lead * mix_f[span] + value
                poly_f[span] = poly
                store_both(prod_b, at, w, poly)

            symmetric_product(mix_b, poly_b, width, join)
            poly_b, prod_b = prod_b, poly_b
        lead = lead * poly_first
        if step < FIRST_STEPS - 1:

            def keep(at, w, value):
                prod_f[0 : at + w, at : at + w] = value
                store_both(prod_b, at, w, value)

            symmetric_product(gram_b, mix_b, width, keep)

            def next_gram(at, w, value):
                span = (slice(0, at + w), slice(at, at + w))
                new = poly_first**2 * gram_f[span] + 2 * poly_first * prod_f[span] + value
                gram_f[span] = new
                store_both(gram_b, at, w, new)

            symmetric_product(prod_b, mix_b, width, next_gram)
    slab = slab_ref[...]
    moved = ((lead * slab.astype(F32) + dot_nn(slab, poly_b[...])) * inverse).astype(BF)
    slab_out[...] = moved
    slab_t[...] = moved.T
    gram_into(moved, slab_t, packed)
    deal(packed, offset_ref, kept, sent, sems)


def first_steps(pairs, slab, offsets):
    rows, width = slab.shape
    square = (width, width)
    units = offsets.shape[0]
    size = packed_rows(width, units)
    part = shape_of((units // 2, size // units, 256), BF)
    return pl.pallas_call(
        functools.partial(first_steps_kernel, len(pairs)),
        out_shape=[shape_of((rows, width), BF), part, part],
        in_specs=[SMEM] + in_vmem(1) + [ANYWHERE] * len(pairs),
        out_specs=in_vmem(1) + [ANYWHERE] * 2,
        scratch_shapes=[pltpu.VMEM(square, F32)] * 4
        + [pltpu.VMEM(square, BF)] * 4
        + [pltpu.VMEM((width, rows), BF), pltpu.VMEM((size, 256), BF)]
        + [pltpu.SemaphoreType.DMA((units,))],
        compiler_params=pltpu.CompilerParams(vmem_limit_bytes=60 * MIB),
        cost_estimate=pl.CostEstimate(
            flops=18 * width**3,
            bytes_accessed=4 * rows * width + 4 * width * width,
            transcendentals=0,
        ),
        name="first_steps",
    )(offsets, slab, *pairs)


def last_steps_kernel(count, offset_ref, slab_ref, *refs):
    pairs, refs = refs[:count], refs[count:]
    slab_out, gram_b, poly_b, prod_b, join_b, packed, sems = refs
    width = slab_ref.shape[1]
    collect(pairs, offset_ref, packed, sems)
    unpack(packed, width, lambda at, w, value: store_both(gram_b, at, w, value))
    for step in range(LAST_STEPS):

        def make_poly(at, w, value):
            held = gram_b[0 : at + w, at : at + w].astype(F32)
            poly = poly_second * held + poly_third * value
            poly = poly + jnp.where(on_diagonal(at, w), poly_first, 0.0)
            store_both(poly_b, at, w, poly)
            if step == 0:
                store_both(join_b, at, w, poly)

        symmetric_product(gram_b, gram_b, width, make_poly)
        if step > 0:
            symmetric_product(
                poly_b, join_b, width, lambda at, w, value: store_both(prod_b, at, w, value)
            )
            join_b, prod_b = prod_b, join_b
        if step < LAST_STEPS - 1:
            symmetric_product(
                gram_b, poly_b, width, lambda at, w, value: store_both(prod_b, at, w, value)
            )
            symmetric_product(
                prod_b, poly_b, width, lambda at, w, value: store_both(gram_b, at, w, value)
            )
    slab_out[...] = dot_nn(slab_ref[...], join_b[...]).astype(BF)


def last_steps(pairs, slab, offsets):
    rows, width = slab.shape
    units = offsets.shape[0]
    size = packed_rows(width, units)
    return pl.pallas_call(
        functools.partial(last_steps_kernel, len(pairs)),
        out_shape=shape_of((rows, width), BF),
        in_specs=[SMEM] + in_vmem(1) + [ANYWHERE] * len(pairs),
        out_specs=in_vmem(1)[0],
        scratch_shapes=[pltpu.VMEM((width, width), BF)] * 4
        + [pltpu.VMEM((size, 256), BF), pltpu.SemaphoreType.DMA((units,))],
        compiler_params=pltpu.CompilerParams(vmem_limit_bytes=60 * MIB),
        cost_estimate=pl.CostEstimate(
            flops=10 * width**3,
            bytes_accessed=4 * rows * width + 2 * width * width,
            transcendentals=0,
        ),
        name="last_steps",
    )(offsets, slab, *pairs)


def line_up_kernel(counts, place_ref, *refs):
    line, qkv, proj, small_at = counts
    blocks, (former, latter, held, joined) = refs[:line], refs[line:]
    for step, block in enumerate(blocks):
        held[step] = block[...]
    total = None
    for index in range(line):
        step = lax.rem(place_ref[0] - index + line, line)
        value = held[step].astype(F32)
        joined[index * qkv : (index + 1) * qkv, :] = value[:qkv]
        at = line * qkv + index * proj
        joined[at : at + proj, :] = value[qkv : qkv + proj]
        small = value[small_at:]
        total = small if total is None else total + small
    half = former.shape[0]
    rest = line * (qkv + proj) - half
    former[...] = joined[:half, :].astype(BF)
    latter[:rest, :] = joined[half:, :].astype(BF)
    latter[rest:, :] = total.astype(BF)


def line_up(blocks, place, qkv, proj):
    line = len(blocks)
    rows, width = blocks[0].shape
    small_at = -(-(qkv + proj) // 16) * 16
    half = line * (qkv + proj) // 2
    return pl.pallas_call(
        functools.partial(line_up_kernel, (line, qkv, proj, small_at)),
        out_shape=[
            shape_of((half, width), BF),
            shape_of((line * (qkv + proj) - half + rows - small_at, width), BF),
        ],
        in_specs=[SMEM] + in_vmem(line),
        out_specs=in_vmem(2),
        scratch_shapes=[
            pltpu.VMEM((line, rows, width), BF),
            pltpu.VMEM((line * (qkv + proj), width), F32),
        ],
        compiler_params=pltpu.CompilerParams(vmem_limit_bytes=40 * MIB),
        name="line_up",
    )(place.reshape(1), *blocks)


def packed_grad_kernel(offset_ref, query_ref, own_ref, arrived_ref, other_ref, packed, kept, sent, grad, sems):
    width = query_ref.shape[1]
    packed[:, :width] = query_ref[...]
    total = own_ref[...].astype(F32) + arrived_ref[...].astype(F32)
    packed[:, width:] = total.astype(BF)
    qkv_grad_kernel(offset_ref, packed, other_ref, kept, sent, grad, sems)


def packed_grad_of(query_grad, own, arrived, other_side, offsets):
    rows, width = query_grad.shape
    long = 3 * width
    units = offsets.shape[0]
    unit = long // units
    if unit % 16:
        total = (own.astype(F32) + arrived.astype(F32)).astype(BF)
        packed = jnp.concatenate([query_grad, total], axis=1)
        return packed, *qkv_grad(packed, other_side, offsets)
    part = shape_of((units // 2, unit, width), BF)
    return pl.pallas_call(
        packed_grad_kernel,
        out_shape=[shape_of((rows, long), BF), part, part],
        in_specs=[SMEM] + in_vmem(4),
        out_specs=in_vmem(1) + [ANYWHERE] * 2,
        scratch_shapes=[pltpu.VMEM((long, width), BF), pltpu.SemaphoreType.DMA((units,))],
        compiler_params=pltpu.CompilerParams(vmem_limit_bytes=50 * MIB),
        cost_estimate=pl.CostEstimate(
            flops=2 * rows * long * width,
            bytes_accessed=2 * rows * (2 * long + width) + 2 * long * width,
            transcendentals=0,
        ),
        name="packed_grad",
    )(offsets, query_grad, own, arrived, other_side)


def first_norm_kernel(packed_ref, weight_ref, standard_ref, inverse_ref, after_ref, gain_ref, low_ref, sums_ref):
    grad = dot_nn(packed_ref[...], weight_ref[...])
    standard = standard_ref[...]
    sums_ref[...] = jnp.zeros_like(sums_ref)
    sums_ref[0:1, :] = jnp.sum(grad * standard, axis=0, keepdims=True)
    sums_ref[1:2, :] = jnp.sum(grad, axis=0, keepdims=True)
    scaled = grad * gain_ref[...]
    average = jnp.mean(scaled, axis=1, keepdims=True)
    along = jnp.mean(scaled * standard, axis=1, keepdims=True)
    token = after_ref[...] + inverse_ref[...] * (scaled - average - standard * along)
    low_ref[...] = token.astype(BF)
    rows = token.shape[0] - 16
    sums_ref[8:16, :] = token[rows : rows + 8, :]


def first_norm_back(packed_grad, weight, standard, inverse, after, gain):
    rows, width = standard.shape
    long = weight.shape[0]
    low, sums = pl.pallas_call(
        first_norm_kernel,
        out_shape=[shape_of((rows, width), BF), shape_of((16, width), F32)],
        in_specs=in_vmem(6),
        out_specs=in_vmem(2),
        compiler_params=pltpu.CompilerParams(vmem_limit_bytes=60 * MIB),
        cost_estimate=pl.CostEstimate(
            flops=2 * rows * long * width,
            bytes_accessed=2 * rows * (long + 5 * width) + 2 * long * width,
            transcendentals=0,
        ),
        name="first_norm_back",
    )(packed_grad, weight, standard, inverse, after, gain)
    return low, sums[0:2], sums[8:9]


def qkv_grad_kernel(offset_ref, long_ref, other_ref, kept, sent, grad, sems):
    other = other_ref[...]
    for at, w in [(at, 384) for at in range(0, grad.shape[0], 384)]:
        grad[at : at + w, :] = dot_tn(long_ref[:, at : at + w], other).astype(BF)
    deal(grad, offset_ref, kept, sent, sems)


def qkv_grad(long_side, other_side, offsets):
    rows, long = long_side.shape
    width = other_side.shape[1]
    units = offsets.shape[0]
    unit = long // units
    if unit % 16:
        grad = dot_tn(long_side, other_side).astype(BF).reshape(units, unit, width)
        parts = [
            lax.dynamic_index_in_dim(grad, offsets[index] // unit, 0, False)
            for index in range(units)
        ]
        return jnp.stack(parts[: units // 2]), jnp.stack(parts[units // 2 :])
    part = shape_of((units // 2, unit, width), BF)
    return pl.pallas_call(
        qkv_grad_kernel,
        out_shape=[part, part],
        in_specs=[SMEM] + in_vmem(2),
        out_specs=[ANYWHERE] * 2,
        scratch_shapes=[pltpu.VMEM((long, width), BF), pltpu.SemaphoreType.DMA((units,))],
        compiler_params=pltpu.CompilerParams(vmem_limit_bytes=50 * MIB),
        cost_estimate=pl.CostEstimate(
            flops=2 * rows * long * width,
            bytes_accessed=2 * rows * (long + width) + 2 * long * width,
            transcendentals=0,
        ),
        name="qkv_grad",
    )(offsets, long_side, other_side)


def place_kernel(moves, count, outputs, offset_ref, *refs):
    pieces, outs, sems = refs[:count], refs[count : count + outputs], refs[count + outputs]
    copies = []
    for index, (piece, at, rows, out, _) in enumerate(moves):
        start = pl.multiple_of(offset_ref[index], 16)
        copy = pltpu.make_async_copy(
            pieces[piece].at[pl.ds(at, rows)], outs[out].at[pl.ds(start, rows)], sems.at[index]
        )
        copy.start()
        copies.append(copy)
    for copy in copies:
        copy.wait()


def place(pieces, moves, sizes):
    width = pieces[0].shape[1]
    if any(at % 16 or rows % 16 for _, at, rows, _, _ in moves):
        outs = [jnp.zeros((size, width), BF) for size in sizes]
        for piece, at, rows, out, offset in moves:
            part = pieces[piece][at : at + rows]
            outs[out] = lax.dynamic_update_slice_in_dim(outs[out], part, offset, 0)
        return outs
    offsets = jnp.stack([move[4] for move in moves]).astype(jnp.int32)
    static = [move[:4] + (None,) for move in moves]
    return pl.pallas_call(
        functools.partial(place_kernel, static, len(pieces), len(sizes)),
        out_shape=[shape_of((size, width), BF) for size in sizes],
        in_specs=[pl.BlockSpec(memory_space=pltpu.SMEM)]
        + [pl.BlockSpec(memory_space=pl.ANY)] * len(pieces),
        out_specs=in_vmem(len(sizes)),
        scratch_shapes=[pltpu.SemaphoreType.DMA((len(moves),))],
        compiler_params=pltpu.CompilerParams(vmem_limit_bytes=40 * MIB),
        cost_estimate=pl.CostEstimate(
            flops=0, bytes_accessed=4 * sum(sizes) * width, transcendentals=0
        ),
        name="place",
    )(offsets, *pieces)


def together_kernel(*refs):
    pass


def together(*arrays, cost=0):
    anywhere = pl.BlockSpec(memory_space=pl.ANY)
    return pl.pallas_call(
        together_kernel,
        out_shape=[shape_of(array.shape, array.dtype) for array in arrays],
        in_specs=[anywhere] * len(arrays),
        out_specs=[anywhere] * len(arrays),
        input_output_aliases={index: index for index in range(len(arrays))},
        cost_estimate=pl.CostEstimate(flops=cost, bytes_accessed=0, transcendentals=0),
        name="together",
    )(*arrays)


def beside(*arrays):
    got = together(*arrays, cost=10**11)
    return got if len(arrays) > 1 else got[0]


def shift(values, step, seq_count):
    return lax.ppermute(
        values, "seq", [(rank, (rank + step) % seq_count) for rank in range(seq_count)]
    )


def swap(values, bit, batch_count):
    return lax.ppermute(values, "batch", [(rank, rank ^ bit) for rank in range(batch_count)])


def line_gather(values, seq_count):
    return [values] + [shift(values, step, seq_count) for step in range(1, seq_count)]


def line_reduce(blocks, seq_count):
    total = blocks[0].astype(F32)
    for step in range(1, seq_count):
        total = total + shift(blocks[step], -step, seq_count).astype(F32)
    return total


def from_own(values, seq_count):
    rank = lax.axis_index("seq")
    blocks = values.reshape(seq_count, -1, values.shape[1])
    return [
        lax.dynamic_index_in_dim(blocks, (rank - step) % seq_count, 0, False)
        for step in range(seq_count)
    ]


def in_line(blocks, seq_count):
    stacked = jnp.stack(blocks)
    rank = lax.axis_index("seq")
    order = (rank - jnp.arange(seq_count, dtype=jnp.int32)) % seq_count
    return jnp.take(stacked, order, axis=0)


def plane_gather(block, bits, batch_count):
    blocks = {0: block}
    for bit in bits:
        for mask in list(blocks):
            blocks[mask ^ bit] = swap(blocks[mask], bit, batch_count)
    return blocks


def plane_reduce(blocks, bits, batch_count):
    blocks = dict(blocks)
    for bit in bits:
        kept = [mask for mask in blocks if not mask & bit]
        rows = blocks[0].shape[0]
        arrived = swap(jnp.concatenate([blocks[mask ^ bit] for mask in kept], axis=0), bit, batch_count)
        blocks = {
            mask: (
                blocks[mask].astype(F32) + arrived[index * rows : (index + 1) * rows].astype(F32)
            ).astype(BF)
            for index, mask in enumerate(kept)
        }
    return blocks[0]


def gather_small(values, batch_count, seq_count):
    return gather_batch(in_line(line_gather(values, seq_count), seq_count), batch_count)


def gather_batch(values, batch_count):
    joined = values[None]
    bit = 1
    while bit < batch_count:
        joined = jnp.concatenate([joined, swap(joined, bit, batch_count)], axis=0)
        bit *= 2
    order = lax.axis_index("batch") ^ jnp.arange(batch_count, dtype=jnp.int32)
    return jnp.take(joined, order, axis=0)


def standardize(values):
    average = jnp.mean(values, axis=-1, keepdims=True)
    centred = values - average
    variance = jnp.mean(centred * centred, axis=-1, keepdims=True)
    inverse = lax.rsqrt(variance + norm_eps)
    return centred * inverse, inverse


def standardize_back(grad, standard, inverse):
    average = jnp.mean(grad, axis=-1, keepdims=True)
    along = jnp.mean(grad * standard, axis=-1, keepdims=True)
    return inverse * (grad - average - standard * along)


def time_token(step_values, model_width):
    half_width = model_width // 2
    frequency = jnp.exp(-math.log(10000.0) * jnp.arange(half_width, dtype=F32) / half_width)
    angles = step_values.astype(F32)[:, None] * frequency[None, :]
    return jnp.concatenate([jnp.cos(angles), jnp.sin(angles)], axis=-1)


def adam_step(parameter, first_state, second, gradient):
    first_new = beta_one * first_state + (1.0 - beta_one) * gradient
    second_new = beta_two * second + (1.0 - beta_two) * gradient * gradient
    first_hat = first_new / (1.0 - beta_one**STEP)
    second_hat = second_new / (1.0 - beta_two**STEP)
    return (
        first_new,
        second_new,
        parameter - adam_rate * first_hat / (jnp.sqrt(second_hat) + adam_eps),
    )


def body(
    patches, timesteps, labels, next_grad, skip_grad, next_extra, skip_extra,
    w_qkv, w_proj, w_up, w_down, mom_qkv, mom_proj, mom_up, mom_down,
    vectors, vec_first, vec_second, table, table_first, table_second,
):
    images, patch_rows, width = patches.shape
    batch_count = lax.axis_size("batch")
    seq_count = lax.axis_size("seq")
    shards = batch_count * seq_count
    batch_rank = lax.axis_index("batch")
    seq_rank = lax.axis_index("seq")
    shard_rank = batch_rank * seq_count + seq_rank
    core = batch_rank % 2
    chips = seq_count // (2 * images)
    own_image = seq_rank // chips
    own_core, own_slot = own_image // images, own_image % images
    sub_rank = seq_rank % chips
    bits = [1 << level for level in range(1, (batch_count - 1).bit_length())]
    up_bits, down_bits = bits, bits[::-1]

    def route(matching):
        pairs = []
        for rank in range(batch_count):
            for place_z in range(seq_count):
                code = place_z ^ matching
                slot, rest = code // (2 * chips), code % (2 * chips)
                to_core, sub = rest // chips, rest % chips
                to_z = ((rank % 2) * images + slot) * chips + sub
                pairs.append((rank * seq_count + place_z, (rank - rank % 2 + to_core) * seq_count + to_z))
        return pairs

    piece_rows = images * patch_rows // seq_count

    def send(values):
        pieces = values.reshape(seq_count, piece_rows, width)
        return [
            lax.ppermute(
                lax.dynamic_index_in_dim(pieces, seq_rank ^ matching, 0, False),
                ("batch", "seq"),
                route(matching),
            )
            for matching in range(seq_count)
        ]

    def send_back(values):
        pieces = jnp.stack([array.reshape(seq_count, piece_rows, width) for array in values], axis=1)
        return [
            lax.ppermute(
                pieces[matching], ("batch", "seq"), [(to, at) for at, to in route(matching)]
            )
            for matching in range(seq_count)
        ]

    def join_back(moved, index):
        moved = jnp.stack([piece[index] for piece in moved])
        pieces = [
            lax.dynamic_index_in_dim(moved, seq_rank ^ code, 0, True) for code in range(seq_count)
        ]
        return jnp.concatenate(pieces, axis=0).reshape(images, patch_rows, width)

    rows = seq_count * piece_rows
    padded = rows + 16

    low_qkv = w_qkv.astype(BF).T
    low_proj = w_proj.astype(BF).T
    unit_width, qkv_width, proj_width = w_up.shape[1], low_qkv.shape[0], low_proj.shape[0]
    column_count = table.shape[1]
    class_count = table.shape[0]
    masks = [level << 1 for level in range(batch_count // 2)]
    offsets = batch_rank ^ jnp.array(masks + [mask ^ 1 for mask in masks], jnp.int32)

    own_mlp = jnp.concatenate([w_up.astype(BF).T, w_down.astype(BF)], axis=0)

    facts = lax.all_gather(jnp.stack([timesteps, labels]), "batch", axis=0)
    all_labels = facts[:, 1].reshape(-1)
    selector = (
        all_labels[:, None] == jnp.arange(class_count, dtype=jnp.int32)[None, :]
    ).astype(BF)
    class_part = dot_nn(selector, table.astype(BF)).astype(BF)
    small = jnp.concatenate([vectors.astype(BF), class_part], axis=0)
    small_rows = -(-small.shape[0] // 16) * 16
    small = lax.dynamic_update_slice(
        jnp.zeros((small_rows, width), BF), small, (0, shard_rank * column_count)
    )

    gap = -(qkv_width + proj_width) % 16
    load = [low_qkv, low_proj] + ([jnp.zeros((gap, width), BF)] if gap else []) + [small]
    line = line_gather(jnp.concatenate(load, axis=0), seq_count)
    former, latter = line_up(line, seq_rank, qkv_width, proj_width)
    former, latter, patches, own_mlp = together(former, latter, patches, own_mlp)

    same_core = [
        [rank * seq_count + at for rank in range(side, batch_count, 2) for at in range(seq_count)]
        for side in (0, 1)
    ]
    all_mlp = lax.all_gather(
        own_mlp, ("batch", "seq"), axis=0, tiled=True, axis_index_groups=same_core
    )
    qkv_rows, proj_rows = qkv_width * seq_count, proj_width * seq_count

    def spread_start(former, latter):
        return (
            {mask: swap(former, mask, batch_count) for mask in bits},
            {mask: swap(latter, mask, batch_count) for mask in bits},
        )

    def spread_rest(former, latter, arrived):
        former_got, latter_got = dict(arrived[0]), dict(arrived[1])
        former_got[0], latter_got[0] = former, latter
        for got, order in ((former_got, bits), (latter_got, bits[::-1])):
            for index, bit in enumerate(order):
                lower = order[:index]
                for mask in [m for m in list(got) if m and not m & bit]:
                    if all(not (mask & other) or other in lower for other in bits):
                        if (mask ^ bit) not in got:
                            got[mask ^ bit] = swap(got[mask], bit, batch_count)
        return former_got, latter_got

    def flat(groups):
        return [group[mask] for group in groups for mask in sorted(group)]

    def unflat(arrays, groups):
        arrays = list(arrays)
        return [{mask: arrays.pop(0) for mask in sorted(group)} for group in groups]

    arrived = spread_start(former, latter)
    moved_patches = send(patches)
    gathered = spread_rest(former, latter, arrived)
    grad_in = (next_grad.astype(F32) + skip_grad.astype(F32)).astype(BF)
    grad_in, *got = together(grad_in, *flat(gathered), *moved_patches)
    moved_grad = send(grad_in)
    moved_patches = jnp.concatenate(got[len(got) - seq_count :], axis=0)
    gathered = unflat(got[: len(got) - seq_count], gathered)
    pieces, moves, small = [], [], 0.0
    unit = former.shape[0]
    rest = qkv_rows - unit
    for group, blocks in enumerate(gathered):
        for mask in masks:
            for side in (0, 1):
                block = swap(blocks[mask], 1, batch_count) if side else blocks[mask]
                target = batch_rank ^ mask ^ side
                number = len(pieces)
                pieces.append(block)
                if group == 0:
                    moves.append((number, 0, unit, 0, target * qkv_rows))
                else:
                    moves.append((number, 0, rest, 0, target * qkv_rows + unit))
                    moves.append((number, rest, proj_rows, 1, target * proj_rows))
                    small = small + block[rest + proj_rows :].astype(F32)
    full_qkv, full_proj = place(pieces, moves, [qkv_rows * batch_count, proj_rows * batch_count])
    vec_values, class_rows = small[:10], small[10 : 10 + images * batch_count]
    home = batch_rank - core + own_core
    own_time = lax.dynamic_index_in_dim(facts[:, 0].reshape(-1), home * images + own_slot, 0, True)
    time_row = time_token(own_time, width)
    class_row = lax.dynamic_index_in_dim(class_rows, home * images + own_slot, 0, True)
    has_extra = sub_rank == 0
    extra_row = jnp.where(core == 0, time_row, class_row) * has_extra.astype(F32)
    row_index = lax.broadcasted_iota(jnp.int32, (padded, 1), 0)
    row_valid = (row_index < rows + has_extra.astype(jnp.int32)).astype(F32)
    first_row = lax.broadcasted_iota(jnp.int32, (16, 1), 0) == 0

    extra_tile = jnp.where(first_row, extra_row, 0.0)
    tokens = jnp.concatenate([moved_patches.astype(F32), extra_tile], axis=0)
    standard_one, inverse_one = standardize(tokens)
    normed = ((standard_one * vec_values[0] + vec_values[1]) * row_valid).astype(BF)
    packed = dot_nt(normed, full_qkv).astype(BF)

    def rotate(values, step, core_bit, back):
        pairs = []
        for rank in range(batch_count):
            for place_z in range(seq_count):
                base, sub = place_z - place_z % chips, place_z % chips
                source = (rank ^ core_bit) * seq_count + base + (sub + step) % chips
                here = rank * seq_count + place_z
                pairs.append((here, source) if back else (source, here))
        return lax.ppermute(values, ("batch", "seq"), pairs)

    peers = [(step, bit) for step in range(chips) for bit in (0, 1)][1:]
    sooner = seq_count // 2
    packed, *moved_grad[:sooner] = together(packed, *moved_grad[:sooner])
    own_kv = packed[:, width:]
    other_kv = [rotate(own_kv, step, bit, False) for step, bit in peers]
    valid = jnp.stack(
        [has_extra.astype(jnp.int32)]
        + [((sub_rank + step) % chips == 0).astype(jnp.int32) for step, bit in peers]
    )
    in_extra = (next_extra.astype(F32) + skip_extra.astype(F32)).astype(BF)
    in_extra_other = swap(in_extra, 1, batch_count)
    attended, lse, lse_extra = attention_forward(valid, packed, other_kv)
    attended, in_extra_other, *moved_grad = together(attended, in_extra_other, *moved_grad)
    in_extra = jnp.where(own_core == core, in_extra, in_extra_other)
    in_extra = lax.dynamic_index_in_dim(in_extra, own_slot, 0, False)
    in_extra = lax.dynamic_index_in_dim(in_extra, core, 0, True)
    in_extra = jnp.where(first_row & has_extra, in_extra, jnp.zeros_like(in_extra))
    incoming_low = jnp.concatenate([*moved_grad, in_extra], axis=0)
    incoming = incoming_low.astype(F32)
    other_incoming = swap(incoming_low, 1, batch_count)
    line_order = (seq_rank - jnp.arange(seq_count, dtype=jnp.int32)) % seq_count
    chip_order = (batch_rank ^ jnp.array(masks, jnp.int32)) >> 1
    first_rows = (chip_order[:, None] * seq_count + line_order[None, :]).reshape(-1) * (2 * unit_width)
    all_bias = vec_values[6:].reshape(batch_count // 2, 2, seq_count, unit_width)
    core_bias = lax.dynamic_index_in_dim(all_bias, core, 1, False)
    core_bias = jnp.take(jnp.take(core_bias, chip_order, axis=0), line_order, axis=1).reshape(1, -1)
    middle = tokens + (dot_nt(attended, full_proj) + vec_values[4]) * row_valid
    standard_two, inverse_two = standardize(middle)
    normed_two = ((standard_two * vec_values[2] + vec_values[3]) * row_valid).astype(BF)
    other_normed = swap(normed_two, 1, batch_count)
    out_own, out_other, dn_own, dn_other, grad_up, grad_down, grad_bias = mlp(
        (normed_two, other_normed), (incoming_low, other_incoming), core_bias, all_mlp, first_rows
    )

    def blocks_of(grad):
        parts = grad.reshape(len(masks), -1, width)
        return {mask: parts[index] for index, mask in enumerate(masks)}

    def sum_start(groups):
        moved = []
        for blocks, bit in zip(groups, (bits[-1], bits[0])):
            kept = [mask for mask in masks if not mask & bit]
            moved.append(swap(jnp.concatenate([blocks[mask ^ bit] for mask in kept], axis=0), bit, batch_count))
        return moved

    def sum_add(groups, moved):
        sums = []
        for blocks, arrived, bit in zip(groups, moved, (bits[-1], bits[0])):
            kept = [mask for mask in masks if not mask & bit]
            count = blocks[0].shape[0]
            sums.append(
                {
                    mask: (
                        blocks[mask].astype(F32)
                        + arrived[index * count : (index + 1) * count].astype(F32)
                    ).astype(BF)
                    for index, mask in enumerate(kept)
                }
            )
        return sums

    def sum_rest(groups):
        return [
            plane_reduce(blocks, order, batch_count)
            for blocks, order in zip(groups, (bits[::-1][1:], bits[1:]))
        ]

    def line_blocks(former, latter):
        joined = [values.reshape(seq_count, -1, width) for values in (former, latter)]
        return jnp.concatenate(joined, axis=1)

    mlp_groups = [blocks_of(grad_up), blocks_of(grad_down)]
    moved = sum_start(mlp_groups)
    normed_two_grad = dn_own + swap(dn_other, 1, batch_count).astype(F32)
    middle_grad = incoming + standardize_back(
        normed_two_grad * vec_values[2], standard_two, inverse_two
    )
    middle_low = middle_grad.astype(BF)

    attended_grad = dot_nn(middle_low, full_proj).astype(BF)
    out_arrived = swap(out_other, 1, batch_count)
    backward = attention_backward(valid, packed, other_kv, attended, attended_grad, lse, lse_extra)
    *backward, moved_up, moved_down, out_arrived, middle_low, attended, middle = together(
        *backward, *moved, out_arrived, middle_low, attended, middle
    )
    mlp_groups = sum_add(mlp_groups, [moved_up, moved_down])

    def halves(values):
        cut = values.shape[1] // 32 * 16
        cut = cut if cut else values.shape[1] // 2
        return [
            {mask: part[index] for index, mask in enumerate(masks)}
            for part in (values[:, :cut], values[:, cut:])
        ]

    def next_axis(groups, orders):
        moved = []
        for blocks, order in zip(groups, orders):
            kept = [mask for mask in blocks if not mask & order[0]]
            load = jnp.concatenate([blocks[mask ^ order[0]] for mask in kept], axis=0)
            moved.append(swap(load, order[0], batch_count))
        return moved

    def next_add(groups, orders, moved):
        sums = []
        for blocks, order, arrived in zip(groups, orders, moved):
            kept = [mask for mask in blocks if not mask & order[0]]
            count = blocks[0].shape[0]
            sums.append(
                plane_reduce(
                    {
                        mask: (
                            blocks[mask].astype(F32)
                            + arrived[index * count : (index + 1) * count].astype(F32)
                        ).astype(BF)
                        for index, mask in enumerate(kept)
                    },
                    order[1:],
                    batch_count,
                )
            )
        return sums

    orders = (bits[::-1][1:], bits[1:])
    mlp_moved = next_axis(mlp_groups, orders)
    query_grad, own_dkv = backward[0], backward[1]
    arrived = [rotate(term, step, bit, True) for (step, bit), term in zip(peers, backward[2:])]
    middle_low, attended = beside(middle_low, attended)
    proj_kept, proj_sent = qkv_grad(middle_low, attended, offsets * proj_rows)
    own_dkv, proj_kept, proj_sent, *arrived = together(own_dkv, proj_kept, proj_sent, *arrived)

    proj_arrived = swap(proj_sent, 1, batch_count)
    far_dkv = arrived[0]
    for term in arrived[1:]:
        far_dkv = (far_dkv.astype(F32) + term.astype(F32)).astype(BF)
    packed_grad, kept, sent = packed_grad_of(
        query_grad, own_dkv, far_dkv, normed, offsets * qkv_rows
    )
    packed_grad, kept, sent, proj_kept, proj_arrived, *mlp_moved = together(
        packed_grad, kept, sent, proj_kept, proj_arrived, *mlp_moved
    )

    arrived = swap(sent, 1, batch_count)
    proj_kept, proj_arrived, *mlp_moved = beside(proj_kept, proj_arrived, *mlp_moved)
    mlp_up, mlp_down = next_add(mlp_groups, orders, mlp_moved)
    joined = line_blocks(mlp_up, mlp_down)
    proj_groups = halves((proj_kept.astype(F32) + proj_arrived.astype(F32)).astype(BF))
    joined = [joined[step] for step in range(seq_count)]
    arrived, *joined = together(arrived, *joined)

    groups = halves((kept.astype(F32) + arrived.astype(F32)).astype(BF))
    moved = sum_start(groups)
    near_steps = (1, seq_count - 1)
    far_steps = tuple(range(2, seq_count - 1))
    near_line = [shift(joined[step], -step, seq_count) for step in near_steps]
    first_proj = sum_start(proj_groups)
    packed_grad = beside(packed_grad)
    token_low, norm_sums, extra_grad = first_norm_back(
        packed_grad, full_qkv, standard_one, inverse_one, middle_grad, vec_values[0:1]
    )
    far_line = [joined[step] for step in far_steps]
    moved_up, moved_down, token_low, norm_sums, extra_grad, *got = together(
        *moved, token_low, norm_sums, extra_grad, *near_line, *far_line, *first_proj
    )
    near_line, far_line, first_proj = got[:2], got[2:-2], got[-2:]
    far_line = [shift(part, -step, seq_count) for step, part in zip(far_steps, far_line)]
    bias_parts = jnp.take(grad_bias.reshape(len(masks), seq_count, -1), line_order, axis=1)
    bias_sum = jnp.zeros((batch_count // 2, seq_count, unit_width), F32)
    bias_sum = jnp.take(bias_parts, (batch_rank ^ jnp.arange(0, batch_count, 2)) >> 1, axis=0)
    bias_sum = jnp.where(
        jnp.arange(2, dtype=jnp.int32)[None, :, None, None] == core, bias_sum[:, None], 0.0
    )
    class_slots = jnp.arange(images * batch_count, dtype=jnp.int32) == home * images + own_slot
    holds_class = (core == 1) & has_extra
    class_grad = jnp.where((class_slots & holds_class)[:, None], extra_grad, 0.0)
    vec_grad = jnp.concatenate(
        [
            norm_sums,
            jnp.sum(normed_two_grad * standard_two, axis=0)[None],
            jnp.sum(normed_two_grad, axis=0)[None],
            jnp.sum(middle_low.astype(F32), axis=0)[None],
            jnp.sum(incoming_low.astype(F32), axis=0)[None],
            bias_sum.reshape(4, width),
            class_grad,
        ],
        axis=0,
    )
    sums = next_axis(sum_add(groups, [moved_up, moved_down]), orders)
    proj_groups = sum_add(proj_groups, first_proj)
    proj_up, proj_down = next_axis(proj_groups, orders)
    vec_far = swap(vec_grad, 1, batch_count)
    sums_up, sums_down, vec_far, proj_up, proj_down, *far_line = together(
        *sums, vec_far, proj_up, proj_down, *far_line
    )
    sums = next_add(sum_add(groups, [moved_up, moved_down]), orders, [sums_up, sums_down])
    proj_one, proj_two = next_add(proj_groups, orders, [proj_up, proj_down])
    vec_grad = vec_grad + vec_far

    qkv_parts = from_own(jnp.concatenate(sums, axis=0), seq_count)
    proj_parts = from_own(jnp.concatenate([proj_one, proj_two], axis=0), seq_count)
    late = [jnp.concatenate(parts, axis=0) for parts in zip(qkv_parts, proj_parts)]
    late = [late[0]] + [shift(late[step], -step, seq_count) for step in range(1, seq_count)]
    output = (middle + (out_own + out_arrived.astype(F32) + vec_values[5])).astype(BF)
    for bit in bits:
        vec_grad = vec_grad + swap(vec_grad, bit, batch_count)
    *late, vec_grad, output = together(*late, vec_grad, output)
    total_mlp = functools.reduce(
        jnp.add, [part.astype(F32) for part in (joined[0], *near_line, *far_line)]
    )
    share_up, share_down = total_mlp[:unit_width], total_mlp[unit_width:]

    turned = (mom_qkv.T, mom_proj.T, mom_up.T, mom_down)
    widest = unit_width
    spread = seq_count // 4
    home_plane = [spread * turn for turn in (1, 2, 3, 0)]
    plane_of = {plane: index for index, plane in enumerate(home_plane)}
    held = jnp.take(
        jnp.array([plane_of.get(plane - plane % spread) for plane in range(seq_count)], jnp.int32),
        (seq_rank + jnp.arange(seq_count, dtype=jnp.int32)) % seq_count,
    )

    late = functools.reduce(jnp.add, [part.astype(F32) for part in late])
    shares = (late[:qkv_width], late[qkv_width:], share_up, share_down)
    fresh = [muon_momentum * old + share for old, share in zip(turned, shares)]
    stacked = jnp.stack(
        [jnp.pad(new.astype(BF), ((0, widest - new.shape[0]), (0, 0))) for new in fresh]
    )
    small = lax.dynamic_slice_in_dim(vec_grad, batch_rank * (seq_count * column_count), seq_count * column_count, 1)
    small = jnp.transpose(small.reshape(-1, seq_count, column_count), (1, 0, 2)).reshape(seq_count, -1)
    small = jnp.pad(small, ((0, 0), (0, width - small.shape[1])))
    small_high = small.astype(BF)
    small_low = (small - small_high.astype(F32)).astype(BF)
    y_own = jnp.broadcast_to(output[rows : rows + 1], (seq_count, width))
    small = jnp.pad(jnp.stack([small_high, small_low, y_own], axis=1), ((0, 0), (0, 13), (0, 0)))
    slab = []
    for step in range(seq_count):
        part = lax.dynamic_index_in_dim(stacked, held[step], 0, False)
        rider = lax.dynamic_index_in_dim(small, (seq_rank + step) % seq_count, 0, False)
        part = jnp.concatenate([part, rider], axis=0)
        slab.append(shift(part, step, seq_count) if step else part)
    *slab, token_low, output = together(*slab, token_low, output)
    riders = [part[widest : widest + 3] for part in slab]
    slab = jnp.concatenate([part[:widest] for part in slab], axis=0)
    back_moved = send_back([output[:rows], token_low[:rows]])
    y_line = jnp.stack([part[2:3] for part in riders])
    y_far = swap(y_line, 1, batch_count)

    def plane_sum(kept, sent):
        chip = (kept.astype(F32) + swap(sent, 1, batch_count).astype(F32)).astype(BF)
        total = chip[0].astype(F32)
        for index, mask in enumerate(masks[1:]):
            total = total + swap(chip[index + 1], mask, batch_count).astype(F32)
        total = total.astype(BF)
        pair = jnp.stack([total, swap(total, 1, batch_count)])
        return [pair] + [swap(pair, mask, batch_count) for mask in masks[1:]]

    unit_offsets = offsets * (packed_rows(width, batch_count) // batch_count)
    slab, kept, sent = first_steps(plane_sum(*gram(slab, unit_offsets)), slab, unit_offsets)
    slab, kept, sent, y_far = together(slab, kept, sent, y_far)
    slab = last_steps(plane_sum(kept, sent), slab, unit_offsets)
    slab, *back_moved = together(slab, *back_moved)
    y_patches, dx_patches = join_back(back_moved, 0), join_back(back_moved, 1)
    back = slab.reshape(seq_count, widest, width)
    back = jnp.stack(
        [back[0]] + [shift(back[step], -step, seq_count) for step in range(1, seq_count)]
    )
    masters = (w_qkv, w_proj, w_up, w_down)
    ratios = (3.0, 1.0, 4.0, 0.25)
    updated = []
    for index in range(4):
        own_part = lax.dynamic_index_in_dim(
            back, (home_plane[index] - seq_rank) % seq_count, 0, False
        )[: fresh[index].shape[0]].astype(F32)
        if index < 3:
            own_part = own_part.T
        factor = math.sqrt(max(1.0, ratios[index]))
        updated.append(
            masters[index] * (1.0 - muon_rate * muon_decay) - muon_rate * factor * own_part
        )

    vec_sum = functools.reduce(
        jnp.add, [part[0].astype(F32) + part[1].astype(F32) for part in riders]
    )
    vec_sum = vec_sum[: vec_grad.shape[0] * column_count].reshape(-1, column_count)
    vec_sum, class_sums = vec_sum[:10], vec_sum[10:]
    chosen = (
        jnp.arange(class_count, dtype=jnp.int32)[:, None] == all_labels[None, :]
    ).astype(F32)
    table_sum = jnp.dot(chosen, class_sums, precision=highest, preferred_element_type=F32)
    y_rows = []
    for slot in range(images):
        turn = (seq_rank - (core * images + slot) * chips) % seq_count
        near = lax.dynamic_index_in_dim(y_line, turn, 0, False)
        far = lax.dynamic_index_in_dim(y_far, turn, 0, False)
        time_y = jnp.where(core == 0, near, far)
        class_y = jnp.where(core == 0, far, near)
        y_rows.append(jnp.concatenate([time_y, class_y], axis=0))
    y_rows = jnp.stack(y_rows)
    vec_new = adam_step(vectors, vec_first, vec_second, vec_sum)
    table_new = adam_step(table, table_first, table_second, table_sum)
    return (
        y_patches,
        y_rows,
        dx_patches,
        *updated,
        fresh[0].T,
        fresh[1].T,
        fresh[2].T,
        fresh[3],
        *vec_new,
        *table_new,
    )


def solution(mesh):
    tokens = P("batch", "seq", None)
    images = P("batch")
    extras = P("batch", None, None)
    columns = P(None, ("batch", "seq"))
    rows = P(("batch", "seq"), None)
    return jax.shard_map(
        body,
        mesh=mesh,
        in_specs=(
            tokens, images, images, tokens, tokens, extras, extras,
            columns, columns, columns, rows, columns, columns, columns, rows,
            columns, columns, columns, columns, columns, columns,
        ),
        out_specs=(
            tokens, extras, tokens, columns, columns, columns, rows,
            columns, columns, columns, rows, columns, columns, columns, columns, columns, columns,
        ),
        check_vma=False,
    )
```

time: 3400 us -> 802 us (0.24)
  waiting for transfers between devices: 1980 us -> 268 us
  matrix products: 624 us -> 15.1 us
  local copies, waits for them, and re-layouts: 319 us -> 69 us
  Pallas kernels: 0 us -> 233 us
  blocking collectives: 237 us -> 9.52 us
  other arithmetic: 190 us -> 75.6 us
  starting transfers between devices: 14.9 us -> 90.8 us
    unnamed x24 -> x1, waiting for transfers between devices: 1170 us -> 0.02 us
    dot_general x43 -> x5, matrix products: 624 us -> 15.1 us  [the longest x2 10.6 us: dot_nt(): lax.dot_general(former, latter, (((1,), (1,)), ((), ())), preferred_eleme...]
    psum x6 -> x0, waiting for transfers between devices: 495 us -> none  [the longest x5 495 us: body(): lax.psum(matmul_last(current, current, highest).astype(jnp.bfloat16), 'seq')]
    all_gather x10 -> x1, waiting for transfers between devices: 318 us -> 0.02 us  [body(): lax.all_gather(own_mlp, ('batch', 'seq'), axis=0, tiled=True, axis_index_...]
    ppermute x0 -> x82, waiting for transfers between devices: none -> 268 us  [the longest x15 124 us: shift(): lax.ppermute(values, 'seq', [(rank, (rank + step) % seq_count) for rank i...]
    pallas_call x0 -> x28, Pallas kernels: none -> 233 us  [the longest x1 59.3 us: mlp(): pl.pallas_call(functools.partial(mlp_kernel, units, unit, block), grid=(h...]
    unnamed x2 -> x0, blocking collectives: 157 us -> none
    reshape x18 -> x8, local copies, waits for them, and re-layouts: 114 us -> 1.35 us  [the longest x1 0.7 us: body(): jnp.take(jnp.take(core_bias, chip_order, axis=0), line_order, axis=1)]
  transfers between devices with their start and end apart: 22 -> 83, of which waited for: 14 -> 36; matrix products, arithmetic and copies ran while one was open for 15% -> 12% of each run, Pallas kernels for 0% -> 21%
where the time goes in v1:
time: 802 us; the launch traced here: 786 us
  waiting for transfers between devices  268 us (33%)
  Pallas kernels  233 us (29%)
  starting transfers between devices  90.8 us (11%)
  other arithmetic  75.6 us (9%)
  local copies, waits for them, and re-layouts  69 us (9%)
  between operations  24.8 us (3%)
  matrix products  15.1 us (2%)
  blocking collectives  9.52 us (1%)
    ppermute x15, waiting for transfers between devices, shift(): lax.ppermute(values, 'seq', [(rank, (rank + step) % seq_count) for rank i...  124 us
    ppermute x53, waiting for transfers between devices, swap(): lax.ppermute(values, 'batch', [(rank, rank ^ bit) for rank in range(batch...  87.3 us
    pallas_call x1, Pallas kernels, mlp(): pl.pallas_call(functools.partial(mlp_kernel, units, unit, block), grid=(h...  59.3 us
    ppermute x8, waiting for transfers between devices, send(): lax.ppermute(lax.dynamic_index_in_dim(pieces, seq_rank ^ matching, 0, Fal...  56.7 us
    pallas_call x1, Pallas kernels, attention_backward(): pl.pallas_call(functools.partial(attention_backward_kernel, groups), out_...  48 us
    ppermute x53, starting transfers between devices, swap(): lax.ppermute(values, 'batch', [(rank, rank ^ bit) for rank in range(batch...  39.3 us
    pallas_call x1, Pallas kernels, first_steps(): pl.pallas_call(functools.partial(first_steps_kernel, len(pairs)), out_sha...  31.5 us
    pallas_call x1, Pallas kernels, attention_forward(): pl.pallas_call(functools.partial(attention_forward_kernel, groups), out_s...  30.3 us
  transfers between devices with their start and end apart: 83, of which 36 were waited for; matrix products, arithmetic and copies ran while one was open for 12% of the time, Pallas kernels for 21%

profile of v1, /device:TPU:9, one launch (start us, length us, event | category | flops | bytes accessed | tf_op | source)
XLA Modules:
  0.0 786.4 jit_solution(16341750785867488076)
XLA Ops:
  7.3 2.4 copy.267.refs_2_
  9.8 9.5 %all-gather.1 = s32[8,2,2]{2,1,0:T(2,128)S(1)} all-gather(s32[1,2,2]{2,1,0:T(2,128)S(1)} %add_bitcast_fusion), channel_id=2, replica_groups=mesh['batch'=8,'seq'=4] {'batch'}, dimensions={0}, use_global_device_ids=true | all-gather | bytes 144 | tf_op jit(solution)/shard_map/all_gather | solution.py:1020
  26.2 5.1 collective-permute-done.2.refs_3_
  31.3 17.5 %collective-permute-done.1.refs_2_ = bf16[176,1152]{1,0:T(8,128)(2,1)S(1)} collective-permute-done((bf16[176,1152]{1,0:T(8,128)(2,1)S(1)}, bf16[176,1152]{1,0:T(8,128)(2,1)S(1)}, u32[]{:S(2)}, u32[]{:S(2)}) %collective-permute-start.1) | collective-permute-done | bytes 405536 | tf_op jit(solution)/shard_map/ppermute | solution.py:841
  48.8 8.7 %collective-permute-done.refs_1_ = bf16[176,1152]{1,0:T(8,128)(2,1)S(1)} collective-permute-done((bf16[176,1152]{1,0:T(8,128)(2,1)S(1)}, bf16[176,1152]{1,0:T(8,128)(2,1)S(1)}, u32[]{:S(2)}, u32[]{:S(2)}) %collective-permute-start) | collective-permute-done | bytes 405536 | tf_op jit(solution)/shard_map/ppermute | solution.py:841
  64.7 5.1 collective-permute-start.11
  69.7 8.7 %collective-permute-done.12.refs_12_ = bf16[128,1152]{1,0:T(8,128)(2,1)S(1)} collective-permute-done((bf16[128,1152]{1,0:T(8,128)(2,1)S(1)}, bf16[128,1152]{1,0:T(8,128)(2,1)S(1)}, u32[]{:S(2)}, u32[]{:S(2)}) %collective-permute-start.12) | collective-permute-done | bytes 294944 | tf_op jit(solution)/shard_map/ppermute | solution.py:983
  82.5 9.7 %collective-permute-done.11.refs_11_ = bf16[128,1152]{1,0:T(8,128)(2,1)S(1)} collective-permute-done((bf16[128,1152]{1,0:T(8,128)(2,1)S(1)}, bf16[128,1152]{1,0:T(8,128)(2,1)S(1)}, u32[]{:S(2)}, u32[]{:S(2)}) %collective-permute-start.11) | collective-permute-done | bytes 294944 | tf_op jit(solution)/shard_map/ppermute | solution.py:983
  93.7 9.6 %collective-permute-done.10.refs_10_ = bf16[128,1152]{1,0:T(8,128)(2,1)S(1)} collective-permute-done((bf16[128,1152]{1,0:T(8,128)(2,1)S(1)}, bf16[128,1152]{1,0:T(8,128)(2,1)S(1)}, u32[]{:S(2)}, u32[]{:S(2)}) %collective-permute-start.10) | collective-permute-done | bytes 294944 | tf_op jit(solution)/shard_map/ppermute | solution.py:983
  106.0 2.6 add_convert_fusion.9.refs_0_
  108.7 16.4 %collective-permute-done.9.refs_9_ = bf16[128,1152]{1,0:T(8,128)(2,1)S(1)} collective-permute-done((bf16[128,1152]{1,0:T(8,128)(2,1)S(1)}, bf16[128,1152]{1,0:T(8,128)(2,1)S(1)}, u32[]{:S(2)}, u32[]{:S(2)}) %collective-permute-start.9) | collective-permute-done | bytes 294944 | tf_op jit(solution)/shard_map/ppermute | solution.py:983
  125.1 6.1 collective-permute-done.5.refs_4_
  138.0 2.5 dynamic-slice_bitcast_fusion.4
  140.5 3.1 collective-permute-start.22
  146.8 9.1 %place.1 = (bf16[3456,1152]{1,0:T(8,128)(2,1)}, bf16[1152,1152]{1,0:T(8,128)(2,1)S(1)}) custom-call(s32[24]{0:T(128)S(1)} %stack.204.offset_ref, bf16[288,1152]{1,0:T(8,128)(2,1)S(1)} %copy-done.9, bf16[288,1152]{1,0:T(8,128)(2,1)S(1)} %collective-permute-done.17.refs_1_, bf16[288,1152]{1,0:T(8,128)(2,1)S(1)} %copy-done.16, ...), custom_call_target="tpu_custom_call" | custom-call | bytes 21233664 | tf_op jit(solution)/shard_map/place/pallas_call | solution.py:803
  160.6 6.6 convolution_convert_fusion.refs_0_
  167.2 12.2 %collective-permute-done.21.refs_1_ = bf16[128,1152]{1,0:T(8,128)(2,1)S(1)} collective-permute-done((bf16[128,1152]{1,0:T(8,128)(2,1)S(1)}, bf16[128,1152]{1,0:T(8,128)(2,1)S(1)}, u32[]{:S(2)}, u32[]{:S(2)}) %collective-permute-start.21) | collective-permute-done | bytes 294944 | tf_op jit(solution)/shard_map/ppermute | solution.py:983
  195.2 4.2 collective-permute-start.25
  199.9 30.3 %attention_forward.1 = (bf16[528,1152]{1,0:T(8,128)(2,1)}, f32[16,512]{1,0:T(8,128)}, f32[16,128]{1,0:T(8,128)}) custom-call(s32[2]{0:T(128)} %stack.176.valid_ref, bf16[528,3456]{1,0:T(8,128)(2,1)} %get-tuple-element.161.own_ref, bf16[528,2304]{1,0:T(8,128)(2,1)} %collective-permute-done.23.refs_0_), custom_call_target="tpu_custom_call" | custom-call | flops 9663676416 | bytes 7299072 | tf_op jit(solution)/shard_map/attention_forward/pallas_call | solution.py:134
  231.1 4.1 fusion.72
  242.8 59.3 %mlp.1 = (f32[528,1152]{1,0:T(8,128)}, bf16[528,1152]{1,0:T(8,128)(2,1)}, f32[528,1152]{1,0:T(8,128)}, bf16[528,1152]{1,0:T(8,128)(2,1)}, bf16[2304,1152]{1,0:T(...) custom-call(s32[16]{0:T(128)} %mul.403.first_ref, f32[1,2304]{1,0:T(1,128)} %reshape.460.bias_ref, ...), custom_call_target="tpu_custom_call" | custom-call | flops 33634123776 | bytes 40697856 | tf_op jit(solution)/shard_map/mlp/pallas_call | solution.py:338
  304.1 3.6 concatenate.97
  312.9 2.6 fusion.65
  315.5 3.0 convolution_convert_fusion.1.refs_2_
  318.5 48.0 %attention_backward.1 = (bf16[528,1152]{1,0:T(8,128)(2,1)}, bf16[528,2304]{1,0:T(8,128)(2,1)}, bf16[528,2304]{1,0:T(8,128)(2,1)}) custom-call(s32[2]{0:T(128)} %stack.176.valid_ref, bf16[528,3456]{1,0:T(8,128)(2,1)} %get-tuple-element.161.own_ref, bf16[528,2304]{1,0:T(8,128)(2,1)} %collective-permute-done.23.refs_0_, ...), custom_call_target="tpu_custom_call" | custom-call | flops 21743271936 | bytes 14598144 | tf_op jit(solution)/shard_map/attention_backward/pallas_call | solution.py:239
  366.5 2.6 collective-permute-done.31.refs_4_
  370.0 3.1 add_convert_fusion.7
  373.1 3.1 add_convert_fusion.6
  382.4 4.8 qkv_grad.1
  394.5 14.5 %packed_grad.1 = (bf16[528,3456]{1,0:T(8,128)(2,1)}, bf16[4,432,1152]{2,1,0:T(8,128)(2,1)}, bf16[4,432,1152]{2,1,0:T(8,128)(2,1)}) custom-call(s32[8]{0:T(128)S(1)} %get-tuple-element.376.offset_ref, bf16[528,1152]{1,0:T(8,128)(2,1)S(1)} %copy-done.24, bf16[528,2304]{1,0:T(8,128)(2,1)} %get-tuple-element.192.own_ref, ...), custom_call_target="tpu_custom_call" | custom-call | flops 4204265472 | bytes 16478208 | tf_op jit(solution)/shard_map/packed_grad/pallas_call | solution.py:693
  412.3 2.6 add_convert_fusion.2
  414.9 2.6 add_convert_fusion.4
  419.1 4.3 add_convert_fusion
  432.6 12.5 %first_norm_back.1 = (bf16[528,1152]{1,0:T(8,128)(2,1)}, f32[16,1152]{1,0:T(8,128)}) custom-call(bf16[528,3456]{1,0:T(8,128)(2,1)} %together.27.packed_ref, bf16[3456,1152]{1,0:T(8,128)(2,1)} %get-tuple-element.159.weight_ref, f32[528,1152]{1,0:T(8,128)} %get-tuple-element.288.standard_ref, f32[528,1]{1,0:T(8,128)} %rsqrt.16.inverse_ref, ...), custom_call_target="tpu_custom_call" | custom-call | flops 4204265472 | bytes 17694720 | tf_op jit(solution)/shard_map/first_norm_back/pallas_call | solution.py:727
  447.8 13.3 %collective-permute-done.43.refs_9_ = bf16[160,1152]{1,0:T(8,128)(2,1)S(1)} collective-permute-done((bf16[160,1152]{1,0:T(8,128)(2,1)}, bf16[160,1152]{1,0:T(8,128)(2,1)S(1)}, u32[]{:S(2)}, u32[]{:S(2)}) %collective-permute-start.43) | collective-permute-done | bytes 368672 | tf_op jit(solution)/shard_map/ppermute | solution.py:847
  467.0 2.5 collective-permute-start.46
  477.8 3.2 add_convert_fusion.8.refs_5_
  481.1 4.3 collective-permute-done.44.refs_0_
  487.7 18.1 %collective-permute-done.49.refs_5_ = bf16[288,1152]{1,0:T(8,128)(2,1)S(1)} collective-permute-done((bf16[288,1152]{1,0:T(8,128)(2,1)S(1)}, bf16[288,1152]{1,0:T(8,128)(2,1)S(1)}, u32[]{:S(2)}, u32[]{:S(2)}) %collective-permute-start.49) | collective-permute-done | bytes 663584 | tf_op jit(solution)/shard_map/ppermute | solution.py:841
  516.9 2.4 collective-permute-start.52
  524.2 2.5 collective-permute-done.54
  527.4 10.5 %collective-permute-done.51.refs_2_ = bf16[144,1152]{1,0:T(8,128)(2,1)S(1)} collective-permute-done((bf16[144,1152]{1,0:T(8,128)(2,1)S(1)}, bf16[144,1152]{1,0:T(8,128)(2,1)S(1)}, u32[]{:S(2)}, u32[]{:S(2)}) %collective-permute-start.51) | collective-permute-done | bytes 331808 | tf_op jit(solution)/shard_map/ppermute | solution.py:841
  537.8 7.1 collective-permute-done.52.refs_3_
  554.8 4.9 collective-permute-done.55.refs_1_
  559.7 23.2 %collective-permute-done.56.refs_2_ = bf16[160,1152]{1,0:T(8,128)(2,1)S(1)} collective-permute-done((bf16[160,1152]{1,0:T(8,128)(2,1)S(1)}, bf16[160,1152]{1,0:T(8,128)(2,1)S(1)}, u32[]{:S(2)}, u32[]{:S(2)}) %collective-permute-start.56) | collective-permute-done | bytes 368672 | tf_op jit(solution)/shard_map/ppermute | solution.py:841
  582.9 2.9 collective-permute-done.57.refs_3_
  590.5 4.5 gram.1
  600.6 3.6 collective-permute-done.59
  604.2 5.2 collective-permute-done.61
  609.5 2.7 collective-permute-start.62
  617.0 8.0 %collective-permute-done.65.refs_3_ = bf16[2,400,256]{2,1,0:T(8,128)(2,1)S(1)} collective-permute-done((bf16[2,400,256]{2,1,0:T(8,128)(2,1)S(1)}, bf16[2,400,256]{2,1,0:T(8,128)(2,1)S(1)}, u32[]{:S(2)}, u32[]{:S(2)}) %collective-permute-start.65) | collective-permute-done | bytes 409632 | tf_op jit(solution)/shard_map/ppermute | solution.py:847
  625.0 9.4 %collective-permute-done.64.refs_2_ = bf16[2,400,256]{2,1,0:T(8,128)(2,1)S(1)} collective-permute-done((bf16[2,400,256]{2,1,0:T(8,128)(2,1)S(1)}, bf16[2,400,256]{2,1,0:T(8,128)(2,1)S(1)}, u32[]{:S(2)}, u32[]{:S(2)}) %collective-permute-start.64) | collective-permute-done | bytes 409632 | tf_op jit(solution)/shard_map/ppermute | solution.py:847
  636.0 31.5 %first_steps.1 = (bf16[576,1152]{1,0:T(8,128)(2,1)}, bf16[4,400,256]{2,1,0:T(8,128)(2,1)}, bf16[4,400,256]{2,1,0:T(8,128)(2,1)}) custom-call(s32[8]{0:T(128)} %copy-done.25, bf16[576,1152]{1,0:T(8,128)(2,1)} %copy-done.21, bf16[2,400,256]{2,1,0:T(8,128)(2,1)} %copy-done.106, bf16[2,400,256]{2,1,0:T(8,128)(2,1)} %copy-done.148, ...), custom_call_target="tpu_custom_call" | custom-call | flops 27518828544 | bytes 7962624 | tf_op jit(solution)/shard_map/first_steps/pallas_call | solution.py:560
  674.7 4.5 collective-permute-start.75
  684.2 3.6 collective-permute-done.68
  687.8 4.6 collective-permute-done.70
  692.5 2.7 collective-permute-start.71
  699.7 8.3 %collective-permute-done.74.refs_3_ = bf16[2,400,256]{2,1,0:T(8,128)(2,1)S(1)} collective-permute-done((bf16[2,400,256]{2,1,0:T(8,128)(2,1)S(1)}, bf16[2,400,256]{2,1,0:T(8,128)(2,1)S(1)}, u32[]{:S(2)}, u32[]{:S(2)}) %collective-permute-start.74) | collective-permute-done | bytes 409632 | tf_op jit(solution)/shard_map/ppermute | solution.py:847
  708.8 8.7 %collective-permute-done.73.refs_2_ = bf16[2,400,256]{2,1,0:T(8,128)(2,1)S(1)} collective-permute-done((bf16[2,400,256]{2,1,0:T(8,128)(2,1)S(1)}, bf16[2,400,256]{2,1,0:T(8,128)(2,1)S(1)}, u32[]{:S(2)}, u32[]{:S(2)}) %collective-permute-start.73) | collective-permute-done | bytes 409632 | tf_op jit(solution)/shard_map/ppermute | solution.py:847
  718.9 18.3 %last_steps.1.refs_0_ = bf16[576,1152]{1,0:T(8,128)(2,1)} custom-call(s32[8]{0:T(128)} %copy-done.25, bf16[576,1152]{1,0:T(8,128)(2,1)} %get-tuple-element.254.slab_ref, bf16[2,400,256]{2,1,0:T(8,128)(2,1)} %copy-done.105, bf16[2,400,256]{2,1,0:T(8,128)(2,1)} %copy-done.145, bf16[2,400,256]{2,1,0:T(8,128)(2,1)} %copy-done.144, bf16[2,400,256]{2,1,0:T(8,128)(2,1)} %copy-done.143), custom_call_target="tpu_custom_call" | custom-call | flops 15288238080 | bytes 5308416 | tf_op jit(solution)/shard_map/last_steps/pallas_call | solution.py:615
  743.6 2.4 collective-permute-start.80
  749.3 3.7 collective-permute-done.81
  753.0 19.3 %collective-permute-done.80 = bf16[144,1152]{1,0:T(8,128)(2,1)S(1)} collective-permute-done((bf16[144,1152]{1,0:T(8,128)(2,1)S(1)}, bf16[144,1152]{1,0:T(8,128)(2,1)S(1)}, u32[]{:S(2)}, u32[]{:S(2)}) %collective-permute-start.80) | collective-permute-done | bytes 331808 | tf_op jit(solution)/shard_map/ppermute | solution.py:841
  772.4 3.3 collective-permute-done.79
  (653 shorter events, 181.9 us)
Async XLA Ops:
  7.3 235.5 %all-gather.4.cloned.1.call-start = ((), (), s32[]{:S(2)}) async-start(), calls=%async_computation | async-start | bytes 11280384 | tf_op jit(solution)/shard_map/all_gather | solution.py:1042
  20.5 10.8 %collective-permute-start.2 = (bf16[176,1152]{1,0:T(8,128)(2,1)S(1)}, bf16[176,1152]{1,0:T(8,128)(2,1)S(1)}, u32[]{:S(2)}, u32[]{:S(2)}) collective-permute-start(bf16[176,1152]{1,0:T(8,128)(2,1)S(1)} %pad_maximum_fusion.17.refs_0_), channel_id=1, source_target_pairs={{0,3},{1,0},{2,1},{3,2},{4,7},{5,4},{6,5},{7,6},{8,11},{9,8},{10,9... | collective-permute-start | bytes 1216520 | tf_op jit(solution)/shard_map/ppermute | solution.py:841
  20.7 28.1 %collective-permute-start.1 = (bf16[176,1152]{1,0:T(8,128)(2,1)S(1)}, bf16[176,1152]{1,0:T(8,128)(2,1)S(1)}, u32[]{:S(2)}, u32[]{:S(2)}) collective-permute-start(bf16[176,1152]{1,0:T(8,128)(2,1)S(1)} %pad_maximum_fusion.17.refs_0_), channel_id=1, source_target_pairs={{0,2},{1,3},{2,0},{3,1},{4,6},{5,7},{6,4},{7,5},{8,10},{9,11},{10,... | collective-permute-start | bytes 1216520 | tf_op jit(solution)/shard_map/ppermute | solution.py:841
  23.0 34.5 %collective-permute-start = (bf16[176,1152]{1,0:T(8,128)(2,1)S(1)}, bf16[176,1152]{1,0:T(8,128)(2,1)S(1)}, u32[]{:S(2)}, u32[]{:S(2)}) collective-permute-start(bf16[176,1152]{1,0:T(8,128)(2,1)S(1)} %pad_maximum_fusion.17.refs_0_), channel_id=1, source_target_pairs={{0,1},{1,2},{2,3},{3,0},{4,5},{5,6},{6,7},{7,4},{8,9},{9,10},{10,1... | collective-permute-start | bytes 1216520 | tf_op jit(solution)/shard_map/ppermute | solution.py:841
  59.8 21.4 %collective-permute-start.7 = (bf16[320,1152]{1,0:T(8,128)(2,1)}, bf16[320,1152]{1,0:T(8,128)(2,1)S(1)}, u32[]{:S(2)}, u32[]{:S(2)}) collective-permute-start(bf16[320,1152]{1,0:T(8,128)(2,1)} %get-tuple-element.145.refs_5_), channel_id=1, source_target_pairs={{0,16},{4,20},{8,24},{12,28},{16,0},{20,4},{24,8},{28,12},{1,17},{... | collective-permute-start | bytes 2211848 | tf_op jit(solution)/shard_map/ppermute | solution.py:847
  61.1 32.4 %collective-permute-start.3 = (bf16[288,1152]{1,0:T(8,128)(2,1)}, bf16[288,1152]{1,0:T(8,128)(2,1)S(1)}, u32[]{:S(2)}, u32[]{:S(2)}) collective-permute-start(bf16[288,1152]{1,0:T(8,128)(2,1)} %get-tuple-element.144.refs_1_), channel_id=1, source_target_pairs={{0,8},{4,12},{8,0},{12,4},{16,24},{20,28},{24,16},{28,20},{1,9},{5... | collective-permute-start | bytes 1990664 | tf_op jit(solution)/shard_map/ppermute | solution.py:847
  62.7 15.8 %collective-permute-start.12 = (bf16[128,1152]{1,0:T(8,128)(2,1)S(1)}, bf16[128,1152]{1,0:T(8,128)(2,1)S(1)}, u32[]{:S(2)}, u32[]{:S(2)}) collective-permute-start(bf16[128,1152]{1,0:T(8,128)(2,1)S(1)} %get-tuple-element.334), channel_id=1, source_target_pairs={{0,5},{1,1},{2,4},{3,0},{4,7},{5,3},{6,6},{7,2},{8,13},{9,9},{10,1... | collective-permute-start | bytes 884744 | tf_op jit(solution)/shard_map/ppermute | solution.py:983
  64.7 27.5 %collective-permute-start.11 = (bf16[128,1152]{1,0:T(8,128)(2,1)S(1)}, bf16[128,1152]{1,0:T(8,128)(2,1)S(1)}, u32[]{:S(2)}, u32[]{:S(2)}) collective-permute-start(bf16[128,1152]{1,0:T(8,128)(2,1)S(1)} %get-tuple-element.335), channel_id=1, source_target_pairs={{0,1},{1,5},{2,0},{3,4},{4,3},{5,7},{6,2},{7,6},{8,9},{9,13},{10,8... | collective-permute-start | bytes 884744 | tf_op jit(solution)/shard_map/ppermute | solution.py:983
  69.7 33.6 %collective-permute-start.10 = (bf16[128,1152]{1,0:T(8,128)(2,1)S(1)}, bf16[128,1152]{1,0:T(8,128)(2,1)S(1)}, u32[]{:S(2)}, u32[]{:S(2)}) collective-permute-start(bf16[128,1152]{1,0:T(8,128)(2,1)S(1)} %get-tuple-element.336), channel_id=1, source_target_pairs={{0,4},{1,0},{2,5},{3,1},{4,6},{5,2},{6,7},{7,3},{8,12},{9,8},{10,1... | collective-permute-start | bytes 884744 | tf_op jit(solution)/shard_map/ppermute | solution.py:983
  78.5 46.6 %collective-permute-start.6 = (bf16[320,1152]{1,0:T(8,128)(2,1)S(1)}, bf16[320,1152]{1,0:T(8,128)(2,1)S(1)}, u32[]{:S(2)}, u32[]{:S(2)}) collective-permute-start(bf16[320,1152]{1,0:T(8,128)(2,1)S(1)} %copy-done.5), channel_id=1, source_target_pairs={{0,8},{4,12},{8,0},{12,4},{16,24},{20,28},{24,16},{28,20},{1,9},{5... | collective-permute-start | bytes 2211848 | tf_op jit(solution)/shard_map/ppermute | solution.py:847
  81.2 50.8 %collective-permute-start.8 = (bf16[320,1152]{1,0:T(8,128)(2,1)S(1)}, bf16[320,1152]{1,0:T(8,128)(2,1)}, u32[]{:S(2)}, u32[]{:S(2)}) collective-permute-start(bf16[320,1152]{1,0:T(8,128)(2,1)S(1)} %collective-permute-done.7.refs_7_), channel_id=1, source_target_pairs={{0,8},{4,12},{8,0},{12,4},{16,24},{20,28},{24,16},{28,20},{1,9},{5... | collective-permute-start | bytes 2211848 | tf_op jit(solution)/shard_map/ppermute | solution.py:847
  92.2 32.8 %collective-permute-start.4 = (bf16[288,1152]{1,0:T(8,128)(2,1)S(1)}, bf16[288,1152]{1,0:T(8,128)(2,1)S(1)}, u32[]{:S(2)}, u32[]{:S(2)}) collective-permute-start(bf16[288,1152]{1,0:T(8,128)(2,1)S(1)} %copy-done.8), channel_id=1, source_target_pairs={{0,16},{4,20},{8,24},{12,28},{16,0},{20,4},{24,8},{28,12},{1,17},{... | collective-permute-start | bytes 1990664 | tf_op jit(solution)/shard_map/ppermute | solution.py:847
  93.5 37.7 %collective-permute-start.5 = (bf16[288,1152]{1,0:T(8,128)(2,1)S(1)}, bf16[288,1152]{1,0:T(8,128)(2,1)S(1)}, u32[]{:S(2)}, u32[]{:S(2)}) collective-permute-start(bf16[288,1152]{1,0:T(8,128)(2,1)S(1)} %collective-permute-done.3.refs_2_), channel_id=1, source_target_pairs={{0,16},{4,20},{8,24},{12,28},{16,0},{20,4},{24,8},{28,12},{1,17},{... | collective-permute-start | bytes 1990664 | tf_op jit(solution)/shard_map/ppermute | solution.py:847
  104.1 21.0 %collective-permute-start.9 = (bf16[128,1152]{1,0:T(8,128)(2,1)S(1)}, bf16[128,1152]{1,0:T(8,128)(2,1)S(1)}, u32[]{:S(2)}, u32[]{:S(2)}) collective-permute-start(bf16[128,1152]{1,0:T(8,128)(2,1)S(1)} %get-tuple-element.337), channel_id=1, source_target_pairs={{0,0},{1,4},{2,1},{3,5},{4,2},{5,6},{6,3},{7,7},{8,8},{9,12},{10,9... | collective-permute-start | bytes 884744 | tf_op jit(solution)/shard_map/ppermute | solution.py:983
  135.2 9.4 %collective-permute-start.17 = (bf16[288,1152]{1,0:T(8,128)(2,1)}, bf16[288,1152]{1,0:T(8,128)(2,1)S(1)}, u32[]{:S(2)}, u32[]{:S(2)}) collective-permute-start(bf16[288,1152]{1,0:T(8,128)(2,1)} %get-tuple-element.155.refs_0_), channel_id=1, source_target_pairs={{0,4},{4,0},{8,12},{12,8},{16,20},{20,16},{24,28},{28,24},{1,5},{5... | collective-permute-start | bytes 1990664 | tf_op jit(solution)/shard_map/ppermute | solution.py:847
  136.9 9.8 %collective-permute-start.18 = (bf16[288,1152]{1,0:T(8,128)(2,1)S(1)}, bf16[288,1152]{1,0:T(8,128)(2,1)S(1)}, u32[]{:S(2)}, u32[]{:S(2)}) collective-permute-start(bf16[288,1152]{1,0:T(8,128)(2,1)S(1)} %copy-done.16), channel_id=1, source_target_pairs={{0,4},{4,0},{8,12},{12,8},{16,20},{20,16},{24,28},{28,24},{1,5},{5... | collective-permute-start | bytes 1990664 | tf_op jit(solution)/shard_map/ppermute | solution.py:847
  140.5 26.7 %collective-permute-start.22 = (bf16[128,1152]{1,0:T(8,128)(2,1)S(1)}, bf16[128,1152]{1,0:T(8,128)(2,1)S(1)}, u32[]{:S(2)}, u32[]{:S(2)}) collective-permute-start(bf16[128,1152]{1,0:T(8,128)(2,1)S(1)} %get-tuple-element.332), channel_id=1, source_target_pairs={{0,4},{1,0},{2,5},{3,1},{4,6},{5,2},{6,7},{7,3},{8,12},{9,8},{10,1... | collective-permute-start | bytes 884744 | tf_op jit(solution)/shard_map/ppermute | solution.py:983
  144.6 34.8 %collective-permute-start.21 = (bf16[128,1152]{1,0:T(8,128)(2,1)S(1)}, bf16[128,1152]{1,0:T(8,128)(2,1)S(1)}, u32[]{:S(2)}, u32[]{:S(2)}) collective-permute-start(bf16[128,1152]{1,0:T(8,128)(2,1)S(1)} %get-tuple-element.333), channel_id=1, source_target_pairs={{0,0},{1,4},{2,1},{3,5},{4,2},{5,6},{6,3},{7,7},{8,8},{9,12},{10,9... | collective-permute-start | bytes 884744 | tf_op jit(solution)/shard_map/ppermute | solution.py:983
  182.0 17.4 %collective-permute-start.23 = (bf16[528,2304]{1,0:T(8,128)(2,1)S(1)}, bf16[528,2304]{1,0:T(8,128)(2,1)}, u32[]{:S(2)}, u32[]{:S(2)}) collective-permute-start(bf16[528,2304]{1,0:T(8,128)(2,1)S(1)} %slice.433), channel_id=1, source_target_pairs={{4,0},{5,1},{6,2},{7,3},{0,4},{1,5},{2,6},{3,7},{12,8},{13,9},{14,... | collective-permute-start | bytes 7299080 | tf_op jit(solution)/shard_map/ppermute | solution.py:1122
  182.1 48.1 %collective-permute-start.24 = (bf16[2,2,1152]{2,1,0:T(2,128)(2,1)S(1)}, bf16[2,2,1152]{2,1,0:T(2,128)(2,1)S(1)}, u32[]{:S(2)}, u32[]{:S(2)}) collective-permute-start(bf16[2,2,1152]{2,1,0:T(2,128)(2,1)S(1)} %add_convert_fusion.16), channel_id=1, source_target_pairs={{0,4},{4,0},{8,12},{12,8},{16,20},{20,16},{24,28},{28,24},{1,5},{5... | collective-permute-start | bytes 27656 | tf_op jit(solution)/shard_map/ppermute | solution.py:847
  193.2 37.0 %collective-permute-start.26 = (bf16[128,1152]{1,0:T(8,128)(2,1)}, bf16[128,1152]{1,0:T(8,128)(2,1)S(1)}, u32[]{:S(2)}, u32[]{:S(2)}) collective-permute-start(bf16[128,1152]{1,0:T(8,128)(2,1)} %get-tuple-element.330), channel_id=1, source_target_pairs={{0,5},{1,1},{2,4},{3,0},{4,7},{5,3},{6,6},{7,2},{8,13},{9,9},{10,1... | collective-permute-start | bytes 884744 | tf_op jit(solution)/shard_map/ppermute | solution.py:983
  195.2 35.1 %collective-permute-start.25 = (bf16[128,1152]{1,0:T(8,128)(2,1)}, bf16[128,1152]{1,0:T(8,128)(2,1)S(1)}, u32[]{:S(2)}, u32[]{:S(2)}) collective-permute-start(bf16[128,1152]{1,0:T(8,128)(2,1)} %get-tuple-element.331), channel_id=1, source_target_pairs={{0,1},{1,5},{2,0},{3,4},{4,3},{5,7},{6,2},{7,6},{8,9},{9,13},{10,8... | collective-permute-start | bytes 884744 | tf_op jit(solution)/shard_map/ppermute | solution.py:983
  304.0 62.5 %collective-permute-start.32 = (bf16[528,1152]{1,0:T(8,128)(2,1)}, bf16[528,1152]{1,0:T(8,128)(2,1)S(1)}, u32[]{:S(2)}, u32[]{:S(2)}) collective-permute-start(bf16[528,1152]{1,0:T(8,128)(2,1)} %get-tuple-element.182), channel_id=1, source_target_pairs={{0,4},{4,0},{8,12},{12,8},{16,20},{20,16},{24,28},{28,24},{1,5},{5... | collective-permute-start | bytes 3649544 | tf_op jit(solution)/shard_map/ppermute | solution.py:847
  310.0 59.1 %collective-permute-start.31 = (bf16[1152,1152]{1,0:T(8,128)(2,1)}, bf16[1152,1152]{1,0:T(8,128)(2,1)}, u32[]{:S(2)}, u32[]{:S(2)}) collective-permute-start(bf16[1152,1152]{1,0:T(8,128)(2,1)} %pad_maximum_fusion), channel_id=1, source_target_pairs={{0,8},{4,12},{8,0},{12,4},{16,24},{20,28},{24,16},{28,20},{1,9},{5... | collective-permute-start | bytes 7962632 | tf_op jit(solution)/shard_map/ppermute | solution.py:847
  311.2 58.7 %collective-permute-start.30 = (bf16[1152,1152]{1,0:T(8,128)(2,1)}, bf16[1152,1152]{1,0:T(8,128)(2,1)}, u32[]{:S(2)}, u32[]{:S(2)}) collective-permute-start(bf16[1152,1152]{1,0:T(8,128)(2,1)} %concatenate.97), channel_id=1, source_target_pairs={{0,16},{4,20},{8,24},{12,28},{16,0},{20,4},{24,8},{28,12},{1,17},{... | collective-permute-start | bytes 7962632 | tf_op jit(solution)/shard_map/ppermute | solution.py:847
  376.2 32.8 %collective-permute-start.36 = (bf16[576,1152]{1,0:T(8,128)(2,1)}, bf16[576,1152]{1,0:T(8,128)(2,1)}, u32[]{:S(2)}, u32[]{:S(2)}) collective-permute-start(bf16[576,1152]{1,0:T(8,128)(2,1)} %add_convert_fusion.6), channel_id=1, source_target_pairs={{0,16},{4,20},{8,24},{12,28},{16,0},{20,4},{24,8},{28,12},{1,17},{... | collective-permute-start | bytes 3981320 | tf_op jit(solution)/shard_map/ppermute | solution.py:847
  376.6 32.5 %collective-permute-start.35 = (bf16[576,1152]{1,0:T(8,128)(2,1)}, bf16[576,1152]{1,0:T(8,128)(2,1)}, u32[]{:S(2)}, u32[]{:S(2)}) collective-permute-start(bf16[576,1152]{1,0:T(8,128)(2,1)} %add_convert_fusion.7), channel_id=1, source_target_pairs={{0,8},{4,12},{8,0},{12,4},{16,24},{20,28},{24,16},{28,20},{1,9},{5... | collective-permute-start | bytes 3981320 | tf_op jit(solution)/shard_map/ppermute | solution.py:847
  377.7 10.5 %collective-permute-start.33 = (bf16[528,2304]{1,0:T(8,128)(2,1)}, bf16[528,2304]{1,0:T(8,128)(2,1)}, u32[]{:S(2)}, u32[]{:S(2)}) collective-permute-start(bf16[528,2304]{1,0:T(8,128)(2,1)} %get-tuple-element.191), channel_id=1, source_target_pairs={{0,4},{1,5},{2,6},{3,7},{4,0},{5,1},{6,2},{7,3},{8,12},{9,13},{10,... | collective-permute-start | bytes 7299080 | tf_op jit(solution)/shard_map/ppermute | solution.py:1122
  388.3 20.8 %collective-permute-start.34 = (bf16[4,144,1152]{2,1,0:T(8,128)(2,1)}, bf16[4,144,1152]{2,1,0:T(8,128)(2,1)}, u32[]{:S(2)}, u32[]{:S(2)}) collective-permute-start(bf16[4,144,1152]{2,1,0:T(8,128)(2,1)} %get-tuple-element.198), channel_id=1, source_target_pairs={{0,4},{4,0},{8,12},{12,8},{16,20},{20,16},{24,28},{28,24},{1,5},{5... | collective-permute-start | bytes 3981320 | tf_op jit(solution)/shard_map/ppermute | solution.py:847
  409.1 10.0 %collective-permute-start.37 = (bf16[4,432,1152]{2,1,0:T(8,128)(2,1)}, bf16[4,432,1152]{2,1,0:T(8,128)(2,1)}, u32[]{:S(2)}, u32[]{:S(2)}) collective-permute-start(bf16[4,432,1152]{2,1,0:T(8,128)(2,1)} %get-tuple-element.202), channel_id=1, source_target_pairs={{0,4},{4,0},{8,12},{12,8},{16,20},{20,16},{24,28},{28,24},{1,5},{5... | collective-permute-start | bytes 11943944 | tf_op jit(solution)/shard_map/ppermute | solution.py:847
  412.0 19.6 %collective-permute-start.42 = (bf16[128,1152]{1,0:T(8,128)(2,1)}, bf16[128,1152]{1,0:T(8,128)(2,1)}, u32[]{:S(2)}, u32[]{:S(2)}) collective-permute-start(bf16[128,1152]{1,0:T(8,128)(2,1)} %pad_maximum_fusion.28), channel_id=1, source_target_pairs={{0,16},{4,20},{8,24},{12,28},{16,0},{20,4},{24,8},{28,12},{1,17},{... | collective-permute-start | bytes 884744 | tf_op jit(solution)/shard_map/ppermute | solution.py:847
  425.4 35.8 %collective-permute-start.40 = (bf16[288,1152]{1,0:T(8,128)(2,1)}, bf16[288,1152]{1,0:T(8,128)(2,1)}, u32[]{:S(2)}, u32[]{:S(2)}) collective-permute-start(bf16[288,1152]{1,0:T(8,128)(2,1)} %get-tuple-element.213), channel_id=1, source_target_pairs={{0,3},{1,0},{2,1},{3,2},{4,7},{5,4},{6,5},{7,6},{8,11},{9,8},{10,9... | collective-permute-start | bytes 1990664 | tf_op jit(solution)/shard_map/ppermute | solution.py:841
  425.4 35.8 %collective-permute-start.41 = (bf16[288,1152]{1,0:T(8,128)(2,1)}, bf16[288,1152]{1,0:T(8,128)(2,1)}, u32[]{:S(2)}, u32[]{:S(2)}) collective-permute-start(bf16[288,1152]{1,0:T(8,128)(2,1)} %get-tuple-element.214), channel_id=1, source_target_pairs={{0,1},{1,2},{2,3},{3,0},{4,5},{5,6},{6,7},{7,4},{8,9},{9,10},{10,1... | collective-permute-start | bytes 1990664 | tf_op jit(solution)/shard_map/ppermute | solution.py:841
  428.2 33.0 %collective-permute-start.38 = (bf16[416,1152]{1,0:T(8,128)(2,1)}, bf16[416,1152]{1,0:T(8,128)(2,1)S(1)}, u32[]{:S(2)}, u32[]{:S(2)}) collective-permute-start(bf16[416,1152]{1,0:T(8,128)(2,1)} %pad_maximum_fusion.11), channel_id=1, source_target_pairs={{0,16},{4,20},{8,24},{12,28},{16,0},{20,4},{24,8},{28,12},{1,17},{... | collective-permute-start | bytes 2875400 | tf_op jit(solution)/shard_map/ppermute | solution.py:847
  430.4 30.8 %collective-permute-start.39 = (bf16[448,1152]{1,0:T(8,128)(2,1)}, bf16[448,1152]{1,0:T(8,128)(2,1)S(1)}, u32[]{:S(2)}, u32[]{:S(2)}) collective-permute-start(bf16[448,1152]{1,0:T(8,128)(2,1)} %pad_maximum_fusion.9), channel_id=1, source_target_pairs={{0,8},{4,12},{8,0},{12,4},{16,24},{20,28},{24,16},{28,20},{1,9},{5... | collective-permute-start | bytes 3096584 | tf_op jit(solution)/shard_map/ppermute | solution.py:847
  431.6 29.6 %collective-permute-start.43 = (bf16[160,1152]{1,0:T(8,128)(2,1)}, bf16[160,1152]{1,0:T(8,128)(2,1)S(1)}, u32[]{:S(2)}, u32[]{:S(2)}) collective-permute-start(bf16[160,1152]{1,0:T(8,128)(2,1)} %pad_maximum_fusion.18), channel_id=1, source_target_pairs={{0,8},{4,12},{8,0},{12,4},{16,24},{20,28},{24,16},{28,20},{1,9},{5... | collective-permute-start | bytes 1105928 | tf_op jit(solution)/shard_map/ppermute | solution.py:847
  465.0 16.0 %collective-permute-start.47 = (bf16[64,1152]{1,0:T(8,128)(2,1)}, bf16[64,1152]{1,0:T(8,128)(2,1)}, u32[]{:S(2)}, u32[]{:S(2)}) collective-permute-start(bf16[64,1152]{1,0:T(8,128)(2,1)} %fusion.34), channel_id=1, source_target_pairs={{0,8},{4,12},{8,0},{12,4},{16,24},{20,28},{24,16},{28,20},{1,9},{5... | collective-permute-start | bytes 442376 | tf_op jit(solution)/shard_map/ppermute | solution.py:847
  470.6 10.4 %collective-permute-start.48 = (bf16[80,1152]{1,0:T(8,128)(2,1)S(1)}, bf16[80,1152]{1,0:T(8,128)(2,1)S(1)}, u32[]{:S(2)}, u32[]{:S(2)}) collective-permute-start(bf16[80,1152]{1,0:T(8,128)(2,1)S(1)} %fusion.29), channel_id=1, source_target_pairs={{0,16},{4,20},{8,24},{12,28},{16,0},{20,4},{24,8},{28,12},{1,17},{... | collective-permute-start | bytes 552968 | tf_op jit(solution)/shard_map/ppermute | solution.py:847
  473.0 12.4 %collective-permute-start.44 = (bf16[208,1152]{1,0:T(8,128)(2,1)S(1)}, bf16[208,1152]{1,0:T(8,128)(2,1)S(1)}, u32[]{:S(2)}, u32[]{:S(2)}) collective-permute-start(bf16[208,1152]{1,0:T(8,128)(2,1)S(1)} %fusion.5), channel_id=1, source_target_pairs={{0,8},{4,12},{8,0},{12,4},{16,24},{20,28},{24,16},{28,20},{1,9},{5... | collective-permute-start | bytes 1437704 | tf_op jit(solution)/shard_map/ppermute | solution.py:847
  474.8 12.9 %collective-permute-start.45 = (bf16[224,1152]{1,0:T(8,128)(2,1)S(1)}, bf16[224,1152]{1,0:T(8,128)(2,1)}, u32[]{:S(2)}, u32[]{:S(2)}) collective-permute-start(bf16[224,1152]{1,0:T(8,128)(2,1)S(1)} %fusion.4), channel_id=1, source_target_pairs={{0,16},{4,20},{8,24},{12,28},{16,0},{20,4},{24,8},{28,12},{1,17},{... | collective-permute-start | bytes 1548296 | tf_op jit(solution)/shard_map/ppermute | solution.py:847
  476.0 29.8 %collective-permute-start.49 = (bf16[288,1152]{1,0:T(8,128)(2,1)S(1)}, bf16[288,1152]{1,0:T(8,128)(2,1)S(1)}, u32[]{:S(2)}, u32[]{:S(2)}) collective-permute-start(bf16[288,1152]{1,0:T(8,128)(2,1)S(1)} %copy-done.39), channel_id=1, source_target_pairs={{0,2},{1,3},{2,0},{3,1},{4,6},{5,7},{6,4},{7,5},{8,10},{9,11},{10,... | collective-permute-start | bytes 1990664 | tf_op jit(solution)/shard_map/ppermute | solution.py:841
  513.6 13.8 %collective-permute-start.50 = (bf16[144,1152]{1,0:T(8,128)(2,1)S(1)}, bf16[144,1152]{1,0:T(8,128)(2,1)S(1)}, u32[]{:S(2)}, u32[]{:S(2)}) collective-permute-start(bf16[144,1152]{1,0:T(8,128)(2,1)S(1)} %pad_maximum_fusion.25), channel_id=1, source_target_pairs={{0,3},{1,0},{2,1},{3,2},{4,7},{5,4},{6,5},{7,6},{8,11},{9,8},{10,9... | collective-permute-start | bytes 995336 | tf_op jit(solution)/shard_map/ppermute | solution.py:841
  514.6 23.2 %collective-permute-start.51 = (bf16[144,1152]{1,0:T(8,128)(2,1)S(1)}, bf16[144,1152]{1,0:T(8,128)(2,1)S(1)}, u32[]{:S(2)}, u32[]{:S(2)}) collective-permute-start(bf16[144,1152]{1,0:T(8,128)(2,1)S(1)} %pad_maximum_fusion.26), channel_id=1, source_target_pairs={{0,2},{1,3},{2,0},{3,1},{4,6},{5,7},{6,4},{7,5},{8,10},{9,11},{10,... | collective-permute-start | bytes 995336 | tf_op jit(solution)/shard_map/ppermute | solution.py:841
  516.9 28.0 %collective-permute-start.52 = (bf16[144,1152]{1,0:T(8,128)(2,1)S(1)}, bf16[144,1152]{1,0:T(8,128)(2,1)S(1)}, u32[]{:S(2)}, u32[]{:S(2)}) collective-permute-start(bf16[144,1152]{1,0:T(8,128)(2,1)S(1)} %pad_maximum_fusion.27), channel_id=1, source_target_pairs={{0,1},{1,2},{2,3},{3,0},{4,5},{5,6},{6,7},{7,4},{8,9},{9,10},{10,1... | collective-permute-start | bytes 995336 | tf_op jit(solution)/shard_map/ppermute | solution.py:841
  550.4 9.3 %collective-permute-start.55 = (bf16[160,1152]{1,0:T(8,128)(2,1)S(1)}, bf16[160,1152]{1,0:T(8,128)(2,1)S(1)}, u32[]{:S(2)}, u32[]{:S(2)}) collective-permute-start(bf16[160,1152]{1,0:T(8,128)(2,1)S(1)} %pad_maximum_fusion.20), channel_id=1, source_target_pairs={{0,1},{1,2},{2,3},{3,0},{4,5},{5,6},{6,7},{7,4},{8,9},{9,10},{10,1... | collective-permute-start | bytes 1105928 | tf_op jit(solution)/shard_map/ppermute | solution.py:841
  552.7 30.2 %collective-permute-start.56 = (bf16[160,1152]{1,0:T(8,128)(2,1)S(1)}, bf16[160,1152]{1,0:T(8,128)(2,1)S(1)}, u32[]{:S(2)}, u32[]{:S(2)}) collective-permute-start(bf16[160,1152]{1,0:T(8,128)(2,1)S(1)} %pad_maximum_fusion.21), channel_id=1, source_target_pairs={{0,2},{1,3},{2,0},{3,1},{4,6},{5,7},{6,4},{7,5},{8,10},{9,11},{10,... | collective-permute-start | bytes 1105928 | tf_op jit(solution)/shard_map/ppermute | solution.py:841
  553.1 32.7 %collective-permute-start.57 = (bf16[160,1152]{1,0:T(8,128)(2,1)S(1)}, bf16[160,1152]{1,0:T(8,128)(2,1)S(1)}, u32[]{:S(2)}, u32[]{:S(2)}) collective-permute-start(bf16[160,1152]{1,0:T(8,128)(2,1)S(1)} %pad_maximum_fusion.22), channel_id=1, source_target_pairs={{0,3},{1,0},{2,1},{3,2},{4,7},{5,4},{6,5},{7,6},{8,11},{9,8},{10,9... | collective-permute-start | bytes 1105928 | tf_op jit(solution)/shard_map/ppermute | solution.py:841
  599.0 10.4 %collective-permute-start.61 = (bf16[400,256]{1,0:T(8,128)(2,1)S(1)}, bf16[400,256]{1,0:T(8,128)(2,1)S(1)}, u32[]{:S(2)}, u32[]{:S(2)}) collective-permute-start(bf16[400,256]{1,0:T(8,128)(2,1)S(1)} %get-tuple-element.348), channel_id=1, source_target_pairs={{0,24},{4,28},{8,16},{12,20},{16,8},{20,12},{24,0},{28,4},{1,25},{... | collective-permute-start | bytes 614408 | tf_op jit(solution)/shard_map/ppermute | solution.py:847
  612.2 55.2 %collective-permute-start.66 = (bf16[4,1,1152]{2,1,0:T(2,128)(2,1)S(1)}, bf16[4,1,1152]{2,1,0:T(2,128)(2,1)S(1)}, u32[]{:S(2)}, u32[]{:S(2)}) collective-permute-start(bf16[4,1,1152]{2,1,0:T(2,128)(2,1)S(1)} %pad_maximum_fusion.29), channel_id=1, source_target_pairs={{0,4},{4,0},{8,12},{12,8},{16,20},{20,16},{24,28},{28,24},{1,5},{5... | collective-permute-start | bytes 27656 | tf_op jit(solution)/shard_map/ppermute | solution.py:847
  613.3 11.7 %collective-permute-start.65 = (bf16[2,400,256]{2,1,0:T(8,128)(2,1)S(1)}, bf16[2,400,256]{2,1,0:T(8,128)(2,1)S(1)}, u32[]{:S(2)}, u32[]{:S(2)}) collective-permute-start(bf16[2,400,256]{2,1,0:T(8,128)(2,1)S(1)} %pad_maximum_fusion.15.refs_0_), channel_id=1, source_target_pairs={{0,24},{4,28},{8,16},{12,20},{16,8},{20,12},{24,0},{28,4},{1,25},{... | collective-permute-start | bytes 1228808 | tf_op jit(solution)/shard_map/ppermute | solution.py:847
  614.6 19.9 %collective-permute-start.64 = (bf16[2,400,256]{2,1,0:T(8,128)(2,1)S(1)}, bf16[2,400,256]{2,1,0:T(8,128)(2,1)S(1)}, u32[]{:S(2)}, u32[]{:S(2)}) collective-permute-start(bf16[2,400,256]{2,1,0:T(8,128)(2,1)S(1)} %pad_maximum_fusion.15.refs_0_), channel_id=1, source_target_pairs={{0,16},{4,20},{8,24},{12,28},{16,0},{20,4},{24,8},{28,12},{1,17},{... | collective-permute-start | bytes 1228808 | tf_op jit(solution)/shard_map/ppermute | solution.py:847
  614.9 19.5 %collective-permute-start.63 = (bf16[2,400,256]{2,1,0:T(8,128)(2,1)S(1)}, bf16[2,400,256]{2,1,0:T(8,128)(2,1)S(1)}, u32[]{:S(2)}, u32[]{:S(2)}) collective-permute-start(bf16[2,400,256]{2,1,0:T(8,128)(2,1)S(1)} %pad_maximum_fusion.15.refs_0_), channel_id=1, source_target_pairs={{0,8},{4,12},{8,0},{12,4},{16,24},{20,28},{24,16},{28,20},{1,9},{5... | collective-permute-start | bytes 1228808 | tf_op jit(solution)/shard_map/ppermute | solution.py:847
  668.1 13.1 %collective-permute-start.67 = (bf16[4,400,256]{2,1,0:T(8,128)(2,1)}, bf16[4,400,256]{2,1,0:T(8,128)(2,1)S(1)}, u32[]{:S(2)}, u32[]{:S(2)}) collective-permute-start(bf16[4,400,256]{2,1,0:T(8,128)(2,1)} %get-tuple-element.256), channel_id=1, source_target_pairs={{0,4},{4,0},{8,12},{12,8},{16,20},{20,16},{24,28},{28,24},{1,5},{5... | collective-permute-start | bytes 2457608 | tf_op jit(solution)/shard_map/ppermute | solution.py:847
  672.6 64.6 %collective-permute-start.78 = (bf16[2,128,1152]{2,1,0:T(8,128)(2,1)}, bf16[2,128,1152]{2,1,0:T(8,128)(2,1)S(1)}, u32[]{:S(2)}, u32[]{:S(2)}) collective-permute-start(bf16[2,128,1152]{2,1,0:T(8,128)(2,1)} %get-tuple-element.299), channel_id=1, source_target_pairs={{5,0},{1,1},{4,2},{0,3},{7,4},{3,5},{6,6},{2,7},{13,8},{9,9},{12,1... | collective-permute-start | bytes 1769480 | tf_op jit(solution)/shard_map/ppermute | solution.py:994
  674.7 62.5 %collective-permute-start.75 = (bf16[2,128,1152]{2,1,0:T(8,128)(2,1)}, bf16[2,128,1152]{2,1,0:T(8,128)(2,1)S(1)}, u32[]{:S(2)}, u32[]{:S(2)}) collective-permute-start(bf16[2,128,1152]{2,1,0:T(8,128)(2,1)} %get-tuple-element.300), channel_id=1, source_target_pairs={{0,0},{4,1},{1,2},{5,3},{2,4},{6,5},{3,6},{7,7},{8,8},{12,9},{9,10... | collective-permute-start | bytes 1769480 | tf_op jit(solution)/shard_map/ppermute | solution.py:994
  681.9 10.5 %collective-permute-start.70 = (bf16[400,256]{1,0:T(8,128)(2,1)S(1)}, bf16[400,256]{1,0:T(8,128)(2,1)S(1)}, u32[]{:S(2)}, u32[]{:S(2)}) collective-permute-start(bf16[400,256]{1,0:T(8,128)(2,1)S(1)} %get-tuple-element.345), channel_id=1, source_target_pairs={{0,24},{4,28},{8,16},{12,20},{16,8},{20,12},{24,0},{28,4},{1,25},{... | collective-permute-start | bytes 614408 | tf_op jit(solution)/shard_map/ppermute | solution.py:847
  696.3 11.7 %collective-permute-start.74 = (bf16[2,400,256]{2,1,0:T(8,128)(2,1)S(1)}, bf16[2,400,256]{2,1,0:T(8,128)(2,1)S(1)}, u32[]{:S(2)}, u32[]{:S(2)}) collective-permute-start(bf16[2,400,256]{2,1,0:T(8,128)(2,1)S(1)} %pad_maximum_fusion.16.refs_0_), channel_id=1, source_target_pairs={{0,24},{4,28},{8,16},{12,20},{16,8},{20,12},{24,0},{28,4},{1,25},{... | collective-permute-start | bytes 1228808 | tf_op jit(solution)/shard_map/ppermute | solution.py:847
  697.5 20.0 %collective-permute-start.73 = (bf16[2,400,256]{2,1,0:T(8,128)(2,1)S(1)}, bf16[2,400,256]{2,1,0:T(8,128)(2,1)S(1)}, u32[]{:S(2)}, u32[]{:S(2)}) collective-permute-start(bf16[2,400,256]{2,1,0:T(8,128)(2,1)S(1)} %pad_maximum_fusion.16.refs_0_), channel_id=1, source_target_pairs={{0,16},{4,20},{8,24},{12,28},{16,0},{20,4},{24,8},{28,12},{1,17},{... | collective-permute-start | bytes 1228808 | tf_op jit(solution)/shard_map/ppermute | solution.py:847
  698.6 19.5 %collective-permute-start.72 = (bf16[2,400,256]{2,1,0:T(8,128)(2,1)S(1)}, bf16[2,400,256]{2,1,0:T(8,128)(2,1)S(1)}, u32[]{:S(2)}, u32[]{:S(2)}) collective-permute-start(bf16[2,400,256]{2,1,0:T(8,128)(2,1)S(1)} %pad_maximum_fusion.16.refs_0_), channel_id=1, source_target_pairs={{0,8},{4,12},{8,0},{12,4},{16,24},{20,28},{24,16},{28,20},{1,9},{5... | collective-permute-start | bytes 1228808 | tf_op jit(solution)/shard_map/ppermute | solution.py:847
  708.0 29.2 %collective-permute-start.76 = (bf16[2,128,1152]{2,1,0:T(8,128)(2,1)}, bf16[2,128,1152]{2,1,0:T(8,128)(2,1)S(1)}, u32[]{:S(2)}, u32[]{:S(2)}) collective-permute-start(bf16[2,128,1152]{2,1,0:T(8,128)(2,1)} %get-tuple-element.301), channel_id=1, source_target_pairs={{4,0},{0,1},{5,2},{1,3},{6,4},{2,5},{7,6},{3,7},{12,8},{8,9},{13,1... | collective-permute-start | bytes 1769480 | tf_op jit(solution)/shard_map/ppermute | solution.py:994
  717.5 19.8 %collective-permute-start.77 = (bf16[2,128,1152]{2,1,0:T(8,128)(2,1)}, bf16[2,128,1152]{2,1,0:T(8,128)(2,1)S(1)}, u32[]{:S(2)}, u32[]{:S(2)}) collective-permute-start(bf16[2,128,1152]{2,1,0:T(8,128)(2,1)} %get-tuple-element.302), channel_id=1, source_target_pairs={{1,0},{5,1},{0,2},{4,3},{3,4},{7,5},{2,6},{6,7},{9,8},{13,9},{8,10... | collective-permute-start | bytes 1769480 | tf_op jit(solution)/shard_map/ppermute | solution.py:994
  743.5 9.5 %collective-permute-start.81 = (bf16[144,1152]{1,0:T(8,128)(2,1)S(1)}, bf16[144,1152]{1,0:T(8,128)(2,1)S(1)}, u32[]{:S(2)}, u32[]{:S(2)}) collective-permute-start(bf16[144,1152]{1,0:T(8,128)(2,1)S(1)} %get-tuple-element.308), channel_id=1, source_target_pairs={{0,1},{1,2},{2,3},{3,0},{4,5},{5,6},{6,7},{7,4},{8,9},{9,10},{10,1... | collective-permute-start | bytes 995336 | tf_op jit(solution)/shard_map/ppermute | solution.py:841
  743.6 28.7 %collective-permute-start.80 = (bf16[144,1152]{1,0:T(8,128)(2,1)S(1)}, bf16[144,1152]{1,0:T(8,128)(2,1)S(1)}, u32[]{:S(2)}, u32[]{:S(2)}) collective-permute-start(bf16[144,1152]{1,0:T(8,128)(2,1)S(1)} %get-tuple-element.309), channel_id=1, source_target_pairs={{0,2},{1,3},{2,0},{3,1},{4,6},{5,7},{6,4},{7,5},{8,10},{9,11},{10,... | collective-permute-start | bytes 995336 | tf_op jit(solution)/shard_map/ppermute | solution.py:841
  746.0 29.7 %collective-permute-start.79 = (bf16[144,1152]{1,0:T(8,128)(2,1)S(1)}, bf16[144,1152]{1,0:T(8,128)(2,1)S(1)}, u32[]{:S(2)}, u32[]{:S(2)}) collective-permute-start(bf16[144,1152]{1,0:T(8,128)(2,1)S(1)} %get-tuple-element.310), channel_id=1, source_target_pairs={{0,3},{1,0},{2,1},{3,2},{4,7},{5,4},{6,5},{7,6},{8,11},{9,8},{10,9... | collective-permute-start | bytes 995336 | tf_op jit(solution)/shard_map/ppermute | solution.py:841
  (170 other events, 1490.3 us)
Sparse Core Ops, SparseCore 0:
  59.9 166.6 all-gather.3

commit v2 on v1

--- a/solution.py
+++ b/solution.py
@@ -97,7 +97,7 @@
         lse_ref[pl.ds(head, 1), :] = largest + jnp.log2(total)
         return carry
 
-    lax.fori_loop(0, HEADS, one_head, 0)
+    lax.fori_loop(0, HEADS, one_head, 0, unroll=4)
     o_ref[:rows, :] = acc[...].astype(BF)
     head_row = lax.broadcasted_iota(jnp.int32, (HEADS, width), 0)
     lane = lax.broadcasted_iota(jnp.int32, (HEADS, width), 1)
@@ -225,7 +225,7 @@
         dq_acc[:, window] += jnp.where(mask, query_grad.T, 0.0)
         return carry
 
-    lax.fori_loop(0, HEADS, one_head, 0)
+    lax.fori_loop(0, HEADS, one_head, 0, unroll=4)
     dq_ref[:rows, :] = (dq_acc[...] * scale).astype(BF)
     for group, dkv_ref in enumerate(dkv_refs):
         dkv_ref[:, :width] = (dk_acc[group] * scale).astype(dkv_ref.dtype)
@@ -314,7 +314,7 @@
         dn_other[...] = dn_acc[half:, :].astype(BF)
 
 
-def mlp(normed, dm, bias, gathered, first_rows, block=384):
+def mlp(normed, dm, bias, gathered, first_rows, block=768):
     half, width = normed[0].shape
     hidden = bias.shape[1]
     rows = 2 * half
@@ -435,16 +435,15 @@
         copy.wait()
 
 
-def collect(pairs, offset_ref, packed, sems):
+def collect(near, far, offset_ref, packed, sems):
     copies = []
-    unit = pairs[0].shape[1]
-    for index, pair in enumerate(pairs):
-        for side in (0, 1):
-            at = side * len(pairs) + index
-            start = pl.multiple_of(offset_ref[at], 16)
-            copy = pltpu.make_async_copy(pair.at[side], packed.at[pl.ds(start, unit)], sems.at[at])
-            copy.start()
-            copies.append(copy)
+    count, unit = far.shape[0], far.shape[1]
+    for index in range(2 * count):
+        start = pl.multiple_of(offset_ref[index], 16)
+        source = near[index] if index < count else far.at[index - count]
+        copy = pltpu.make_async_copy(source, packed.at[pl.ds(start, unit)], sems.at[index])
+        copy.start()
+        copies.append(copy)
     for copy in copies:
         copy.wait()
 
@@ -489,7 +488,7 @@
     slab_out, kept, sent = refs[:3]
     gram_f, mix_f, prod_f, poly_f, gram_b, mix_b, prod_b, poly_b, slab_t, packed, sems = refs[3:]
     width = slab_ref.shape[1]
-    collect(pairs, offset_ref, packed, sems)
+    collect(pairs[:-1], pairs[-1], offset_ref, packed, sems)
     square = [jnp.zeros((1, 1), F32)]
 
     def add_diagonal(at, w, value):
@@ -580,7 +579,7 @@
     pairs, refs = refs[:count], refs[count:]
     slab_out, gram_b, poly_b, prod_b, join_b, packed, sems = refs
     width = slab_ref.shape[1]
-    collect(pairs, offset_ref, packed, sems)
+    collect(pairs[:-1], pairs[-1], offset_ref, packed, sems)
     unpack(packed, width, lambda at, w, value: store_both(gram_b, at, w, value))
     for step in range(LAST_STEPS):
 
@@ -1074,7 +1073,6 @@
     gathered = spread_rest(former, latter, arrived)
     grad_in = (next_grad.astype(F32) + skip_grad.astype(F32)).astype(BF)
     grad_in, *got = together(grad_in, *flat(gathered), *moved_patches)
-    moved_grad = send(grad_in)
     moved_patches = jnp.concatenate(got[len(got) - seq_count :], axis=0)
     gathered = unflat(got[: len(got) - seq_count], gathered)
     pieces, moves, small = [], [], 0.0
@@ -1122,8 +1120,8 @@
         return lax.ppermute(values, ("batch", "seq"), pairs)
 
     peers = [(step, bit) for step in range(chips) for bit in (0, 1)][1:]
-    sooner = seq_count // 2
-    packed, *moved_grad[:sooner] = together(packed, *moved_grad[:sooner])
+    packed, grad_in = together(packed, grad_in)
+    moved_grad = send(grad_in)
     own_kv = packed[:, width:]
     other_kv = [rotate(own_kv, step, bit, False) for step, bit in peers]
     valid = jnp.stack(
@@ -1374,8 +1372,8 @@
         for index, mask in enumerate(masks[1:]):
             total = total + swap(chip[index + 1], mask, batch_count).astype(F32)
         total = total.astype(BF)
-        pair = jnp.stack([total, swap(total, 1, batch_count)])
-        return [pair] + [swap(pair, mask, batch_count) for mask in masks[1:]]
+        near = [total] + [swap(total, mask, batch_count) for mask in masks[1:]]
+        return near + [swap(jnp.stack(near), 1, batch_count)]
 
     unit_offsets = offsets * (packed_rows(width, batch_count) // batch_count)
     slab, kept, sent = first_steps(plane_sum(*gram(slab, unit_offsets)), slab, unit_offsets)

time: 802 us -> 776 us (0.968)
  Pallas kernels: 233 us -> 222 us
  waiting for transfers between devices: 268 us -> 259 us
    ppermute x53, waiting for transfers between devices: 87.3 us -> 71.9 us  [swap(): lax.ppermute(values, 'batch', [(rank, rank ^ bit) for rank in range(batch...]
    unnamed x311 -> x295, local copies, waits for them, and re-layouts: 29.4 us -> 29.2 us
  transfers between devices with their start and end apart: 83 -> 83, of which waited for: 36 -> 42; matrix products, arithmetic and copies ran while one was open for 12% -> 13% of each run, Pallas kernels for 21% -> 21%
where the time goes in v2:
time: 776 us; the launch traced here: 767 us
  waiting for transfers between devices  259 us (33%)
  Pallas kernels  222 us (29%)
  starting transfers between devices  92.3 us (12%)
  other arithmetic  77.1 us (10%)
  local copies, waits for them, and re-layouts  66.8 us (9%)
  between operations  25.2 us (3%)
  matrix products  15.1 us (2%)
  blocking collectives  9.52 us (1%)
    ppermute x15, waiting for transfers between devices, shift(): lax.ppermute(values, 'seq', [(rank, (rank + step) % seq_count) for rank i...  121 us
    ppermute x53, waiting for transfers between devices, swap(): lax.ppermute(values, 'batch', [(rank, rank ^ bit) for rank in range(batch...  71.9 us
    ppermute x8, waiting for transfers between devices, send(): lax.ppermute(lax.dynamic_index_in_dim(pieces, seq_rank ^ matching, 0, Fal...  63.3 us
    pallas_call x1, Pallas kernels, mlp(): pl.pallas_call(functools.partial(mlp_kernel, units, unit, block), grid=(h...  56.9 us
    pallas_call x1, Pallas kernels, attention_backward(): pl.pallas_call(functools.partial(attention_backward_kernel, groups), out_...  43.9 us
    ppermute x53, starting transfers between devices, swap(): lax.ppermute(values, 'batch', [(rank, rank ^ bit) for rank in range(batch...  39.4 us
    pallas_call x1, Pallas kernels, first_steps(): pl.pallas_call(functools.partial(first_steps_kernel, len(pairs)), out_sha...  31.2 us
    unnamed x295, local copies, waits for them, and re-layouts  29.2 us
  transfers between devices with their start and end apart: 83, of which 42 were waited for; matrix products, arithmetic and copies ran while one was open for 13% of the time, Pallas kernels for 21%

profile of v2, /device:TPU:9, one launch (start us, length us, event | category | flops | bytes accessed | tf_op | source)
XLA Modules:
  0.0 766.8 jit_solution(2512466192566778231)
XLA Ops:
  7.3 2.4 copy.265.refs_2_
  9.8 9.5 %all-gather.1 = s32[8,2,2]{2,1,0:T(2,128)S(1)} all-gather(s32[1,2,2]{2,1,0:T(2,128)S(1)} %add_bitcast_fusion), channel_id=2, replica_groups=mesh['batch'=8,'seq'=4] {'batch'}, dimensions={0}, use_global_device_ids=true | all-gather | bytes 144 | tf_op jit(solution)/shard_map/all_gather | solution.py:1019
  26.2 5.1 collective-permute-done.2.refs_3_
  31.3 17.5 %collective-permute-done.1.refs_2_ = bf16[176,1152]{1,0:T(8,128)(2,1)S(1)} collective-permute-done((bf16[176,1152]{1,0:T(8,128)(2,1)S(1)}, bf16[176,1152]{1,0:T(8,128)(2,1)S(1)}, u32[]{:S(2)}, u32[]{:S(2)}) %collective-permute-start.1) | collective-permute-done | bytes 405536 | tf_op jit(solution)/shard_map/ppermute | solution.py:840
  48.8 8.7 %collective-permute-done.refs_1_ = bf16[176,1152]{1,0:T(8,128)(2,1)S(1)} collective-permute-done((bf16[176,1152]{1,0:T(8,128)(2,1)S(1)}, bf16[176,1152]{1,0:T(8,128)(2,1)S(1)}, u32[]{:S(2)}, u32[]{:S(2)}) %collective-permute-start) | collective-permute-done | bytes 405536 | tf_op jit(solution)/shard_map/ppermute | solution.py:840
  64.7 5.1 collective-permute-start.11
  69.7 8.7 %collective-permute-done.12.refs_12_ = bf16[128,1152]{1,0:T(8,128)(2,1)S(1)} collective-permute-done((bf16[128,1152]{1,0:T(8,128)(2,1)S(1)}, bf16[128,1152]{1,0:T(8,128)(2,1)S(1)}, u32[]{:S(2)}, u32[]{:S(2)}) %collective-permute-start.12) | collective-permute-done | bytes 294944 | tf_op jit(solution)/shard_map/ppermute | solution.py:982
  82.5 9.7 %collective-permute-done.11.refs_11_ = bf16[128,1152]{1,0:T(8,128)(2,1)S(1)} collective-permute-done((bf16[128,1152]{1,0:T(8,128)(2,1)S(1)}, bf16[128,1152]{1,0:T(8,128)(2,1)S(1)}, u32[]{:S(2)}, u32[]{:S(2)}) %collective-permute-start.11) | collective-permute-done | bytes 294944 | tf_op jit(solution)/shard_map/ppermute | solution.py:982
  93.7 9.6 %collective-permute-done.10.refs_10_ = bf16[128,1152]{1,0:T(8,128)(2,1)S(1)} collective-permute-done((bf16[128,1152]{1,0:T(8,128)(2,1)S(1)}, bf16[128,1152]{1,0:T(8,128)(2,1)S(1)}, u32[]{:S(2)}, u32[]{:S(2)}) %collective-permute-start.10) | collective-permute-done | bytes 294944 | tf_op jit(solution)/shard_map/ppermute | solution.py:982
  106.0 2.6 add_convert_fusion.9.refs_0_
  108.7 16.4 %collective-permute-done.9.refs_9_ = bf16[128,1152]{1,0:T(8,128)(2,1)S(1)} collective-permute-done((bf16[128,1152]{1,0:T(8,128)(2,1)S(1)}, bf16[128,1152]{1,0:T(8,128)(2,1)S(1)}, u32[]{:S(2)}, u32[]{:S(2)}) %collective-permute-start.9) | collective-permute-done | bytes 294944 | tf_op jit(solution)/shard_map/ppermute | solution.py:982
  125.1 6.1 collective-permute-done.5.refs_4_
  142.5 8.1 %place.1 = (bf16[3456,1152]{1,0:T(8,128)(2,1)}, bf16[1152,1152]{1,0:T(8,128)(2,1)S(1)}) custom-call(s32[24]{0:T(128)S(1)} %stack.216.offset_ref, bf16[288,1152]{1,0:T(8,128)(2,1)S(1)} %copy-done.9, bf16[288,1152]{1,0:T(8,128)(2,1)S(1)} %collective-permute-done.17.refs_1_, bf16[288,1152]{1,0:T(8,128)(2,1)S(1)} %copy-done.16, ...), custom_call_target="tpu_custom_call" | custom-call | bytes 21233664 | tf_op jit(solution)/shard_map/place/pallas_call | solution.py:802
  156.6 6.6 convolution_convert_fusion.refs_0_
  163.3 3.4 slice.433
  179.0 3.7 collective-permute-start.26
  188.1 26.2 %attention_forward.1 = (bf16[528,1152]{1,0:T(8,128)(2,1)}, f32[16,512]{1,0:T(8,128)}, f32[16,128]{1,0:T(8,128)}) custom-call(s32[2]{0:T(128)} %stack.188.valid_ref, bf16[528,3456]{1,0:T(8,128)(2,1)} %get-tuple-element.160.own_ref, bf16[528,2304]{1,0:T(8,128)(2,1)} %collective-permute-done.21.refs_0_), custom_call_target="tpu_custom_call" | custom-call | flops 9663676416 | bytes 7299072 | tf_op jit(solution)/shard_map/attention_forward/pallas_call | solution.py:134
  214.4 11.2 %collective-permute-done.25.refs_4_ = bf16[128,1152]{1,0:T(8,128)(2,1)S(1)} collective-permute-done((bf16[128,1152]{1,0:T(8,128)(2,1)}, bf16[128,1152]{1,0:T(8,128)(2,1)S(1)}, u32[]{:S(2)}, u32[]{:S(2)}) %collective-permute-start.25) | collective-permute-done | bytes 294944 | tf_op jit(solution)/shard_map/ppermute | solution.py:982
  225.6 6.4 collective-permute-done.24.refs_3_
  233.2 4.1 fusion.72
  238.7 2.7 collective-permute-start.27
  248.0 56.9 %mlp.1 = (f32[528,1152]{1,0:T(8,128)}, bf16[528,1152]{1,0:T(8,128)(2,1)}, f32[528,1152]{1,0:T(8,128)}, bf16[528,1152]{1,0:T(8,128)(2,1)}, bf16[2304,1152]{1,0:T(...) custom-call(s32[16]{0:T(128)} %mul.403.first_ref, f32[1,2304]{1,0:T(1,128)} %reshape.460.bias_ref, ...), custom_call_target="tpu_custom_call" | custom-call | flops 33634123776 | bytes 40697856 | tf_op jit(solution)/shard_map/mlp/pallas_call | solution.py:338
  306.9 3.6 concatenate.97
  316.5 2.5 fusion.65
  319.0 2.9 convolution_convert_fusion.1.refs_2_
  321.9 43.9 %attention_backward.1 = (bf16[528,1152]{1,0:T(8,128)(2,1)}, bf16[528,2304]{1,0:T(8,128)(2,1)}, bf16[528,2304]{1,0:T(8,128)(2,1)}) custom-call(s32[2]{0:T(128)} %stack.188.valid_ref, bf16[528,3456]{1,0:T(8,128)(2,1)} %get-tuple-element.160.own_ref, bf16[528,2304]{1,0:T(8,128)(2,1)} %collective-permute-done.21.refs_0_, ...), custom_call_target="tpu_custom_call" | custom-call | flops 21743271936 | bytes 14598144 | tf_op jit(solution)/shard_map/attention_backward/pallas_call | solution.py:239
  365.8 6.5 collective-permute-done.31.refs_4_
  373.0 3.1 add_convert_fusion.7
  376.2 3.1 add_convert_fusion.6
  385.2 5.0 qkv_grad.1
  397.5 14.5 %packed_grad.1 = (bf16[528,3456]{1,0:T(8,128)(2,1)}, bf16[4,432,1152]{2,1,0:T(8,128)(2,1)}, bf16[4,432,1152]{2,1,0:T(8,128)(2,1)}) custom-call(s32[8]{0:T(128)S(1)} %get-tuple-element.374.offset_ref, bf16[528,1152]{1,0:T(8,128)(2,1)S(1)} %copy-done.24, bf16[528,2304]{1,0:T(8,128)(2,1)} %get-tuple-element.190.own_ref, ...), custom_call_target="tpu_custom_call" | custom-call | flops 4204265472 | bytes 16478208 | tf_op jit(solution)/shard_map/packed_grad/pallas_call | solution.py:692
  415.4 2.6 add_convert_fusion.2
  418.0 2.6 add_convert_fusion.4
  422.2 4.3 add_convert_fusion
  435.7 12.5 %first_norm_back.1 = (bf16[528,1152]{1,0:T(8,128)(2,1)}, f32[16,1152]{1,0:T(8,128)}) custom-call(bf16[528,3456]{1,0:T(8,128)(2,1)} %together.27.packed_ref, bf16[3456,1152]{1,0:T(8,128)(2,1)} %get-tuple-element.158.weight_ref, f32[528,1152]{1,0:T(8,128)} %get-tuple-element.286.standard_ref, f32[528,1]{1,0:T(8,128)} %rsqrt.16.inverse_ref, ...), custom_call_target="tpu_custom_call" | custom-call | flops 4204265472 | bytes 17694720 | tf_op jit(solution)/shard_map/first_norm_back/pallas_call | solution.py:726
  450.9 13.5 %collective-permute-done.43.refs_9_ = bf16[160,1152]{1,0:T(8,128)(2,1)S(1)} collective-permute-done((bf16[160,1152]{1,0:T(8,128)(2,1)}, bf16[160,1152]{1,0:T(8,128)(2,1)S(1)}, u32[]{:S(2)}, u32[]{:S(2)}) %collective-permute-start.43) | collective-permute-done | bytes 368672 | tf_op jit(solution)/shard_map/ppermute | solution.py:846
  470.2 2.9 collective-permute-start.46
  479.1 3.2 add_convert_fusion.8.refs_5_
  482.4 5.9 collective-permute-done.44.refs_0_
  489.0 2.4 collective-permute-done.45.refs_1_
  491.5 15.5 %collective-permute-done.49.refs_5_ = bf16[288,1152]{1,0:T(8,128)(2,1)S(1)} collective-permute-done((bf16[288,1152]{1,0:T(8,128)(2,1)S(1)}, bf16[288,1152]{1,0:T(8,128)(2,1)S(1)}, u32[]{:S(2)}, u32[]{:S(2)}) %collective-permute-start.49) | collective-permute-done | bytes 663584 | tf_op jit(solution)/shard_map/ppermute | solution.py:840
  515.3 2.8 collective-permute-start.50
  518.6 2.4 collective-permute-start.52
  525.2 3.2 collective-permute-done.54
  529.1 10.4 %collective-permute-done.51.refs_2_ = bf16[144,1152]{1,0:T(8,128)(2,1)S(1)} collective-permute-done((bf16[144,1152]{1,0:T(8,128)(2,1)S(1)}, bf16[144,1152]{1,0:T(8,128)(2,1)S(1)}, u32[]{:S(2)}, u32[]{:S(2)}) %collective-permute-start.51) | collective-permute-done | bytes 331808 | tf_op jit(solution)/shard_map/ppermute | solution.py:840
  539.5 7.1 collective-permute-done.52.refs_3_
  556.5 4.9 collective-permute-done.55.refs_1_
  561.4 23.2 %collective-permute-done.56.refs_2_ = bf16[160,1152]{1,0:T(8,128)(2,1)S(1)} collective-permute-done((bf16[160,1152]{1,0:T(8,128)(2,1)S(1)}, bf16[160,1152]{1,0:T(8,128)(2,1)S(1)}, u32[]{:S(2)}, u32[]{:S(2)}) %collective-permute-start.56) | collective-permute-done | bytes 368672 | tf_op jit(solution)/shard_map/ppermute | solution.py:840
  590.6 4.8 gram.1
  602.9 2.9 collective-permute-done.59
  605.8 4.4 collective-permute-done.61
  616.0 5.4 collective-permute-done.63.refs_2_
  626.3 31.2 %first_steps.1 = (bf16[576,1152]{1,0:T(8,128)(2,1)}, bf16[4,400,256]{2,1,0:T(8,128)(2,1)}, bf16[4,400,256]{2,1,0:T(8,128)(2,1)}) custom-call(s32[8]{0:T(128)} %copy-done.25, bf16[576,1152]{1,0:T(8,128)(2,1)} %copy-done.21, bf16[400,256]{1,0:T(8,128)(2,1)} %copy-done.92, bf16[400,256]{1,0:T(8,128)(2,1)} %copy-done.107, bf16[400,256]{1,0:T(8,128)(2,1)} %copy-done.106, ...), custom_call_target="tpu_custom_call" | custom-call | flops 27518828544 | bytes 7962624 | tf_op jit(solution)/shard_map/first_steps/pallas_call | solution.py:559
  663.0 4.9 collective-permute-start.75
  675.2 4.8 collective-permute-done.70
  683.4 2.3 collective-permute-done.73.refs_3_
  685.8 4.9 collective-permute-start.76
  690.7 2.4 collective-permute-start.77
  696.8 18.3 %last_steps.1.refs_0_ = bf16[576,1152]{1,0:T(8,128)(2,1)} custom-call(s32[8]{0:T(128)} %copy-done.25, bf16[576,1152]{1,0:T(8,128)(2,1)} %get-tuple-element.252.slab_ref, bf16[400,256]{1,0:T(8,128)(2,1)} %copy-done.91, bf16[400,256]{1,0:T(8,128)(2,1)} %copy-done.104, bf16[400,256]{1,0:T(8,128)(2,1)} %copy-done.103, bf16[400,256]{1,0:T(8,128)(2,1)} %copy-done.102, ...), custom_call_target="tpu_custom_call" | custom-call | flops 15288238080 | bytes 5308416 | tf_op jit(solution)/shard_map/last_steps/pallas_call | solution.py:614
  715.2 2.5 collective-permute-done.76.refs_2_
  723.7 3.2 collective-permute-start.80
  729.2 4.2 collective-permute-done.81
  733.5 18.1 %collective-permute-done.80 = bf16[144,1152]{1,0:T(8,128)(2,1)S(1)} collective-permute-done((bf16[144,1152]{1,0:T(8,128)(2,1)S(1)}, bf16[144,1152]{1,0:T(8,128)(2,1)S(1)}, u32[]{:S(2)}, u32[]{:S(2)}) %collective-permute-start.80) | collective-permute-done | bytes 331808 | tf_op jit(solution)/shard_map/ppermute | solution.py:840
  751.5 4.3 collective-permute-done.79
  (637 shorter events, 187.2 us)
Async XLA Ops:
  7.3 240.7 %all-gather.4.cloned.1.call-start = ((), (), s32[]{:S(2)}) async-start(), calls=%async_computation | async-start | bytes 11280384 | tf_op jit(solution)/shard_map/all_gather | solution.py:1041
  20.5 10.8 %collective-permute-start.2 = (bf16[176,1152]{1,0:T(8,128)(2,1)S(1)}, bf16[176,1152]{1,0:T(8,128)(2,1)S(1)}, u32[]{:S(2)}, u32[]{:S(2)}) collective-permute-start(bf16[176,1152]{1,0:T(8,128)(2,1)S(1)} %pad_maximum_fusion.17.refs_0_), channel_id=1, source_target_pairs={{0,3},{1,0},{2,1},{3,2},{4,7},{5,4},{6,5},{7,6},{8,11},{9,8},{10,9... | collective-permute-start | bytes 1216520 | tf_op jit(solution)/shard_map/ppermute | solution.py:840
  20.7 28.1 %collective-permute-start.1 = (bf16[176,1152]{1,0:T(8,128)(2,1)S(1)}, bf16[176,1152]{1,0:T(8,128)(2,1)S(1)}, u32[]{:S(2)}, u32[]{:S(2)}) collective-permute-start(bf16[176,1152]{1,0:T(8,128)(2,1)S(1)} %pad_maximum_fusion.17.refs_0_), channel_id=1, source_target_pairs={{0,2},{1,3},{2,0},{3,1},{4,6},{5,7},{6,4},{7,5},{8,10},{9,11},{10,... | collective-permute-start | bytes 1216520 | tf_op jit(solution)/shard_map/ppermute | solution.py:840
  23.0 34.5 %collective-permute-start = (bf16[176,1152]{1,0:T(8,128)(2,1)S(1)}, bf16[176,1152]{1,0:T(8,128)(2,1)S(1)}, u32[]{:S(2)}, u32[]{:S(2)}) collective-permute-start(bf16[176,1152]{1,0:T(8,128)(2,1)S(1)} %pad_maximum_fusion.17.refs_0_), channel_id=1, source_target_pairs={{0,1},{1,2},{2,3},{3,0},{4,5},{5,6},{6,7},{7,4},{8,9},{9,10},{10,1... | collective-permute-start | bytes 1216520 | tf_op jit(solution)/shard_map/ppermute | solution.py:840
  59.8 21.4 %collective-permute-start.7 = (bf16[320,1152]{1,0:T(8,128)(2,1)}, bf16[320,1152]{1,0:T(8,128)(2,1)S(1)}, u32[]{:S(2)}, u32[]{:S(2)}) collective-permute-start(bf16[320,1152]{1,0:T(8,128)(2,1)} %get-tuple-element.144.refs_5_), channel_id=1, source_target_pairs={{0,16},{4,20},{8,24},{12,28},{16,0},{20,4},{24,8},{28,12},{1,17},{... | collective-permute-start | bytes 2211848 | tf_op jit(solution)/shard_map/ppermute | solution.py:846
  61.1 32.4 %collective-permute-start.3 = (bf16[288,1152]{1,0:T(8,128)(2,1)}, bf16[288,1152]{1,0:T(8,128)(2,1)S(1)}, u32[]{:S(2)}, u32[]{:S(2)}) collective-permute-start(bf16[288,1152]{1,0:T(8,128)(2,1)} %get-tuple-element.143.refs_1_), channel_id=1, source_target_pairs={{0,8},{4,12},{8,0},{12,4},{16,24},{20,28},{24,16},{28,20},{1,9},{5... | collective-permute-start | bytes 1990664 | tf_op jit(solution)/shard_map/ppermute | solution.py:846
  62.7 15.8 %collective-permute-start.12 = (bf16[128,1152]{1,0:T(8,128)(2,1)S(1)}, bf16[128,1152]{1,0:T(8,128)(2,1)S(1)}, u32[]{:S(2)}, u32[]{:S(2)}) collective-permute-start(bf16[128,1152]{1,0:T(8,128)(2,1)S(1)} %get-tuple-element.332), channel_id=1, source_target_pairs={{0,5},{1,1},{2,4},{3,0},{4,7},{5,3},{6,6},{7,2},{8,13},{9,9},{10,1... | collective-permute-start | bytes 884744 | tf_op jit(solution)/shard_map/ppermute | solution.py:982
  64.7 27.5 %collective-permute-start.11 = (bf16[128,1152]{1,0:T(8,128)(2,1)S(1)}, bf16[128,1152]{1,0:T(8,128)(2,1)S(1)}, u32[]{:S(2)}, u32[]{:S(2)}) collective-permute-start(bf16[128,1152]{1,0:T(8,128)(2,1)S(1)} %get-tuple-element.333), channel_id=1, source_target_pairs={{0,1},{1,5},{2,0},{3,4},{4,3},{5,7},{6,2},{7,6},{8,9},{9,13},{10,8... | collective-permute-start | bytes 884744 | tf_op jit(solution)/shard_map/ppermute | solution.py:982
  69.7 33.6 %collective-permute-start.10 = (bf16[128,1152]{1,0:T(8,128)(2,1)S(1)}, bf16[128,1152]{1,0:T(8,128)(2,1)S(1)}, u32[]{:S(2)}, u32[]{:S(2)}) collective-permute-start(bf16[128,1152]{1,0:T(8,128)(2,1)S(1)} %get-tuple-element.334), channel_id=1, source_target_pairs={{0,4},{1,0},{2,5},{3,1},{4,6},{5,2},{6,7},{7,3},{8,12},{9,8},{10,1... | collective-permute-start | bytes 884744 | tf_op jit(solution)/shard_map/ppermute | solution.py:982
  78.5 46.6 %collective-permute-start.6 = (bf16[320,1152]{1,0:T(8,128)(2,1)S(1)}, bf16[320,1152]{1,0:T(8,128)(2,1)S(1)}, u32[]{:S(2)}, u32[]{:S(2)}) collective-permute-start(bf16[320,1152]{1,0:T(8,128)(2,1)S(1)} %copy-done.5), channel_id=1, source_target_pairs={{0,8},{4,12},{8,0},{12,4},{16,24},{20,28},{24,16},{28,20},{1,9},{5... | collective-permute-start | bytes 2211848 | tf_op jit(solution)/shard_map/ppermute | solution.py:846
  81.2 50.8 %collective-permute-start.8 = (bf16[320,1152]{1,0:T(8,128)(2,1)S(1)}, bf16[320,1152]{1,0:T(8,128)(2,1)}, u32[]{:S(2)}, u32[]{:S(2)}) collective-permute-start(bf16[320,1152]{1,0:T(8,128)(2,1)S(1)} %collective-permute-done.7.refs_7_), channel_id=1, source_target_pairs={{0,8},{4,12},{8,0},{12,4},{16,24},{20,28},{24,16},{28,20},{1,9},{5... | collective-permute-start | bytes 2211848 | tf_op jit(solution)/shard_map/ppermute | solution.py:846
  92.2 32.8 %collective-permute-start.4 = (bf16[288,1152]{1,0:T(8,128)(2,1)S(1)}, bf16[288,1152]{1,0:T(8,128)(2,1)S(1)}, u32[]{:S(2)}, u32[]{:S(2)}) collective-permute-start(bf16[288,1152]{1,0:T(8,128)(2,1)S(1)} %copy-done.8), channel_id=1, source_target_pairs={{0,16},{4,20},{8,24},{12,28},{16,0},{20,4},{24,8},{28,12},{1,17},{... | collective-permute-start | bytes 1990664 | tf_op jit(solution)/shard_map/ppermute | solution.py:846
  93.5 37.7 %collective-permute-start.5 = (bf16[288,1152]{1,0:T(8,128)(2,1)S(1)}, bf16[288,1152]{1,0:T(8,128)(2,1)S(1)}, u32[]{:S(2)}, u32[]{:S(2)}) collective-permute-start(bf16[288,1152]{1,0:T(8,128)(2,1)S(1)} %collective-permute-done.3.refs_2_), channel_id=1, source_target_pairs={{0,16},{4,20},{8,24},{12,28},{16,0},{20,4},{24,8},{28,12},{1,17},{... | collective-permute-start | bytes 1990664 | tf_op jit(solution)/shard_map/ppermute | solution.py:846
  104.1 21.0 %collective-permute-start.9 = (bf16[128,1152]{1,0:T(8,128)(2,1)S(1)}, bf16[128,1152]{1,0:T(8,128)(2,1)S(1)}, u32[]{:S(2)}, u32[]{:S(2)}) collective-permute-start(bf16[128,1152]{1,0:T(8,128)(2,1)S(1)} %get-tuple-element.335), channel_id=1, source_target_pairs={{0,0},{1,4},{2,1},{3,5},{4,2},{5,6},{6,3},{7,7},{8,8},{9,12},{10,9... | collective-permute-start | bytes 884744 | tf_op jit(solution)/shard_map/ppermute | solution.py:982
  166.6 18.8 %collective-permute-start.21 = (bf16[528,2304]{1,0:T(8,128)(2,1)}, bf16[528,2304]{1,0:T(8,128)(2,1)}, u32[]{:S(2)}, u32[]{:S(2)}) collective-permute-start(bf16[528,2304]{1,0:T(8,128)(2,1)} %slice.433), channel_id=1, source_target_pairs={{4,0},{5,1},{6,2},{7,3},{0,4},{1,5},{2,6},{3,7},{12,8},{13,9},{14,... | collective-permute-start | bytes 7299080 | tf_op jit(solution)/shard_map/ppermute | solution.py:1120
  167.3 47.1 %collective-permute-start.22 = (bf16[2,2,1152]{2,1,0:T(2,128)(2,1)S(1)}, bf16[2,2,1152]{2,1,0:T(2,128)(2,1)S(1)}, u32[]{:S(2)}, u32[]{:S(2)}) collective-permute-start(bf16[2,2,1152]{2,1,0:T(2,128)(2,1)S(1)} %add_convert_fusion.16), channel_id=1, source_target_pairs={{0,4},{4,0},{8,12},{12,8},{16,20},{20,16},{24,28},{28,24},{1,5},{5... | collective-permute-start | bytes 27656 | tf_op jit(solution)/shard_map/ppermute | solution.py:846
  179.0 35.4 %collective-permute-start.26 = (bf16[128,1152]{1,0:T(8,128)(2,1)}, bf16[128,1152]{1,0:T(8,128)(2,1)S(1)}, u32[]{:S(2)}, u32[]{:S(2)}) collective-permute-start(bf16[128,1152]{1,0:T(8,128)(2,1)} %get-tuple-element.328), channel_id=1, source_target_pairs={{0,5},{1,1},{2,4},{3,0},{4,7},{5,3},{6,6},{7,2},{8,13},{9,9},{10,1... | collective-permute-start | bytes 884744 | tf_op jit(solution)/shard_map/ppermute | solution.py:982
  182.7 42.9 %collective-permute-start.25 = (bf16[128,1152]{1,0:T(8,128)(2,1)}, bf16[128,1152]{1,0:T(8,128)(2,1)S(1)}, u32[]{:S(2)}, u32[]{:S(2)}) collective-permute-start(bf16[128,1152]{1,0:T(8,128)(2,1)} %get-tuple-element.329), channel_id=1, source_target_pairs={{0,1},{1,5},{2,0},{3,4},{4,3},{5,7},{6,2},{7,6},{8,9},{9,13},{10,8... | collective-permute-start | bytes 884744 | tf_op jit(solution)/shard_map/ppermute | solution.py:982
  184.3 47.8 %collective-permute-start.24 = (bf16[128,1152]{1,0:T(8,128)(2,1)}, bf16[128,1152]{1,0:T(8,128)(2,1)}, u32[]{:S(2)}, u32[]{:S(2)}) collective-permute-start(bf16[128,1152]{1,0:T(8,128)(2,1)} %get-tuple-element.330), channel_id=1, source_target_pairs={{0,4},{1,0},{2,5},{3,1},{4,6},{5,2},{6,7},{7,3},{8,12},{9,8},{10,1... | collective-permute-start | bytes 884744 | tf_op jit(solution)/shard_map/ppermute | solution.py:982
  185.5 47.7 %collective-permute-start.23 = (bf16[128,1152]{1,0:T(8,128)(2,1)S(1)}, bf16[128,1152]{1,0:T(8,128)(2,1)}, u32[]{:S(2)}, u32[]{:S(2)}) collective-permute-start(bf16[128,1152]{1,0:T(8,128)(2,1)S(1)} %get-tuple-element.331), channel_id=1, source_target_pairs={{0,0},{1,4},{2,1},{3,5},{4,2},{5,6},{6,3},{7,7},{8,8},{9,12},{10,9... | collective-permute-start | bytes 884744 | tf_op jit(solution)/shard_map/ppermute | solution.py:982
  238.7 9.2 %collective-permute-start.27 = (bf16[528,1152]{1,0:T(8,128)(2,1)S(1)}, bf16[528,1152]{1,0:T(8,128)(2,1)}, u32[]{:S(2)}, u32[]{:S(2)}) collective-permute-start(bf16[528,1152]{1,0:T(8,128)(2,1)S(1)} %multiply_convert_fusion.n_own), channel_id=1, source_target_pairs={{0,4},{4,0},{8,12},{12,8},{16,20},{20,16},{24,28},{28,24},{1,5},{5... | collective-permute-start | bytes 3649544 | tf_op jit(solution)/shard_map/ppermute | solution.py:846
  306.3 8.9 %collective-permute-start.29 = (bf16[528,1152]{1,0:T(8,128)(2,1)}, bf16[528,1152]{1,0:T(8,128)(2,1)S(1)}, u32[]{:S(2)}, u32[]{:S(2)}) collective-permute-start(bf16[528,1152]{1,0:T(8,128)(2,1)} %get-tuple-element.172), channel_id=1, source_target_pairs={{0,4},{4,0},{8,12},{12,8},{16,20},{20,16},{24,28},{28,24},{1,5},{5... | collective-permute-start | bytes 3649544 | tf_op jit(solution)/shard_map/ppermute | solution.py:846
  306.5 59.3 %collective-permute-start.32 = (bf16[528,1152]{1,0:T(8,128)(2,1)}, bf16[528,1152]{1,0:T(8,128)(2,1)S(1)}, u32[]{:S(2)}, u32[]{:S(2)}) collective-permute-start(bf16[528,1152]{1,0:T(8,128)(2,1)} %get-tuple-element.180), channel_id=1, source_target_pairs={{0,4},{4,0},{8,12},{12,8},{16,20},{20,16},{24,28},{28,24},{1,5},{5... | collective-permute-start | bytes 3649544 | tf_op jit(solution)/shard_map/ppermute | solution.py:846
  312.8 59.5 %collective-permute-start.31 = (bf16[1152,1152]{1,0:T(8,128)(2,1)}, bf16[1152,1152]{1,0:T(8,128)(2,1)}, u32[]{:S(2)}, u32[]{:S(2)}) collective-permute-start(bf16[1152,1152]{1,0:T(8,128)(2,1)} %pad_maximum_fusion), channel_id=1, source_target_pairs={{0,8},{4,12},{8,0},{12,4},{16,24},{20,28},{24,16},{28,20},{1,9},{5... | collective-permute-start | bytes 7962632 | tf_op jit(solution)/shard_map/ppermute | solution.py:846
  314.0 59.0 %collective-permute-start.30 = (bf16[1152,1152]{1,0:T(8,128)(2,1)}, bf16[1152,1152]{1,0:T(8,128)(2,1)}, u32[]{:S(2)}, u32[]{:S(2)}) collective-permute-start(bf16[1152,1152]{1,0:T(8,128)(2,1)} %concatenate.97), channel_id=1, source_target_pairs={{0,16},{4,20},{8,24},{12,28},{16,0},{20,4},{24,8},{28,12},{1,17},{... | collective-permute-start | bytes 7962632 | tf_op jit(solution)/shard_map/ppermute | solution.py:846
  379.3 32.8 %collective-permute-start.36 = (bf16[576,1152]{1,0:T(8,128)(2,1)}, bf16[576,1152]{1,0:T(8,128)(2,1)}, u32[]{:S(2)}, u32[]{:S(2)}) collective-permute-start(bf16[576,1152]{1,0:T(8,128)(2,1)} %add_convert_fusion.6), channel_id=1, source_target_pairs={{0,16},{4,20},{8,24},{12,28},{16,0},{20,4},{24,8},{28,12},{1,17},{... | collective-permute-start | bytes 3981320 | tf_op jit(solution)/shard_map/ppermute | solution.py:846
  380.5 31.5 %collective-permute-start.35 = (bf16[576,1152]{1,0:T(8,128)(2,1)}, bf16[576,1152]{1,0:T(8,128)(2,1)}, u32[]{:S(2)}, u32[]{:S(2)}) collective-permute-start(bf16[576,1152]{1,0:T(8,128)(2,1)} %add_convert_fusion.7), channel_id=1, source_target_pairs={{0,8},{4,12},{8,0},{12,4},{16,24},{20,28},{24,16},{28,20},{1,9},{5... | collective-permute-start | bytes 3981320 | tf_op jit(solution)/shard_map/ppermute | solution.py:846
  380.9 10.4 %collective-permute-start.33 = (bf16[528,2304]{1,0:T(8,128)(2,1)}, bf16[528,2304]{1,0:T(8,128)(2,1)}, u32[]{:S(2)}, u32[]{:S(2)}) collective-permute-start(bf16[528,2304]{1,0:T(8,128)(2,1)} %get-tuple-element.189), channel_id=1, source_target_pairs={{0,4},{1,5},{2,6},{3,7},{4,0},{5,1},{6,2},{7,3},{8,12},{9,13},{10,... | collective-permute-start | bytes 7299080 | tf_op jit(solution)/shard_map/ppermute | solution.py:1120
  391.3 20.8 %collective-permute-start.34 = (bf16[4,144,1152]{2,1,0:T(8,128)(2,1)}, bf16[4,144,1152]{2,1,0:T(8,128)(2,1)}, u32[]{:S(2)}, u32[]{:S(2)}) collective-permute-start(bf16[4,144,1152]{2,1,0:T(8,128)(2,1)} %get-tuple-element.196), channel_id=1, source_target_pairs={{0,4},{4,0},{8,12},{12,8},{16,20},{20,16},{24,28},{28,24},{1,5},{5... | collective-permute-start | bytes 3981320 | tf_op jit(solution)/shard_map/ppermute | solution.py:846
  412.1 10.0 %collective-permute-start.37 = (bf16[4,432,1152]{2,1,0:T(8,128)(2,1)}, bf16[4,432,1152]{2,1,0:T(8,128)(2,1)}, u32[]{:S(2)}, u32[]{:S(2)}) collective-permute-start(bf16[4,432,1152]{2,1,0:T(8,128)(2,1)} %get-tuple-element.200), channel_id=1, source_target_pairs={{0,4},{4,0},{8,12},{12,8},{16,20},{20,16},{24,28},{28,24},{1,5},{5... | collective-permute-start | bytes 11943944 | tf_op jit(solution)/shard_map/ppermute | solution.py:846
  415.2 19.9 %collective-permute-start.42 = (bf16[128,1152]{1,0:T(8,128)(2,1)}, bf16[128,1152]{1,0:T(8,128)(2,1)}, u32[]{:S(2)}, u32[]{:S(2)}) collective-permute-start(bf16[128,1152]{1,0:T(8,128)(2,1)} %pad_maximum_fusion.28), channel_id=1, source_target_pairs={{0,16},{4,20},{8,24},{12,28},{16,0},{20,4},{24,8},{28,12},{1,17},{... | collective-permute-start | bytes 884744 | tf_op jit(solution)/shard_map/ppermute | solution.py:846
  428.5 35.9 %collective-permute-start.40 = (bf16[288,1152]{1,0:T(8,128)(2,1)}, bf16[288,1152]{1,0:T(8,128)(2,1)}, u32[]{:S(2)}, u32[]{:S(2)}) collective-permute-start(bf16[288,1152]{1,0:T(8,128)(2,1)} %get-tuple-element.211), channel_id=1, source_target_pairs={{0,3},{1,0},{2,1},{3,2},{4,7},{5,4},{6,5},{7,6},{8,11},{9,8},{10,9... | collective-permute-start | bytes 1990664 | tf_op jit(solution)/shard_map/ppermute | solution.py:840
  428.5 35.9 %collective-permute-start.41 = (bf16[288,1152]{1,0:T(8,128)(2,1)}, bf16[288,1152]{1,0:T(8,128)(2,1)}, u32[]{:S(2)}, u32[]{:S(2)}) collective-permute-start(bf16[288,1152]{1,0:T(8,128)(2,1)} %get-tuple-element.212), channel_id=1, source_target_pairs={{0,1},{1,2},{2,3},{3,0},{4,5},{5,6},{6,7},{7,4},{8,9},{9,10},{10,1... | collective-permute-start | bytes 1990664 | tf_op jit(solution)/shard_map/ppermute | solution.py:840
  431.1 33.3 %collective-permute-start.38 = (bf16[416,1152]{1,0:T(8,128)(2,1)}, bf16[416,1152]{1,0:T(8,128)(2,1)S(1)}, u32[]{:S(2)}, u32[]{:S(2)}) collective-permute-start(bf16[416,1152]{1,0:T(8,128)(2,1)} %pad_maximum_fusion.11), channel_id=1, source_target_pairs={{0,16},{4,20},{8,24},{12,28},{16,0},{20,4},{24,8},{28,12},{1,17},{... | collective-permute-start | bytes 2875400 | tf_op jit(solution)/shard_map/ppermute | solution.py:846
  433.4 31.0 %collective-permute-start.39 = (bf16[448,1152]{1,0:T(8,128)(2,1)}, bf16[448,1152]{1,0:T(8,128)(2,1)S(1)}, u32[]{:S(2)}, u32[]{:S(2)}) collective-permute-start(bf16[448,1152]{1,0:T(8,128)(2,1)} %pad_maximum_fusion.9), channel_id=1, source_target_pairs={{0,8},{4,12},{8,0},{12,4},{16,24},{20,28},{24,16},{28,20},{1,9},{5... | collective-permute-start | bytes 3096584 | tf_op jit(solution)/shard_map/ppermute | solution.py:846
  435.2 29.2 %collective-permute-start.43 = (bf16[160,1152]{1,0:T(8,128)(2,1)}, bf16[160,1152]{1,0:T(8,128)(2,1)S(1)}, u32[]{:S(2)}, u32[]{:S(2)}) collective-permute-start(bf16[160,1152]{1,0:T(8,128)(2,1)} %pad_maximum_fusion.18), channel_id=1, source_target_pairs={{0,8},{4,12},{8,0},{12,4},{16,24},{20,28},{24,16},{28,20},{1,9},{5... | collective-permute-start | bytes 1105928 | tf_op jit(solution)/shard_map/ppermute | solution.py:846
  468.3 14.1 %collective-permute-start.47 = (bf16[64,1152]{1,0:T(8,128)(2,1)}, bf16[64,1152]{1,0:T(8,128)(2,1)}, u32[]{:S(2)}, u32[]{:S(2)}) collective-permute-start(bf16[64,1152]{1,0:T(8,128)(2,1)} %fusion.34), channel_id=1, source_target_pairs={{0,8},{4,12},{8,0},{12,4},{16,24},{20,28},{24,16},{28,20},{1,9},{5... | collective-permute-start | bytes 442376 | tf_op jit(solution)/shard_map/ppermute | solution.py:846
  470.2 8.8 %collective-permute-start.46 = (f32[26,1152]{1,0:T(8,128)S(1)}, f32[26,1152]{1,0:T(8,128)S(1)}, u32[]{:S(2)}, u32[]{:S(2)}) collective-permute-start(f32[26,1152]{1,0:T(8,128)S(1)} %concatenate.104), channel_id=1, source_target_pairs={{0,4},{4,0},{8,12},{12,8},{16,20},{20,16},{24,28},{28,24},{1,5},{5... | collective-permute-start | bytes 359432 | tf_op jit(solution)/shard_map/ppermute | solution.py:846
  475.8 12.4 %collective-permute-start.44 = (bf16[208,1152]{1,0:T(8,128)(2,1)S(1)}, bf16[208,1152]{1,0:T(8,128)(2,1)S(1)}, u32[]{:S(2)}, u32[]{:S(2)}) collective-permute-start(bf16[208,1152]{1,0:T(8,128)(2,1)S(1)} %fusion.5), channel_id=1, source_target_pairs={{0,8},{4,12},{8,0},{12,4},{16,24},{20,28},{24,16},{28,20},{1,9},{5... | collective-permute-start | bytes 1437704 | tf_op jit(solution)/shard_map/ppermute | solution.py:846
  477.7 13.8 %collective-permute-start.45 = (bf16[224,1152]{1,0:T(8,128)(2,1)S(1)}, bf16[224,1152]{1,0:T(8,128)(2,1)}, u32[]{:S(2)}, u32[]{:S(2)}) collective-permute-start(bf16[224,1152]{1,0:T(8,128)(2,1)S(1)} %fusion.4), channel_id=1, source_target_pairs={{0,16},{4,20},{8,24},{12,28},{16,0},{20,4},{24,8},{28,12},{1,17},{... | collective-permute-start | bytes 1548296 | tf_op jit(solution)/shard_map/ppermute | solution.py:846
  479.0 28.0 %collective-permute-start.49 = (bf16[288,1152]{1,0:T(8,128)(2,1)S(1)}, bf16[288,1152]{1,0:T(8,128)(2,1)S(1)}, u32[]{:S(2)}, u32[]{:S(2)}) collective-permute-start(bf16[288,1152]{1,0:T(8,128)(2,1)S(1)} %copy-done.40), channel_id=1, source_target_pairs={{0,2},{1,3},{2,0},{3,1},{4,6},{5,7},{6,4},{7,5},{8,10},{9,11},{10,... | collective-permute-start | bytes 1990664 | tf_op jit(solution)/shard_map/ppermute | solution.py:840
  514.3 9.8 %collective-permute-start.53 = (f32[26,1152]{1,0:T(8,128)S(1)}, f32[26,1152]{1,0:T(8,128)S(1)}, u32[]{:S(2)}, u32[]{:S(2)}) collective-permute-start(f32[26,1152]{1,0:T(8,128)S(1)} %add.674), channel_id=1, source_target_pairs={{0,8},{4,12},{8,0},{12,4},{16,24},{20,28},{24,16},{28,20},{1,9},{5... | collective-permute-start | bytes 359432 | tf_op jit(solution)/shard_map/ppermute | solution.py:846
  515.3 13.8 %collective-permute-start.50 = (bf16[144,1152]{1,0:T(8,128)(2,1)S(1)}, bf16[144,1152]{1,0:T(8,128)(2,1)S(1)}, u32[]{:S(2)}, u32[]{:S(2)}) collective-permute-start(bf16[144,1152]{1,0:T(8,128)(2,1)S(1)} %pad_maximum_fusion.25), channel_id=1, source_target_pairs={{0,3},{1,0},{2,1},{3,2},{4,7},{5,4},{6,5},{7,6},{8,11},{9,8},{10,9... | collective-permute-start | bytes 995336 | tf_op jit(solution)/shard_map/ppermute | solution.py:840
  518.2 21.3 %collective-permute-start.51 = (bf16[144,1152]{1,0:T(8,128)(2,1)S(1)}, bf16[144,1152]{1,0:T(8,128)(2,1)S(1)}, u32[]{:S(2)}, u32[]{:S(2)}) collective-permute-start(bf16[144,1152]{1,0:T(8,128)(2,1)S(1)} %pad_maximum_fusion.26), channel_id=1, source_target_pairs={{0,2},{1,3},{2,0},{3,1},{4,6},{5,7},{6,4},{7,5},{8,10},{9,11},{10,... | collective-permute-start | bytes 995336 | tf_op jit(solution)/shard_map/ppermute | solution.py:840
  518.6 28.0 %collective-permute-start.52 = (bf16[144,1152]{1,0:T(8,128)(2,1)S(1)}, bf16[144,1152]{1,0:T(8,128)(2,1)S(1)}, u32[]{:S(2)}, u32[]{:S(2)}) collective-permute-start(bf16[144,1152]{1,0:T(8,128)(2,1)S(1)} %pad_maximum_fusion.27), channel_id=1, source_target_pairs={{0,1},{1,2},{2,3},{3,0},{4,5},{5,6},{6,7},{7,4},{8,9},{9,10},{10,1... | collective-permute-start | bytes 995336 | tf_op jit(solution)/shard_map/ppermute | solution.py:840
  552.1 9.3 %collective-permute-start.55 = (bf16[160,1152]{1,0:T(8,128)(2,1)S(1)}, bf16[160,1152]{1,0:T(8,128)(2,1)S(1)}, u32[]{:S(2)}, u32[]{:S(2)}) collective-permute-start(bf16[160,1152]{1,0:T(8,128)(2,1)S(1)} %pad_maximum_fusion.20), channel_id=1, source_target_pairs={{0,1},{1,2},{2,3},{3,0},{4,5},{5,6},{6,7},{7,4},{8,9},{9,10},{10,1... | collective-permute-start | bytes 1105928 | tf_op jit(solution)/shard_map/ppermute | solution.py:840
  554.4 30.2 %collective-permute-start.56 = (bf16[160,1152]{1,0:T(8,128)(2,1)S(1)}, bf16[160,1152]{1,0:T(8,128)(2,1)S(1)}, u32[]{:S(2)}, u32[]{:S(2)}) collective-permute-start(bf16[160,1152]{1,0:T(8,128)(2,1)S(1)} %pad_maximum_fusion.21), channel_id=1, source_target_pairs={{0,2},{1,3},{2,0},{3,1},{4,6},{5,7},{6,4},{7,5},{8,10},{9,11},{10,... | collective-permute-start | bytes 1105928 | tf_op jit(solution)/shard_map/ppermute | solution.py:840
  554.5 32.1 %collective-permute-start.57 = (bf16[160,1152]{1,0:T(8,128)(2,1)S(1)}, bf16[160,1152]{1,0:T(8,128)(2,1)S(1)}, u32[]{:S(2)}, u32[]{:S(2)}) collective-permute-start(bf16[160,1152]{1,0:T(8,128)(2,1)S(1)} %pad_maximum_fusion.22), channel_id=1, source_target_pairs={{0,3},{1,0},{2,1},{3,2},{4,7},{5,4},{6,5},{7,6},{8,11},{9,8},{10,9... | collective-permute-start | bytes 1105928 | tf_op jit(solution)/shard_map/ppermute | solution.py:840
  600.0 10.2 %collective-permute-start.61 = (bf16[400,256]{1,0:T(8,128)(2,1)S(1)}, bf16[400,256]{1,0:T(8,128)(2,1)S(1)}, u32[]{:S(2)}, u32[]{:S(2)}) collective-permute-start(bf16[400,256]{1,0:T(8,128)(2,1)S(1)} %get-tuple-element.346), channel_id=1, source_target_pairs={{0,24},{4,28},{8,16},{12,20},{16,8},{20,12},{24,0},{28,4},{1,25},{... | collective-permute-start | bytes 614408 | tf_op jit(solution)/shard_map/ppermute | solution.py:846
  601.0 9.3 %collective-permute-start.60 = (bf16[400,256]{1,0:T(8,128)(2,1)S(1)}, bf16[400,256]{1,0:T(8,128)(2,1)S(1)}, u32[]{:S(2)}, u32[]{:S(2)}) collective-permute-start(bf16[400,256]{1,0:T(8,128)(2,1)S(1)} %get-tuple-element.347), channel_id=1, source_target_pairs={{0,16},{4,20},{8,24},{12,28},{16,0},{20,4},{24,8},{28,12},{1,17},{... | collective-permute-start | bytes 614408 | tf_op jit(solution)/shard_map/ppermute | solution.py:846
  611.8 9.6 %collective-permute-start.63 = (bf16[400,256]{1,0:T(8,128)(2,1)S(1)}, bf16[400,256]{1,0:T(8,128)(2,1)S(1)}, u32[]{:S(2)}, u32[]{:S(2)}) collective-permute-start(bf16[400,256]{1,0:T(8,128)(2,1)S(1)} %fusion.27.refs_0_), channel_id=1, source_target_pairs={{0,16},{4,20},{8,24},{12,28},{16,0},{20,4},{24,8},{28,12},{1,17},{... | collective-permute-start | bytes 614408 | tf_op jit(solution)/shard_map/ppermute | solution.py:846
  612.0 9.4 %collective-permute-start.62 = (bf16[400,256]{1,0:T(8,128)(2,1)S(1)}, bf16[400,256]{1,0:T(8,128)(2,1)S(1)}, u32[]{:S(2)}, u32[]{:S(2)}) collective-permute-start(bf16[400,256]{1,0:T(8,128)(2,1)S(1)} %fusion.27.refs_0_), channel_id=1, source_target_pairs={{0,8},{4,12},{8,0},{12,4},{16,24},{20,28},{24,16},{28,20},{1,9},{5... | collective-permute-start | bytes 614408 | tf_op jit(solution)/shard_map/ppermute | solution.py:846
  624.4 33.2 %collective-permute-start.66 = (bf16[4,1,1152]{2,1,0:T(2,128)(2,1)S(1)}, bf16[4,1,1152]{2,1,0:T(2,128)(2,1)S(1)}, u32[]{:S(2)}, u32[]{:S(2)}) collective-permute-start(bf16[4,1,1152]{2,1,0:T(2,128)(2,1)S(1)} %pad_maximum_fusion.29), channel_id=1, source_target_pairs={{0,4},{4,0},{8,12},{12,8},{16,20},{20,16},{24,28},{28,24},{1,5},{5... | collective-permute-start | bytes 27656 | tf_op jit(solution)/shard_map/ppermute | solution.py:846
  658.2 9.7 %collective-permute-start.67 = (bf16[4,400,256]{2,1,0:T(8,128)(2,1)}, bf16[4,400,256]{2,1,0:T(8,128)(2,1)}, u32[]{:S(2)}, u32[]{:S(2)}) collective-permute-start(bf16[4,400,256]{2,1,0:T(8,128)(2,1)} %get-tuple-element.254), channel_id=1, source_target_pairs={{0,4},{4,0},{8,12},{12,8},{16,20},{20,16},{24,28},{28,24},{1,5},{5... | collective-permute-start | bytes 2457608 | tf_op jit(solution)/shard_map/ppermute | solution.py:846
  661.0 54.1 %collective-permute-start.78 = (bf16[2,128,1152]{2,1,0:T(8,128)(2,1)}, bf16[2,128,1152]{2,1,0:T(8,128)(2,1)S(1)}, u32[]{:S(2)}, u32[]{:S(2)}) collective-permute-start(bf16[2,128,1152]{2,1,0:T(8,128)(2,1)} %get-tuple-element.297), channel_id=1, source_target_pairs={{5,0},{1,1},{4,2},{0,3},{7,4},{3,5},{6,6},{2,7},{13,8},{9,9},{12,1... | collective-permute-start | bytes 1769480 | tf_op jit(solution)/shard_map/ppermute | solution.py:993
  663.0 52.2 %collective-permute-start.75 = (bf16[2,128,1152]{2,1,0:T(8,128)(2,1)}, bf16[2,128,1152]{2,1,0:T(8,128)(2,1)S(1)}, u32[]{:S(2)}, u32[]{:S(2)}) collective-permute-start(bf16[2,128,1152]{2,1,0:T(8,128)(2,1)} %get-tuple-element.298), channel_id=1, source_target_pairs={{0,0},{4,1},{1,2},{5,3},{2,4},{6,5},{3,6},{7,7},{8,8},{12,9},{9,10... | collective-permute-start | bytes 1769480 | tf_op jit(solution)/shard_map/ppermute | solution.py:993
  670.0 9.9 %collective-permute-start.70 = (bf16[400,256]{1,0:T(8,128)(2,1)S(1)}, bf16[400,256]{1,0:T(8,128)(2,1)S(1)}, u32[]{:S(2)}, u32[]{:S(2)}) collective-permute-start(bf16[400,256]{1,0:T(8,128)(2,1)S(1)} %get-tuple-element.343), channel_id=1, source_target_pairs={{0,24},{4,28},{8,16},{12,20},{16,8},{20,12},{24,0},{28,4},{1,25},{... | collective-permute-start | bytes 614408 | tf_op jit(solution)/shard_map/ppermute | solution.py:846
  681.2 9.5 %collective-permute-start.72 = (bf16[400,256]{1,0:T(8,128)(2,1)S(1)}, bf16[400,256]{1,0:T(8,128)(2,1)S(1)}, u32[]{:S(2)}, u32[]{:S(2)}) collective-permute-start(bf16[400,256]{1,0:T(8,128)(2,1)S(1)} %fusion.24.refs_0_), channel_id=1, source_target_pairs={{0,16},{4,20},{8,24},{12,28},{16,0},{20,4},{24,8},{28,12},{1,17},{... | collective-permute-start | bytes 614408 | tf_op jit(solution)/shard_map/ppermute | solution.py:846
  682.4 10.8 %collective-permute-start.71 = (bf16[400,256]{1,0:T(8,128)(2,1)S(1)}, bf16[400,256]{1,0:T(8,128)(2,1)S(1)}, u32[]{:S(2)}, u32[]{:S(2)}) collective-permute-start(bf16[400,256]{1,0:T(8,128)(2,1)S(1)} %fusion.24.refs_0_), channel_id=1, source_target_pairs={{0,8},{4,12},{8,0},{12,4},{16,24},{20,28},{24,16},{28,20},{1,9},{5... | collective-permute-start | bytes 614408 | tf_op jit(solution)/shard_map/ppermute | solution.py:846
  685.8 31.9 %collective-permute-start.76 = (bf16[2,128,1152]{2,1,0:T(8,128)(2,1)}, bf16[2,128,1152]{2,1,0:T(8,128)(2,1)S(1)}, u32[]{:S(2)}, u32[]{:S(2)}) collective-permute-start(bf16[2,128,1152]{2,1,0:T(8,128)(2,1)} %get-tuple-element.299), channel_id=1, source_target_pairs={{4,0},{0,1},{5,2},{1,3},{6,4},{2,5},{7,6},{3,7},{12,8},{8,9},{13,1... | collective-permute-start | bytes 1769480 | tf_op jit(solution)/shard_map/ppermute | solution.py:993
  690.7 26.9 %collective-permute-start.77 = (bf16[2,128,1152]{2,1,0:T(8,128)(2,1)S(1)}, bf16[2,128,1152]{2,1,0:T(8,128)(2,1)S(1)}, u32[]{:S(2)}, u32[]{:S(2)}) collective-permute-start(bf16[2,128,1152]{2,1,0:T(8,128)(2,1)S(1)} %get-tuple-element.300), channel_id=1, source_target_pairs={{1,0},{5,1},{0,2},{4,3},{3,4},{7,5},{2,6},{6,7},{9,8},{13,9},{8,10... | collective-permute-start | bytes 1769480 | tf_op jit(solution)/shard_map/ppermute | solution.py:993
  723.6 9.8 %collective-permute-start.81 = (bf16[144,1152]{1,0:T(8,128)(2,1)S(1)}, bf16[144,1152]{1,0:T(8,128)(2,1)S(1)}, u32[]{:S(2)}, u32[]{:S(2)}) collective-permute-start(bf16[144,1152]{1,0:T(8,128)(2,1)S(1)} %get-tuple-element.306), channel_id=1, source_target_pairs={{0,1},{1,2},{2,3},{3,0},{4,5},{5,6},{6,7},{7,4},{8,9},{9,10},{10,1... | collective-permute-start | bytes 995336 | tf_op jit(solution)/shard_map/ppermute | solution.py:840
  723.7 27.8 %collective-permute-start.80 = (bf16[144,1152]{1,0:T(8,128)(2,1)S(1)}, bf16[144,1152]{1,0:T(8,128)(2,1)S(1)}, u32[]{:S(2)}, u32[]{:S(2)}) collective-permute-start(bf16[144,1152]{1,0:T(8,128)(2,1)S(1)} %get-tuple-element.307), channel_id=1, source_target_pairs={{0,2},{1,3},{2,0},{3,1},{4,6},{5,7},{6,4},{7,5},{8,10},{9,11},{10,... | collective-permute-start | bytes 995336 | tf_op jit(solution)/shard_map/ppermute | solution.py:840
  726.8 29.0 %collective-permute-start.79 = (bf16[144,1152]{1,0:T(8,128)(2,1)S(1)}, bf16[144,1152]{1,0:T(8,128)(2,1)S(1)}, u32[]{:S(2)}, u32[]{:S(2)}) collective-permute-start(bf16[144,1152]{1,0:T(8,128)(2,1)S(1)} %get-tuple-element.308), channel_id=1, source_target_pairs={{0,3},{1,0},{2,1},{3,2},{4,7},{5,4},{6,5},{7,6},{8,11},{9,8},{10,9... | collective-permute-start | bytes 995336 | tf_op jit(solution)/shard_map/ppermute | solution.py:840
  (162 other events, 1622.7 us)
Sparse Core Ops, SparseCore 0:
  59.9 167.6 all-gather.3

commit v3 on v2

--- a/solution.py
+++ b/solution.py
@@ -57,12 +57,12 @@
 
 
 def attention_forward_kernel(groups, valid_ref, own_ref, *refs):
-    others, (o_ref, lse_ref, lsex_ref, acc) = refs[: groups - 1], refs[groups - 1 :]
+    held, (o_ref, lse_ref, lsex_ref, acc) = refs[:groups], refs[groups:]
     rows = own_ref.shape[0] - 16
-    width = own_ref.shape[1] // 3
+    width = own_ref.shape[1]
     size = width // HEADS
     factor = size**-0.5 * LOG2E
-    tables = [(own_ref, width, 2 * width)] + [(ref, 0, width) for ref in others]
+    tables = [(ref, 0, width) for ref in held]
     parts = []
     for group, (ref, key_at, value_at) in enumerate(tables):
         parts.append((ref, pl.ds(0, rows), key_at, value_at, None))
@@ -127,9 +127,9 @@
     lsex_ref[...] = jnp.broadcast_to(largest + jnp.log2(total), (HEADS, 128))
 
 
-def attention_forward(valid, own, others):
-    padded, wide = own.shape
-    rows, width, groups = padded - 16, wide // 3, 1 + len(others)
+def attention_forward(valid, query, held):
+    padded, width = query.shape
+    rows, groups = padded - 16, len(held)
     pairs = rows * groups * rows
     return pl.pallas_call(
         functools.partial(attention_forward_kernel, groups),
@@ -138,31 +138,31 @@
             shape_of((HEADS, rows), F32),
             shape_of((HEADS, 128), F32),
         ],
-        in_specs=[pl.BlockSpec(memory_space=pltpu.SMEM)] + in_vmem(groups),
+        in_specs=[pl.BlockSpec(memory_space=pltpu.SMEM)] + in_vmem(1 + groups),
         out_specs=in_vmem(3),
         scratch_shapes=[pltpu.VMEM((rows, width), F32)],
         compiler_params=pltpu.CompilerParams(vmem_limit_bytes=60 * MIB),
         cost_estimate=pl.CostEstimate(
             flops=16 * pairs * width,
-            bytes_accessed=groups * padded * wide * 2,
+            bytes_accessed=groups * padded * width * 6,
             transcendentals=HEADS * pairs,
         ),
         name="attention_forward",
-    )(valid, own, *others)
+    )(valid, query, *held)
 
 
 def attention_backward_kernel(groups, valid_ref, own_ref, *refs):
-    others, refs = refs[: groups - 1], refs[groups - 1 :]
+    held, refs = refs[:groups], refs[groups:]
     o_ref, do_ref, lse_ref, lsex_ref = refs[:4]
     dq_ref, dkv_refs, refs = refs[4], refs[5 : 5 + groups], refs[5 + groups :]
     dq_acc, dk_acc, dv_acc, delta = refs
     rows = own_ref.shape[0] - 16
     padded = rows + 16
-    width = own_ref.shape[1] // 3
+    width = own_ref.shape[1]
     size = width // HEADS
     scale = size**-0.5
     factor = scale * LOG2E
-    tables = [(own_ref, width, 2 * width)] + [(ref, 0, width) for ref in others]
+    tables = [(ref, 0, width) for ref in held]
     parts = []
     for group, (ref, key_at, value_at) in enumerate(tables):
         parts.append((ref, 0, rows, key_at, value_at, group, None))
@@ -232,15 +232,15 @@
         dkv_ref[:, width:] = dv_acc[group].astype(dkv_ref.dtype)
 
 
-def attention_backward(valid, own, others, attended, attended_grad, lse, lse_extra):
-    padded, wide = own.shape
-    rows, width, groups = padded - 16, wide // 3, 1 + len(others)
+def attention_backward(valid, query, held, attended, attended_grad, lse, lse_extra):
+    padded, width = query.shape
+    rows, groups = padded - 16, len(held)
     pairs = rows * groups * rows
     return pl.pallas_call(
         functools.partial(attention_backward_kernel, groups),
         out_shape=[shape_of((padded, width), BF)]
         + [shape_of((padded, 2 * width), BF) for _ in range(groups)],
-        in_specs=[pl.BlockSpec(memory_space=pltpu.SMEM)] + in_vmem(groups + 4),
+        in_specs=[pl.BlockSpec(memory_space=pltpu.SMEM)] + in_vmem(groups + 5),
         out_specs=in_vmem(1 + groups),
         scratch_shapes=[
             pltpu.VMEM((rows, width), F32),
@@ -251,11 +251,11 @@
         compiler_params=pltpu.CompilerParams(vmem_limit_bytes=60 * MIB),
         cost_estimate=pl.CostEstimate(
             flops=36 * pairs * width,
-            bytes_accessed=2 * groups * padded * wide * 2,
+            bytes_accessed=2 * groups * padded * width * 6,
             transcendentals=HEADS * pairs,
         ),
         name="attention_backward",
-    )(valid, own, *others, attended, attended_grad, lse, lse_extra)
+    )(valid, query, *held, attended, attended_grad, lse, lse_extra)
 
 
 def mlp_kernel(
@@ -629,7 +629,7 @@
 
 
 def line_up_kernel(counts, place_ref, *refs):
-    line, qkv, proj, small_at = counts
+    line, qkv, proj, small_at, folds, columns = counts
     blocks, (former, latter, held, joined) = refs[:line], refs[line:]
     for step, block in enumerate(blocks):
         held[step] = block[...]
@@ -640,7 +640,13 @@
         joined[index * qkv : (index + 1) * qkv, :] = value[:qkv]
         at = line * qkv + index * proj
         joined[at : at + proj, :] = value[qkv : qkv + proj]
-        small = value[small_at:]
+        small = jnp.concatenate(
+            [value[small_at:, 128 * fold : 128 * (fold + 1)] for fold in range(folds)], axis=0
+        )
+        small = jnp.concatenate(
+            [small, jnp.zeros((16 * folds, value.shape[1] - 128), F32)], axis=1
+        )
+        small = pltpu.roll(small, (place_ref[1] * line + index) * columns, 1)
         total = small if total is None else total + small
     half = former.shape[0]
     rest = line * (qkv + proj) - half
@@ -649,16 +655,16 @@
     latter[rest:, :] = total.astype(BF)
 
 
-def line_up(blocks, place, qkv, proj):
+def line_up(blocks, place, qkv, proj, folds, columns):
     line = len(blocks)
     rows, width = blocks[0].shape
     small_at = -(-(qkv + proj) // 16) * 16
     half = line * (qkv + proj) // 2
     return pl.pallas_call(
-        functools.partial(line_up_kernel, (line, qkv, proj, small_at)),
+        functools.partial(line_up_kernel, (line, qkv, proj, small_at, folds, columns)),
         out_shape=[
             shape_of((half, width), BF),
-            shape_of((line * (qkv + proj) - half + rows - small_at, width), BF),
+            shape_of((line * (qkv + proj) - half + 16 * folds, width), BF),
         ],
         in_specs=[SMEM] + in_vmem(line),
         out_specs=in_vmem(2),
@@ -668,7 +674,7 @@
         ],
         compiler_params=pltpu.CompilerParams(vmem_limit_bytes=40 * MIB),
         name="line_up",
-    )(place.reshape(1), *blocks)
+    )(place, *blocks)
 
 
 def packed_grad_kernel(offset_ref, query_ref, own_ref, arrived_ref, other_ref, packed, kept, sent, grad, sems):
@@ -1024,14 +1030,16 @@
     class_part = dot_nn(selector, table.astype(BF)).astype(BF)
     small = jnp.concatenate([vectors.astype(BF), class_part], axis=0)
     small_rows = -(-small.shape[0] // 16) * 16
-    small = lax.dynamic_update_slice(
-        jnp.zeros((small_rows, width), BF), small, (0, shard_rank * column_count)
-    )
+    small = jnp.pad(small, ((0, small_rows - small.shape[0]), (0, 128 - column_count)))
+    small = jnp.transpose(small.reshape(-1, 16, 128), (1, 0, 2)).reshape(16, -1)
+    small = jnp.pad(small, ((0, 0), (0, width - small.shape[1])))
 
     gap = -(qkv_width + proj_width) % 16
     load = [low_qkv, low_proj] + ([jnp.zeros((gap, width), BF)] if gap else []) + [small]
     line = line_gather(jnp.concatenate(load, axis=0), seq_count)
-    former, latter = line_up(line, seq_rank, qkv_width, proj_width)
+    former, latter = line_up(
+        line, jnp.stack([seq_rank, batch_rank]), qkv_width, proj_width, small_rows // 16, column_count
+    )
     former, latter, patches, own_mlp = together(former, latter, patches, own_mlp)
 
     same_core = [
@@ -1107,7 +1115,8 @@
     tokens = jnp.concatenate([moved_patches.astype(F32), extra_tile], axis=0)
     standard_one, inverse_one = standardize(tokens)
     normed = ((standard_one * vec_values[0] + vec_values[1]) * row_valid).astype(BF)
-    packed = dot_nt(normed, full_qkv).astype(BF)
+    own_kv = dot_nt(normed, full_qkv[width:]).astype(BF)
+    query = dot_nt(normed, full_qkv[:width]).astype(BF)
 
     def rotate(values, step, core_bit, back):
         pairs = []
@@ -1120,9 +1129,8 @@
         return lax.ppermute(values, ("batch", "seq"), pairs)
 
     peers = [(step, bit) for step in range(chips) for bit in (0, 1)][1:]
-    packed, grad_in = together(packed, grad_in)
+    own_kv, grad_in = together(own_kv, grad_in)
     moved_grad = send(grad_in)
-    own_kv = packed[:, width:]
     other_kv = [rotate(own_kv, step, bit, False) for step, bit in peers]
     valid = jnp.stack(
         [has_extra.astype(jnp.int32)]
@@ -1130,7 +1138,7 @@
     )
     in_extra = (next_extra.astype(F32) + skip_extra.astype(F32)).astype(BF)
     in_extra_other = swap(in_extra, 1, batch_count)
-    attended, lse, lse_extra = attention_forward(valid, packed, other_kv)
+    attended, lse, lse_extra = attention_forward(valid, query, [own_kv, *other_kv])
     attended, in_extra_other, *moved_grad = together(attended, in_extra_other, *moved_grad)
     in_extra = jnp.where(own_core == core, in_extra, in_extra_other)
     in_extra = lax.dynamic_index_in_dim(in_extra, own_slot, 0, False)
@@ -1200,7 +1208,7 @@
 
     attended_grad = dot_nn(middle_low, full_proj).astype(BF)
     out_arrived = swap(out_other, 1, batch_count)
-    backward = attention_backward(valid, packed, other_kv, attended, attended_grad, lse, lse_extra)
+    backward = attention_backward(valid, query, [own_kv, *other_kv], attended, attended_grad, lse, lse_extra)
     *backward, moved_up, moved_down, out_arrived, middle_low, attended, middle = together(
         *backward, *moved, out_arrived, middle_low, attended, middle
     )

time: 776 us -> 773 us (level)
    unnamed x295 -> x294, local copies, waits for them, and re-layouts: 29.2 us -> 29.7 us
where the time goes in v3:
time: 773 us; the launch traced here: 764 us
  waiting for transfers between devices  255 us (33%)
  Pallas kernels  222 us (29%)
  starting transfers between devices  92.3 us (12%)
  other arithmetic  77.1 us (10%)
  local copies, waits for them, and re-layouts  64.5 us (8%)
  between operations  25 us (3%)
  matrix products  17.9 us (2%)
  blocking collectives  9.52 us (1%)
    ppermute x15, waiting for transfers between devices, shift(): lax.ppermute(values, 'seq', [(rank, (rank + step) % seq_count) for rank i...  118 us
    ppermute x53, waiting for transfers between devices, swap(): lax.ppermute(values, 'batch', [(rank, rank ^ bit) for rank in range(batch...  72.2 us
    ppermute x8, waiting for transfers between devices, send(): lax.ppermute(lax.dynamic_index_in_dim(pieces, seq_rank ^ matching, 0, Fal...  62.4 us
    pallas_call x1, Pallas kernels, mlp(): pl.pallas_call(functools.partial(mlp_kernel, units, unit, block), grid=(h...  56.9 us
    pallas_call x1, Pallas kernels, attention_backward(): pl.pallas_call(functools.partial(attention_backward_kernel, groups), out_...  43.8 us
    ppermute x53, starting transfers between devices, swap(): lax.ppermute(values, 'batch', [(rank, rank ^ bit) for rank in range(batch...  39.5 us
    pallas_call x1, Pallas kernels, first_steps(): pl.pallas_call(functools.partial(first_steps_kernel, len(pairs)), out_sha...  31.2 us
    unnamed x294, local copies, waits for them, and re-layouts  29.7 us
  transfers between devices with their start and end apart: 83, of which 42 were waited for; matrix products, arithmetic and copies ran while one was open for 13% of the time, Pallas kernels for 21%

profile of v3, /device:TPU:9, one launch (start us, length us, event | category | flops | bytes accessed | tf_op | source)
XLA Modules:
  0.0 763.6 jit_solution(6145503022781111478)
XLA Ops:
  7.3 2.5 copy.271.refs_2_
  9.8 9.5 %all-gather.1 = s32[8,2,2]{2,1,0:T(2,128)S(1)} all-gather(s32[1,2,2]{2,1,0:T(2,128)S(1)} %add_bitcast_fusion), channel_id=2, replica_groups=mesh['batch'=8,'seq'=4] {'batch'}, dimensions={0}, use_global_device_ids=true | all-gather | bytes 144 | tf_op jit(solution)/shard_map/all_gather | solution.py:1025
  25.9 4.3 collective-permute-done.2.refs_3_
  30.2 15.9 %collective-permute-done.1.refs_2_ = bf16[160,1152]{1,0:T(8,128)(2,1)S(1)} collective-permute-done((bf16[160,1152]{1,0:T(8,128)(2,1)S(1)}, bf16[160,1152]{1,0:T(8,128)(2,1)S(1)}, u32[]{:S(2)}, u32[]{:S(2)}) %collective-permute-start.1) | collective-permute-done | bytes 368672 | tf_op jit(solution)/shard_map/ppermute | solution.py:846
  46.1 7.9 %collective-permute-done.refs_1_ = bf16[160,1152]{1,0:T(8,128)(2,1)S(1)} collective-permute-done((bf16[160,1152]{1,0:T(8,128)(2,1)S(1)}, bf16[160,1152]{1,0:T(8,128)(2,1)S(1)}, u32[]{:S(2)}, u32[]{:S(2)}) %collective-permute-start) | collective-permute-done | bytes 368672 | tf_op jit(solution)/shard_map/ppermute | solution.py:846
  61.7 5.1 collective-permute-start.11
  66.8 8.9 %collective-permute-done.12.refs_12_ = bf16[128,1152]{1,0:T(8,128)(2,1)S(1)} collective-permute-done((bf16[128,1152]{1,0:T(8,128)(2,1)S(1)}, bf16[128,1152]{1,0:T(8,128)(2,1)S(1)}, u32[]{:S(2)}, u32[]{:S(2)}) %collective-permute-start.12) | collective-permute-done | bytes 294944 | tf_op jit(solution)/shard_map/ppermute | solution.py:988
  79.5 9.8 %collective-permute-done.11.refs_11_ = bf16[128,1152]{1,0:T(8,128)(2,1)S(1)} collective-permute-done((bf16[128,1152]{1,0:T(8,128)(2,1)S(1)}, bf16[128,1152]{1,0:T(8,128)(2,1)S(1)}, u32[]{:S(2)}, u32[]{:S(2)}) %collective-permute-start.11) | collective-permute-done | bytes 294944 | tf_op jit(solution)/shard_map/ppermute | solution.py:988
  90.8 9.6 %collective-permute-done.10.refs_10_ = bf16[128,1152]{1,0:T(8,128)(2,1)S(1)} collective-permute-done((bf16[128,1152]{1,0:T(8,128)(2,1)S(1)}, bf16[128,1152]{1,0:T(8,128)(2,1)S(1)}, u32[]{:S(2)}, u32[]{:S(2)}) %collective-permute-start.10) | collective-permute-done | bytes 294944 | tf_op jit(solution)/shard_map/ppermute | solution.py:988
  103.0 2.6 add_convert_fusion.9.refs_0_
  105.7 16.4 %collective-permute-done.9.refs_9_ = bf16[128,1152]{1,0:T(8,128)(2,1)S(1)} collective-permute-done((bf16[128,1152]{1,0:T(8,128)(2,1)S(1)}, bf16[128,1152]{1,0:T(8,128)(2,1)S(1)}, u32[]{:S(2)}, u32[]{:S(2)}) %collective-permute-start.9) | collective-permute-done | bytes 294944 | tf_op jit(solution)/shard_map/ppermute | solution.py:988
  122.1 6.2 collective-permute-done.5.refs_4_
  139.6 8.1 %place.1 = (bf16[3456,1152]{1,0:T(8,128)(2,1)}, bf16[1152,1152]{1,0:T(8,128)(2,1)S(1)}) custom-call(s32[24]{0:T(128)S(1)} %stack.228.offset_ref, bf16[288,1152]{1,0:T(8,128)(2,1)S(1)} %copy-done.9, bf16[288,1152]{1,0:T(8,128)(2,1)S(1)} %collective-permute-done.17.refs_1_, bf16[288,1152]{1,0:T(8,128)(2,1)S(1)} %copy-done.16, ...), custom_call_target="tpu_custom_call" | custom-call | bytes 21233664 | tf_op jit(solution)/shard_map/place/pallas_call | solution.py:808
  153.7 4.6 fusion.2.refs_0_
  172.1 3.8 collective-permute-start.26
  178.7 4.8 convolution_convert_fusion.1.own_ref
  186.2 26.2 %attention_forward.1 = (bf16[528,1152]{1,0:T(8,128)(2,1)}, f32[16,512]{1,0:T(8,128)}, f32[16,128]{1,0:T(8,128)}) custom-call(s32[2]{0:T(128)} %stack.197.valid_ref, bf16[528,1152]{1,0:T(8,128)(2,1)} %convolution_convert_fusion.1.own_ref, bf16[528,2304]{1,0:T(8,128)(2,1)} %get-tuple-element.160.refs_0_, bf16[528,2304]{1,0:T(8,128)(2,1)} %collective-permute-done.21.refs_1_), custom_call_target="tpu_custom_call" | custom-call | flops 9663676416 | bytes 7299072 | tf_op jit(solution)/shard_map/attention_forward/pallas_call | solution.py:134
  212.4 9.7 %collective-permute-done.25.refs_4_ = bf16[128,1152]{1,0:T(8,128)(2,1)S(1)} collective-permute-done((bf16[128,1152]{1,0:T(8,128)(2,1)}, bf16[128,1152]{1,0:T(8,128)(2,1)S(1)}, u32[]{:S(2)}, u32[]{:S(2)}) %collective-permute-start.25) | collective-permute-done | bytes 294944 | tf_op jit(solution)/shard_map/ppermute | solution.py:988
  222.1 6.9 collective-permute-done.24.refs_3_
  230.2 4.1 fusion.86
  235.7 2.7 collective-permute-start.27
  244.9 56.9 %mlp.1 = (f32[528,1152]{1,0:T(8,128)}, bf16[528,1152]{1,0:T(8,128)(2,1)}, f32[528,1152]{1,0:T(8,128)}, bf16[528,1152]{1,0:T(8,128)(2,1)}, bf16[2304,1152]{1,0:T(...) custom-call(s32[16]{0:T(128)} %mul.395.first_ref, f32[1,2304]{1,0:T(1,128)} %reshape.464.bias_ref, ...), custom_call_target="tpu_custom_call" | custom-call | flops 33634123776 | bytes 40697856 | tf_op jit(solution)/shard_map/mlp/pallas_call | solution.py:338
  303.8 3.7 concatenate.97
  313.4 2.5 fusion.79
  315.9 3.0 convolution_convert_fusion.refs_3_
  318.9 43.8 %attention_backward.1 = (bf16[528,1152]{1,0:T(8,128)(2,1)}, bf16[528,2304]{1,0:T(8,128)(2,1)}, bf16[528,2304]{1,0:T(8,128)(2,1)}) custom-call(s32[2]{0:T(128)} %stack.197.valid_ref, bf16[528,1152]{1,0:T(8,128)(2,1)} %convolution_convert_fusion.1.own_ref, bf16[528,2304]{1,0:T(8,128)(2,1)} %get-tuple-element.160.refs_0_, ...), custom_call_target="tpu_custom_call" | custom-call | flops 21743271936 | bytes 14598144 | tf_op jit(solution)/shard_map/attention_backward/pallas_call | solution.py:239
  362.7 6.4 collective-permute-done.31.refs_4_
  370.0 3.1 add_convert_fusion.7
  373.1 3.1 add_convert_fusion.6
  382.1 5.0 qkv_grad.1
  394.4 14.5 %packed_grad.1 = (bf16[528,3456]{1,0:T(8,128)(2,1)}, bf16[4,432,1152]{2,1,0:T(8,128)(2,1)}, bf16[4,432,1152]{2,1,0:T(8,128)(2,1)}) custom-call(s32[8]{0:T(128)S(1)} %get-tuple-element.374.offset_ref, bf16[528,1152]{1,0:T(8,128)(2,1)S(1)} %copy-done.24, bf16[528,2304]{1,0:T(8,128)(2,1)} %get-tuple-element.190.own_ref, ...), custom_call_target="tpu_custom_call" | custom-call | flops 4204265472 | bytes 16478208 | tf_op jit(solution)/shard_map/packed_grad/pallas_call | solution.py:698
  412.4 2.6 add_convert_fusion.2
  415.0 2.6 add_convert_fusion.4
  419.2 4.3 add_convert_fusion
  432.6 12.5 %first_norm_back.1 = (bf16[528,1152]{1,0:T(8,128)(2,1)}, f32[16,1152]{1,0:T(8,128)}) custom-call(bf16[528,3456]{1,0:T(8,128)(2,1)} %together.27.packed_ref, bf16[3456,1152]{1,0:T(8,128)(2,1)} %get-tuple-element.158.weight_ref, f32[528,1152]{1,0:T(8,128)} %get-tuple-element.286.standard_ref, f32[528,1]{1,0:T(8,128)} %rsqrt.16.inverse_ref, ...), custom_call_target="tpu_custom_call" | custom-call | flops 4204265472 | bytes 17694720 | tf_op jit(solution)/shard_map/first_norm_back/pallas_call | solution.py:732
  447.8 13.5 %collective-permute-done.43.refs_9_ = bf16[160,1152]{1,0:T(8,128)(2,1)S(1)} collective-permute-done((bf16[160,1152]{1,0:T(8,128)(2,1)}, bf16[160,1152]{1,0:T(8,128)(2,1)S(1)}, u32[]{:S(2)}, u32[]{:S(2)}) %collective-permute-start.43) | collective-permute-done | bytes 368672 | tf_op jit(solution)/shard_map/ppermute | solution.py:852
  467.1 2.9 collective-permute-start.46
  476.0 3.2 add_convert_fusion.8.refs_5_
  479.2 5.9 collective-permute-done.44.refs_0_
  485.9 2.5 collective-permute-done.45.refs_1_
  488.4 15.5 %collective-permute-done.49.refs_5_ = bf16[288,1152]{1,0:T(8,128)(2,1)S(1)} collective-permute-done((bf16[288,1152]{1,0:T(8,128)(2,1)S(1)}, bf16[288,1152]{1,0:T(8,128)(2,1)S(1)}, u32[]{:S(2)}, u32[]{:S(2)}) %collective-permute-start.49) | collective-permute-done | bytes 663584 | tf_op jit(solution)/shard_map/ppermute | solution.py:846
  512.2 2.8 collective-permute-start.50
  515.6 2.4 collective-permute-start.52
  522.1 3.3 collective-permute-done.54
  526.0 10.4 %collective-permute-done.51.refs_2_ = bf16[144,1152]{1,0:T(8,128)(2,1)S(1)} collective-permute-done((bf16[144,1152]{1,0:T(8,128)(2,1)S(1)}, bf16[144,1152]{1,0:T(8,128)(2,1)S(1)}, u32[]{:S(2)}, u32[]{:S(2)}) %collective-permute-start.51) | collective-permute-done | bytes 331808 | tf_op jit(solution)/shard_map/ppermute | solution.py:846
  536.5 7.1 collective-permute-done.52.refs_3_
  553.4 4.9 collective-permute-done.55.refs_1_
  558.3 23.2 %collective-permute-done.56.refs_2_ = bf16[160,1152]{1,0:T(8,128)(2,1)S(1)} collective-permute-done((bf16[160,1152]{1,0:T(8,128)(2,1)S(1)}, bf16[160,1152]{1,0:T(8,128)(2,1)S(1)}, u32[]{:S(2)}, u32[]{:S(2)}) %collective-permute-start.56) | collective-permute-done | bytes 368672 | tf_op jit(solution)/shard_map/ppermute | solution.py:846
  587.5 4.8 gram.1
  599.8 2.9 collective-permute-done.59
  602.7 4.4 collective-permute-done.61
  612.9 5.4 collective-permute-done.63.refs_2_
  623.2 31.2 %first_steps.1 = (bf16[576,1152]{1,0:T(8,128)(2,1)}, bf16[4,400,256]{2,1,0:T(8,128)(2,1)}, bf16[4,400,256]{2,1,0:T(8,128)(2,1)}) custom-call(s32[8]{0:T(128)} %copy-done.25, bf16[576,1152]{1,0:T(8,128)(2,1)} %copy-done.21, bf16[400,256]{1,0:T(8,128)(2,1)} %copy-done.91, bf16[400,256]{1,0:T(8,128)(2,1)} %copy-done.106, bf16[400,256]{1,0:T(8,128)(2,1)} %copy-done.105, ...), custom_call_target="tpu_custom_call" | custom-call | flops 27518828544 | bytes 7962624 | tf_op jit(solution)/shard_map/first_steps/pallas_call | solution.py:559
  659.8 4.9 collective-permute-start.75
  672.1 4.9 collective-permute-done.70
  680.4 2.3 collective-permute-done.73.refs_3_
  682.7 4.9 collective-permute-start.76
  687.7 2.4 collective-permute-start.77
  693.8 18.3 %last_steps.1.refs_0_ = bf16[576,1152]{1,0:T(8,128)(2,1)} custom-call(s32[8]{0:T(128)} %copy-done.25, bf16[576,1152]{1,0:T(8,128)(2,1)} %get-tuple-element.252.slab_ref, bf16[400,256]{1,0:T(8,128)(2,1)} %copy-done.90, bf16[400,256]{1,0:T(8,128)(2,1)} %copy-done.103, bf16[400,256]{1,0:T(8,128)(2,1)} %copy-done.102, bf16[400,256]{1,0:T(8,128)(2,1)} %copy-done.101, ...), custom_call_target="tpu_custom_call" | custom-call | flops 15288238080 | bytes 5308416 | tf_op jit(solution)/shard_map/last_steps/pallas_call | solution.py:614
  712.2 2.4 collective-permute-done.76.refs_2_
  720.6 3.2 collective-permute-start.80
  726.1 4.2 collective-permute-done.81
  730.3 18.0 %collective-permute-done.80 = bf16[144,1152]{1,0:T(8,128)(2,1)S(1)} collective-permute-done((bf16[144,1152]{1,0:T(8,128)(2,1)S(1)}, bf16[144,1152]{1,0:T(8,128)(2,1)S(1)}, u32[]{:S(2)}, u32[]{:S(2)}) %collective-permute-start.80) | collective-permute-done | bytes 331808 | tf_op jit(solution)/shard_map/ppermute | solution.py:846
  748.3 4.4 collective-permute-done.79
  (636 shorter events, 188.8 us)
Async XLA Ops:
  7.3 237.6 %all-gather.4.cloned.1.call-start = ((), (), s32[]{:S(2)}) async-start(), calls=%async_computation | async-start | bytes 11280384 | tf_op jit(solution)/shard_map/all_gather | solution.py:1049
  20.1 10.1 %collective-permute-start.2 = (bf16[160,1152]{1,0:T(8,128)(2,1)S(1)}, bf16[160,1152]{1,0:T(8,128)(2,1)S(1)}, u32[]{:S(2)}, u32[]{:S(2)}) collective-permute-start(bf16[160,1152]{1,0:T(8,128)(2,1)S(1)} %fusion.35.refs_0_), channel_id=1, source_target_pairs={{0,3},{1,0},{2,1},{3,2},{4,7},{5,4},{6,5},{7,6},{8,11},{9,8},{10,9... | collective-permute-start | bytes 1105928 | tf_op jit(solution)/shard_map/ppermute | solution.py:846
  20.3 25.7 %collective-permute-start.1 = (bf16[160,1152]{1,0:T(8,128)(2,1)S(1)}, bf16[160,1152]{1,0:T(8,128)(2,1)S(1)}, u32[]{:S(2)}, u32[]{:S(2)}) collective-permute-start(bf16[160,1152]{1,0:T(8,128)(2,1)S(1)} %fusion.35.refs_0_), channel_id=1, source_target_pairs={{0,2},{1,3},{2,0},{3,1},{4,6},{5,7},{6,4},{7,5},{8,10},{9,11},{10,... | collective-permute-start | bytes 1105928 | tf_op jit(solution)/shard_map/ppermute | solution.py:846
  22.6 31.3 %collective-permute-start = (bf16[160,1152]{1,0:T(8,128)(2,1)S(1)}, bf16[160,1152]{1,0:T(8,128)(2,1)S(1)}, u32[]{:S(2)}, u32[]{:S(2)}) collective-permute-start(bf16[160,1152]{1,0:T(8,128)(2,1)S(1)} %fusion.35.refs_0_), channel_id=1, source_target_pairs={{0,1},{1,2},{2,3},{3,0},{4,5},{5,6},{6,7},{7,4},{8,9},{9,10},{10,1... | collective-permute-start | bytes 1105928 | tf_op jit(solution)/shard_map/ppermute | solution.py:846
  56.8 21.4 %collective-permute-start.7 = (bf16[320,1152]{1,0:T(8,128)(2,1)}, bf16[320,1152]{1,0:T(8,128)(2,1)S(1)}, u32[]{:S(2)}, u32[]{:S(2)}) collective-permute-start(bf16[320,1152]{1,0:T(8,128)(2,1)} %get-tuple-element.144.refs_5_), channel_id=1, source_target_pairs={{0,16},{4,20},{8,24},{12,28},{16,0},{20,4},{24,8},{28,12},{1,17},{... | collective-permute-start | bytes 2211848 | tf_op jit(solution)/shard_map/ppermute | solution.py:852
  58.1 32.4 %collective-permute-start.3 = (bf16[288,1152]{1,0:T(8,128)(2,1)}, bf16[288,1152]{1,0:T(8,128)(2,1)S(1)}, u32[]{:S(2)}, u32[]{:S(2)}) collective-permute-start(bf16[288,1152]{1,0:T(8,128)(2,1)} %get-tuple-element.143.refs_1_), channel_id=1, source_target_pairs={{0,8},{4,12},{8,0},{12,4},{16,24},{20,28},{24,16},{28,20},{1,9},{5... | collective-permute-start | bytes 1990664 | tf_op jit(solution)/shard_map/ppermute | solution.py:852
  59.8 15.9 %collective-permute-start.12 = (bf16[128,1152]{1,0:T(8,128)(2,1)S(1)}, bf16[128,1152]{1,0:T(8,128)(2,1)S(1)}, u32[]{:S(2)}, u32[]{:S(2)}) collective-permute-start(bf16[128,1152]{1,0:T(8,128)(2,1)S(1)} %get-tuple-element.332), channel_id=1, source_target_pairs={{0,5},{1,1},{2,4},{3,0},{4,7},{5,3},{6,6},{7,2},{8,13},{9,9},{10,1... | collective-permute-start | bytes 884744 | tf_op jit(solution)/shard_map/ppermute | solution.py:988
  61.7 27.5 %collective-permute-start.11 = (bf16[128,1152]{1,0:T(8,128)(2,1)S(1)}, bf16[128,1152]{1,0:T(8,128)(2,1)S(1)}, u32[]{:S(2)}, u32[]{:S(2)}) collective-permute-start(bf16[128,1152]{1,0:T(8,128)(2,1)S(1)} %get-tuple-element.333), channel_id=1, source_target_pairs={{0,1},{1,5},{2,0},{3,4},{4,3},{5,7},{6,2},{7,6},{8,9},{9,13},{10,8... | collective-permute-start | bytes 884744 | tf_op jit(solution)/shard_map/ppermute | solution.py:988
  66.8 33.6 %collective-permute-start.10 = (bf16[128,1152]{1,0:T(8,128)(2,1)S(1)}, bf16[128,1152]{1,0:T(8,128)(2,1)S(1)}, u32[]{:S(2)}, u32[]{:S(2)}) collective-permute-start(bf16[128,1152]{1,0:T(8,128)(2,1)S(1)} %get-tuple-element.334), channel_id=1, source_target_pairs={{0,4},{1,0},{2,5},{3,1},{4,6},{5,2},{6,7},{7,3},{8,12},{9,8},{10,1... | collective-permute-start | bytes 884744 | tf_op jit(solution)/shard_map/ppermute | solution.py:988
  75.7 46.4 %collective-permute-start.6 = (bf16[320,1152]{1,0:T(8,128)(2,1)S(1)}, bf16[320,1152]{1,0:T(8,128)(2,1)S(1)}, u32[]{:S(2)}, u32[]{:S(2)}) collective-permute-start(bf16[320,1152]{1,0:T(8,128)(2,1)S(1)} %copy-done.5), channel_id=1, source_target_pairs={{0,8},{4,12},{8,0},{12,4},{16,24},{20,28},{24,16},{28,20},{1,9},{5... | collective-permute-start | bytes 2211848 | tf_op jit(solution)/shard_map/ppermute | solution.py:852
  78.2 50.9 %collective-permute-start.8 = (bf16[320,1152]{1,0:T(8,128)(2,1)S(1)}, bf16[320,1152]{1,0:T(8,128)(2,1)}, u32[]{:S(2)}, u32[]{:S(2)}) collective-permute-start(bf16[320,1152]{1,0:T(8,128)(2,1)S(1)} %collective-permute-done.7.refs_7_), channel_id=1, source_target_pairs={{0,8},{4,12},{8,0},{12,4},{16,24},{20,28},{24,16},{28,20},{1,9},{5... | collective-permute-start | bytes 2211848 | tf_op jit(solution)/shard_map/ppermute | solution.py:852
  89.2 32.8 %collective-permute-start.4 = (bf16[288,1152]{1,0:T(8,128)(2,1)S(1)}, bf16[288,1152]{1,0:T(8,128)(2,1)S(1)}, u32[]{:S(2)}, u32[]{:S(2)}) collective-permute-start(bf16[288,1152]{1,0:T(8,128)(2,1)S(1)} %copy-done.8), channel_id=1, source_target_pairs={{0,16},{4,20},{8,24},{12,28},{16,0},{20,4},{24,8},{28,12},{1,17},{... | collective-permute-start | bytes 1990664 | tf_op jit(solution)/shard_map/ppermute | solution.py:852
  90.5 37.8 %collective-permute-start.5 = (bf16[288,1152]{1,0:T(8,128)(2,1)S(1)}, bf16[288,1152]{1,0:T(8,128)(2,1)S(1)}, u32[]{:S(2)}, u32[]{:S(2)}) collective-permute-start(bf16[288,1152]{1,0:T(8,128)(2,1)S(1)} %collective-permute-done.3.refs_2_), channel_id=1, source_target_pairs={{0,16},{4,20},{8,24},{12,28},{16,0},{20,4},{24,8},{28,12},{1,17},{... | collective-permute-start | bytes 1990664 | tf_op jit(solution)/shard_map/ppermute | solution.py:852
  101.1 20.9 %collective-permute-start.9 = (bf16[128,1152]{1,0:T(8,128)(2,1)S(1)}, bf16[128,1152]{1,0:T(8,128)(2,1)S(1)}, u32[]{:S(2)}, u32[]{:S(2)}) collective-permute-start(bf16[128,1152]{1,0:T(8,128)(2,1)S(1)} %get-tuple-element.335), channel_id=1, source_target_pairs={{0,0},{1,4},{2,1},{3,5},{4,2},{5,6},{6,3},{7,7},{8,8},{9,12},{10,9... | collective-permute-start | bytes 884744 | tf_op jit(solution)/shard_map/ppermute | solution.py:988
  158.3 25.3 %collective-permute-start.21 = (bf16[528,2304]{1,0:T(8,128)(2,1)}, bf16[528,2304]{1,0:T(8,128)(2,1)}, u32[]{:S(2)}, u32[]{:S(2)}) collective-permute-start(bf16[528,2304]{1,0:T(8,128)(2,1)} %get-tuple-element.160.refs_0_), channel_id=1, source_target_pairs={{4,0},{5,1},{6,2},{7,3},{0,4},{1,5},{2,6},{3,7},{12,8},{13,9},{14,... | collective-permute-start | bytes 7299080 | tf_op jit(solution)/shard_map/ppermute | solution.py:1129
  159.0 53.4 %collective-permute-start.22 = (bf16[2,2,1152]{2,1,0:T(2,128)(2,1)S(1)}, bf16[2,2,1152]{2,1,0:T(2,128)(2,1)S(1)}, u32[]{:S(2)}, u32[]{:S(2)}) collective-permute-start(bf16[2,2,1152]{2,1,0:T(2,128)(2,1)S(1)} %add_convert_fusion.16), channel_id=1, source_target_pairs={{0,4},{4,0},{8,12},{12,8},{16,20},{20,16},{24,28},{28,24},{1,5},{5... | collective-permute-start | bytes 27656 | tf_op jit(solution)/shard_map/ppermute | solution.py:852
  172.1 40.2 %collective-permute-start.26 = (bf16[128,1152]{1,0:T(8,128)(2,1)}, bf16[128,1152]{1,0:T(8,128)(2,1)S(1)}, u32[]{:S(2)}, u32[]{:S(2)}) collective-permute-start(bf16[128,1152]{1,0:T(8,128)(2,1)} %get-tuple-element.328), channel_id=1, source_target_pairs={{0,5},{1,1},{2,4},{3,0},{4,7},{5,3},{6,6},{7,2},{8,13},{9,9},{10,1... | collective-permute-start | bytes 884744 | tf_op jit(solution)/shard_map/ppermute | solution.py:988
  176.0 46.1 %collective-permute-start.25 = (bf16[128,1152]{1,0:T(8,128)(2,1)}, bf16[128,1152]{1,0:T(8,128)(2,1)S(1)}, u32[]{:S(2)}, u32[]{:S(2)}) collective-permute-start(bf16[128,1152]{1,0:T(8,128)(2,1)} %get-tuple-element.329), channel_id=1, source_target_pairs={{0,1},{1,5},{2,0},{3,4},{4,3},{5,7},{6,2},{7,6},{8,9},{9,13},{10,8... | collective-permute-start | bytes 884744 | tf_op jit(solution)/shard_map/ppermute | solution.py:988
  177.6 51.5 %collective-permute-start.24 = (bf16[128,1152]{1,0:T(8,128)(2,1)}, bf16[128,1152]{1,0:T(8,128)(2,1)}, u32[]{:S(2)}, u32[]{:S(2)}) collective-permute-start(bf16[128,1152]{1,0:T(8,128)(2,1)} %get-tuple-element.330), channel_id=1, source_target_pairs={{0,4},{1,0},{2,5},{3,1},{4,6},{5,2},{6,7},{7,3},{8,12},{9,8},{10,1... | collective-permute-start | bytes 884744 | tf_op jit(solution)/shard_map/ppermute | solution.py:988
  183.6 46.6 %collective-permute-start.23 = (bf16[128,1152]{1,0:T(8,128)(2,1)S(1)}, bf16[128,1152]{1,0:T(8,128)(2,1)}, u32[]{:S(2)}, u32[]{:S(2)}) collective-permute-start(bf16[128,1152]{1,0:T(8,128)(2,1)S(1)} %get-tuple-element.331), channel_id=1, source_target_pairs={{0,0},{1,4},{2,1},{3,5},{4,2},{5,6},{6,3},{7,7},{8,8},{9,12},{10,9... | collective-permute-start | bytes 884744 | tf_op jit(solution)/shard_map/ppermute | solution.py:988
  235.7 9.2 %collective-permute-start.27 = (bf16[528,1152]{1,0:T(8,128)(2,1)S(1)}, bf16[528,1152]{1,0:T(8,128)(2,1)}, u32[]{:S(2)}, u32[]{:S(2)}) collective-permute-start(bf16[528,1152]{1,0:T(8,128)(2,1)S(1)} %multiply_convert_fusion.n_own), channel_id=1, source_target_pairs={{0,4},{4,0},{8,12},{12,8},{16,20},{20,16},{24,28},{28,24},{1,5},{5... | collective-permute-start | bytes 3649544 | tf_op jit(solution)/shard_map/ppermute | solution.py:852
  303.3 8.8 %collective-permute-start.29 = (bf16[528,1152]{1,0:T(8,128)(2,1)}, bf16[528,1152]{1,0:T(8,128)(2,1)S(1)}, u32[]{:S(2)}, u32[]{:S(2)}) collective-permute-start(bf16[528,1152]{1,0:T(8,128)(2,1)} %get-tuple-element.172), channel_id=1, source_target_pairs={{0,4},{4,0},{8,12},{12,8},{16,20},{20,16},{24,28},{28,24},{1,5},{5... | collective-permute-start | bytes 3649544 | tf_op jit(solution)/shard_map/ppermute | solution.py:852
  303.4 59.3 %collective-permute-start.32 = (bf16[528,1152]{1,0:T(8,128)(2,1)}, bf16[528,1152]{1,0:T(8,128)(2,1)S(1)}, u32[]{:S(2)}, u32[]{:S(2)}) collective-permute-start(bf16[528,1152]{1,0:T(8,128)(2,1)} %get-tuple-element.180), channel_id=1, source_target_pairs={{0,4},{4,0},{8,12},{12,8},{16,20},{20,16},{24,28},{28,24},{1,5},{5... | collective-permute-start | bytes 3649544 | tf_op jit(solution)/shard_map/ppermute | solution.py:852
  309.7 59.4 %collective-permute-start.31 = (bf16[1152,1152]{1,0:T(8,128)(2,1)}, bf16[1152,1152]{1,0:T(8,128)(2,1)}, u32[]{:S(2)}, u32[]{:S(2)}) collective-permute-start(bf16[1152,1152]{1,0:T(8,128)(2,1)} %pad_maximum_fusion), channel_id=1, source_target_pairs={{0,8},{4,12},{8,0},{12,4},{16,24},{20,28},{24,16},{28,20},{1,9},{5... | collective-permute-start | bytes 7962632 | tf_op jit(solution)/shard_map/ppermute | solution.py:852
  310.9 59.1 %collective-permute-start.30 = (bf16[1152,1152]{1,0:T(8,128)(2,1)}, bf16[1152,1152]{1,0:T(8,128)(2,1)}, u32[]{:S(2)}, u32[]{:S(2)}) collective-permute-start(bf16[1152,1152]{1,0:T(8,128)(2,1)} %concatenate.97), channel_id=1, source_target_pairs={{0,16},{4,20},{8,24},{12,28},{16,0},{20,4},{24,8},{28,12},{1,17},{... | collective-permute-start | bytes 7962632 | tf_op jit(solution)/shard_map/ppermute | solution.py:852
  376.3 32.7 %collective-permute-start.36 = (bf16[576,1152]{1,0:T(8,128)(2,1)}, bf16[576,1152]{1,0:T(8,128)(2,1)}, u32[]{:S(2)}, u32[]{:S(2)}) collective-permute-start(bf16[576,1152]{1,0:T(8,128)(2,1)} %add_convert_fusion.6), channel_id=1, source_target_pairs={{0,16},{4,20},{8,24},{12,28},{16,0},{20,4},{24,8},{28,12},{1,17},{... | collective-permute-start | bytes 3981320 | tf_op jit(solution)/shard_map/ppermute | solution.py:852
  377.5 31.5 %collective-permute-start.35 = (bf16[576,1152]{1,0:T(8,128)(2,1)}, bf16[576,1152]{1,0:T(8,128)(2,1)}, u32[]{:S(2)}, u32[]{:S(2)}) collective-permute-start(bf16[576,1152]{1,0:T(8,128)(2,1)} %add_convert_fusion.7), channel_id=1, source_target_pairs={{0,8},{4,12},{8,0},{12,4},{16,24},{20,28},{24,16},{28,20},{1,9},{5... | collective-permute-start | bytes 3981320 | tf_op jit(solution)/shard_map/ppermute | solution.py:852
  377.8 10.3 %collective-permute-start.33 = (bf16[528,2304]{1,0:T(8,128)(2,1)}, bf16[528,2304]{1,0:T(8,128)(2,1)}, u32[]{:S(2)}, u32[]{:S(2)}) collective-permute-start(bf16[528,2304]{1,0:T(8,128)(2,1)} %get-tuple-element.189), channel_id=1, source_target_pairs={{0,4},{1,5},{2,6},{3,7},{4,0},{5,1},{6,2},{7,3},{8,12},{9,13},{10,... | collective-permute-start | bytes 7299080 | tf_op jit(solution)/shard_map/ppermute | solution.py:1129
  388.2 20.8 %collective-permute-start.34 = (bf16[4,144,1152]{2,1,0:T(8,128)(2,1)}, bf16[4,144,1152]{2,1,0:T(8,128)(2,1)}, u32[]{:S(2)}, u32[]{:S(2)}) collective-permute-start(bf16[4,144,1152]{2,1,0:T(8,128)(2,1)} %get-tuple-element.196), channel_id=1, source_target_pairs={{0,4},{4,0},{8,12},{12,8},{16,20},{20,16},{24,28},{28,24},{1,5},{5... | collective-permute-start | bytes 3981320 | tf_op jit(solution)/shard_map/ppermute | solution.py:852
  409.0 10.2 %collective-permute-start.37 = (bf16[4,432,1152]{2,1,0:T(8,128)(2,1)}, bf16[4,432,1152]{2,1,0:T(8,128)(2,1)}, u32[]{:S(2)}, u32[]{:S(2)}) collective-permute-start(bf16[4,432,1152]{2,1,0:T(8,128)(2,1)} %get-tuple-element.200), channel_id=1, source_target_pairs={{0,4},{4,0},{8,12},{12,8},{16,20},{20,16},{24,28},{28,24},{1,5},{5... | collective-permute-start | bytes 11943944 | tf_op jit(solution)/shard_map/ppermute | solution.py:852
  412.1 19.9 %collective-permute-start.42 = (bf16[128,1152]{1,0:T(8,128)(2,1)}, bf16[128,1152]{1,0:T(8,128)(2,1)}, u32[]{:S(2)}, u32[]{:S(2)}) collective-permute-start(bf16[128,1152]{1,0:T(8,128)(2,1)} %pad_maximum_fusion.27), channel_id=1, source_target_pairs={{0,16},{4,20},{8,24},{12,28},{16,0},{20,4},{24,8},{28,12},{1,17},{... | collective-permute-start | bytes 884744 | tf_op jit(solution)/shard_map/ppermute | solution.py:852
  425.4 35.9 %collective-permute-start.40 = (bf16[288,1152]{1,0:T(8,128)(2,1)}, bf16[288,1152]{1,0:T(8,128)(2,1)}, u32[]{:S(2)}, u32[]{:S(2)}) collective-permute-start(bf16[288,1152]{1,0:T(8,128)(2,1)} %get-tuple-element.211), channel_id=1, source_target_pairs={{0,3},{1,0},{2,1},{3,2},{4,7},{5,4},{6,5},{7,6},{8,11},{9,8},{10,9... | collective-permute-start | bytes 1990664 | tf_op jit(solution)/shard_map/ppermute | solution.py:846
  425.4 35.9 %collective-permute-start.41 = (bf16[288,1152]{1,0:T(8,128)(2,1)}, bf16[288,1152]{1,0:T(8,128)(2,1)}, u32[]{:S(2)}, u32[]{:S(2)}) collective-permute-start(bf16[288,1152]{1,0:T(8,128)(2,1)} %get-tuple-element.212), channel_id=1, source_target_pairs={{0,1},{1,2},{2,3},{3,0},{4,5},{5,6},{6,7},{7,4},{8,9},{9,10},{10,1... | collective-permute-start | bytes 1990664 | tf_op jit(solution)/shard_map/ppermute | solution.py:846
  428.1 33.3 %collective-permute-start.38 = (bf16[416,1152]{1,0:T(8,128)(2,1)}, bf16[416,1152]{1,0:T(8,128)(2,1)S(1)}, u32[]{:S(2)}, u32[]{:S(2)}) collective-permute-start(bf16[416,1152]{1,0:T(8,128)(2,1)} %pad_maximum_fusion.11), channel_id=1, source_target_pairs={{0,16},{4,20},{8,24},{12,28},{16,0},{20,4},{24,8},{28,12},{1,17},{... | collective-permute-start | bytes 2875400 | tf_op jit(solution)/shard_map/ppermute | solution.py:852
  430.3 31.1 %collective-permute-start.39 = (bf16[448,1152]{1,0:T(8,128)(2,1)}, bf16[448,1152]{1,0:T(8,128)(2,1)S(1)}, u32[]{:S(2)}, u32[]{:S(2)}) collective-permute-start(bf16[448,1152]{1,0:T(8,128)(2,1)} %pad_maximum_fusion.9), channel_id=1, source_target_pairs={{0,8},{4,12},{8,0},{12,4},{16,24},{20,28},{24,16},{28,20},{1,9},{5... | collective-permute-start | bytes 3096584 | tf_op jit(solution)/shard_map/ppermute | solution.py:852
  432.1 29.3 %collective-permute-start.43 = (bf16[160,1152]{1,0:T(8,128)(2,1)}, bf16[160,1152]{1,0:T(8,128)(2,1)S(1)}, u32[]{:S(2)}, u32[]{:S(2)}) collective-permute-start(bf16[160,1152]{1,0:T(8,128)(2,1)} %pad_maximum_fusion.17), channel_id=1, source_target_pairs={{0,8},{4,12},{8,0},{12,4},{16,24},{20,28},{24,16},{28,20},{1,9},{5... | collective-permute-start | bytes 1105928 | tf_op jit(solution)/shard_map/ppermute | solution.py:852
  465.2 14.0 %collective-permute-start.47 = (bf16[64,1152]{1,0:T(8,128)(2,1)}, bf16[64,1152]{1,0:T(8,128)(2,1)}, u32[]{:S(2)}, u32[]{:S(2)}) collective-permute-start(bf16[64,1152]{1,0:T(8,128)(2,1)} %fusion.42), channel_id=1, source_target_pairs={{0,8},{4,12},{8,0},{12,4},{16,24},{20,28},{24,16},{28,20},{1,9},{5... | collective-permute-start | bytes 442376 | tf_op jit(solution)/shard_map/ppermute | solution.py:852
  467.1 8.8 %collective-permute-start.46 = (f32[26,1152]{1,0:T(8,128)S(1)}, f32[26,1152]{1,0:T(8,128)S(1)}, u32[]{:S(2)}, u32[]{:S(2)}) collective-permute-start(f32[26,1152]{1,0:T(8,128)S(1)} %concatenate.104), channel_id=1, source_target_pairs={{0,4},{4,0},{8,12},{12,8},{16,20},{20,16},{24,28},{28,24},{1,5},{5... | collective-permute-start | bytes 359432 | tf_op jit(solution)/shard_map/ppermute | solution.py:852
  472.7 12.4 %collective-permute-start.44 = (bf16[208,1152]{1,0:T(8,128)(2,1)S(1)}, bf16[208,1152]{1,0:T(8,128)(2,1)S(1)}, u32[]{:S(2)}, u32[]{:S(2)}) collective-permute-start(bf16[208,1152]{1,0:T(8,128)(2,1)S(1)} %fusion.11), channel_id=1, source_target_pairs={{0,8},{4,12},{8,0},{12,4},{16,24},{20,28},{24,16},{28,20},{1,9},{5... | collective-permute-start | bytes 1437704 | tf_op jit(solution)/shard_map/ppermute | solution.py:852
  474.6 13.7 %collective-permute-start.45 = (bf16[224,1152]{1,0:T(8,128)(2,1)S(1)}, bf16[224,1152]{1,0:T(8,128)(2,1)}, u32[]{:S(2)}, u32[]{:S(2)}) collective-permute-start(bf16[224,1152]{1,0:T(8,128)(2,1)S(1)} %fusion.10), channel_id=1, source_target_pairs={{0,16},{4,20},{8,24},{12,28},{16,0},{20,4},{24,8},{28,12},{1,17},{... | collective-permute-start | bytes 1548296 | tf_op jit(solution)/shard_map/ppermute | solution.py:852
  475.9 28.0 %collective-permute-start.49 = (bf16[288,1152]{1,0:T(8,128)(2,1)S(1)}, bf16[288,1152]{1,0:T(8,128)(2,1)S(1)}, u32[]{:S(2)}, u32[]{:S(2)}) collective-permute-start(bf16[288,1152]{1,0:T(8,128)(2,1)S(1)} %copy-done.39), channel_id=1, source_target_pairs={{0,2},{1,3},{2,0},{3,1},{4,6},{5,7},{6,4},{7,5},{8,10},{9,11},{10,... | collective-permute-start | bytes 1990664 | tf_op jit(solution)/shard_map/ppermute | solution.py:846
  511.2 9.8 %collective-permute-start.53 = (f32[26,1152]{1,0:T(8,128)S(1)}, f32[26,1152]{1,0:T(8,128)S(1)}, u32[]{:S(2)}, u32[]{:S(2)}) collective-permute-start(f32[26,1152]{1,0:T(8,128)S(1)} %add.670), channel_id=1, source_target_pairs={{0,8},{4,12},{8,0},{12,4},{16,24},{20,28},{24,16},{28,20},{1,9},{5... | collective-permute-start | bytes 359432 | tf_op jit(solution)/shard_map/ppermute | solution.py:852
  512.2 13.8 %collective-permute-start.50 = (bf16[144,1152]{1,0:T(8,128)(2,1)S(1)}, bf16[144,1152]{1,0:T(8,128)(2,1)S(1)}, u32[]{:S(2)}, u32[]{:S(2)}) collective-permute-start(bf16[144,1152]{1,0:T(8,128)(2,1)S(1)} %pad_maximum_fusion.24), channel_id=1, source_target_pairs={{0,3},{1,0},{2,1},{3,2},{4,7},{5,4},{6,5},{7,6},{8,11},{9,8},{10,9... | collective-permute-start | bytes 995336 | tf_op jit(solution)/shard_map/ppermute | solution.py:846
  515.1 21.3 %collective-permute-start.51 = (bf16[144,1152]{1,0:T(8,128)(2,1)S(1)}, bf16[144,1152]{1,0:T(8,128)(2,1)S(1)}, u32[]{:S(2)}, u32[]{:S(2)}) collective-permute-start(bf16[144,1152]{1,0:T(8,128)(2,1)S(1)} %pad_maximum_fusion.25), channel_id=1, source_target_pairs={{0,2},{1,3},{2,0},{3,1},{4,6},{5,7},{6,4},{7,5},{8,10},{9,11},{10,... | collective-permute-start | bytes 995336 | tf_op jit(solution)/shard_map/ppermute | solution.py:846
  515.6 28.0 %collective-permute-start.52 = (bf16[144,1152]{1,0:T(8,128)(2,1)S(1)}, bf16[144,1152]{1,0:T(8,128)(2,1)S(1)}, u32[]{:S(2)}, u32[]{:S(2)}) collective-permute-start(bf16[144,1152]{1,0:T(8,128)(2,1)S(1)} %pad_maximum_fusion.26), channel_id=1, source_target_pairs={{0,1},{1,2},{2,3},{3,0},{4,5},{5,6},{6,7},{7,4},{8,9},{9,10},{10,1... | collective-permute-start | bytes 995336 | tf_op jit(solution)/shard_map/ppermute | solution.py:846
  549.0 9.3 %collective-permute-start.55 = (bf16[160,1152]{1,0:T(8,128)(2,1)S(1)}, bf16[160,1152]{1,0:T(8,128)(2,1)S(1)}, u32[]{:S(2)}, u32[]{:S(2)}) collective-permute-start(bf16[160,1152]{1,0:T(8,128)(2,1)S(1)} %pad_maximum_fusion.19), channel_id=1, source_target_pairs={{0,1},{1,2},{2,3},{3,0},{4,5},{5,6},{6,7},{7,4},{8,9},{9,10},{10,1... | collective-permute-start | bytes 1105928 | tf_op jit(solution)/shard_map/ppermute | solution.py:846
  551.3 30.2 %collective-permute-start.56 = (bf16[160,1152]{1,0:T(8,128)(2,1)S(1)}, bf16[160,1152]{1,0:T(8,128)(2,1)S(1)}, u32[]{:S(2)}, u32[]{:S(2)}) collective-permute-start(bf16[160,1152]{1,0:T(8,128)(2,1)S(1)} %pad_maximum_fusion.20), channel_id=1, source_target_pairs={{0,2},{1,3},{2,0},{3,1},{4,6},{5,7},{6,4},{7,5},{8,10},{9,11},{10,... | collective-permute-start | bytes 1105928 | tf_op jit(solution)/shard_map/ppermute | solution.py:846
  551.4 32.1 %collective-permute-start.57 = (bf16[160,1152]{1,0:T(8,128)(2,1)S(1)}, bf16[160,1152]{1,0:T(8,128)(2,1)S(1)}, u32[]{:S(2)}, u32[]{:S(2)}) collective-permute-start(bf16[160,1152]{1,0:T(8,128)(2,1)S(1)} %pad_maximum_fusion.21), channel_id=1, source_target_pairs={{0,3},{1,0},{2,1},{3,2},{4,7},{5,4},{6,5},{7,6},{8,11},{9,8},{10,9... | collective-permute-start | bytes 1105928 | tf_op jit(solution)/shard_map/ppermute | solution.py:846
  596.9 10.2 %collective-permute-start.61 = (bf16[400,256]{1,0:T(8,128)(2,1)S(1)}, bf16[400,256]{1,0:T(8,128)(2,1)S(1)}, u32[]{:S(2)}, u32[]{:S(2)}) collective-permute-start(bf16[400,256]{1,0:T(8,128)(2,1)S(1)} %get-tuple-element.346), channel_id=1, source_target_pairs={{0,24},{4,28},{8,16},{12,20},{16,8},{20,12},{24,0},{28,4},{1,25},{... | collective-permute-start | bytes 614408 | tf_op jit(solution)/shard_map/ppermute | solution.py:852
  597.9 9.3 %collective-permute-start.60 = (bf16[400,256]{1,0:T(8,128)(2,1)S(1)}, bf16[400,256]{1,0:T(8,128)(2,1)S(1)}, u32[]{:S(2)}, u32[]{:S(2)}) collective-permute-start(bf16[400,256]{1,0:T(8,128)(2,1)S(1)} %get-tuple-element.347), channel_id=1, source_target_pairs={{0,16},{4,20},{8,24},{12,28},{16,0},{20,4},{24,8},{28,12},{1,17},{... | collective-permute-start | bytes 614408 | tf_op jit(solution)/shard_map/ppermute | solution.py:852
  608.7 9.6 %collective-permute-start.63 = (bf16[400,256]{1,0:T(8,128)(2,1)S(1)}, bf16[400,256]{1,0:T(8,128)(2,1)S(1)}, u32[]{:S(2)}, u32[]{:S(2)}) collective-permute-start(bf16[400,256]{1,0:T(8,128)(2,1)S(1)} %fusion.34.refs_0_), channel_id=1, source_target_pairs={{0,16},{4,20},{8,24},{12,28},{16,0},{20,4},{24,8},{28,12},{1,17},{... | collective-permute-start | bytes 614408 | tf_op jit(solution)/shard_map/ppermute | solution.py:852
  609.0 9.3 %collective-permute-start.62 = (bf16[400,256]{1,0:T(8,128)(2,1)S(1)}, bf16[400,256]{1,0:T(8,128)(2,1)S(1)}, u32[]{:S(2)}, u32[]{:S(2)}) collective-permute-start(bf16[400,256]{1,0:T(8,128)(2,1)S(1)} %fusion.34.refs_0_), channel_id=1, source_target_pairs={{0,8},{4,12},{8,0},{12,4},{16,24},{20,28},{24,16},{28,20},{1,9},{5... | collective-permute-start | bytes 614408 | tf_op jit(solution)/shard_map/ppermute | solution.py:852
  621.3 33.2 %collective-permute-start.66 = (bf16[4,1,1152]{2,1,0:T(2,128)(2,1)S(1)}, bf16[4,1,1152]{2,1,0:T(2,128)(2,1)S(1)}, u32[]{:S(2)}, u32[]{:S(2)}) collective-permute-start(bf16[4,1,1152]{2,1,0:T(2,128)(2,1)S(1)} %pad_maximum_fusion.28), channel_id=1, source_target_pairs={{0,4},{4,0},{8,12},{12,8},{16,20},{20,16},{24,28},{28,24},{1,5},{5... | collective-permute-start | bytes 27656 | tf_op jit(solution)/shard_map/ppermute | solution.py:852
  655.1 9.7 %collective-permute-start.67 = (bf16[4,400,256]{2,1,0:T(8,128)(2,1)}, bf16[4,400,256]{2,1,0:T(8,128)(2,1)}, u32[]{:S(2)}, u32[]{:S(2)}) collective-permute-start(bf16[4,400,256]{2,1,0:T(8,128)(2,1)} %get-tuple-element.254), channel_id=1, source_target_pairs={{0,4},{4,0},{8,12},{12,8},{16,20},{20,16},{24,28},{28,24},{1,5},{5... | collective-permute-start | bytes 2457608 | tf_op jit(solution)/shard_map/ppermute | solution.py:852
  657.9 54.2 %collective-permute-start.78 = (bf16[2,128,1152]{2,1,0:T(8,128)(2,1)}, bf16[2,128,1152]{2,1,0:T(8,128)(2,1)S(1)}, u32[]{:S(2)}, u32[]{:S(2)}) collective-permute-start(bf16[2,128,1152]{2,1,0:T(8,128)(2,1)} %get-tuple-element.297), channel_id=1, source_target_pairs={{5,0},{1,1},{4,2},{0,3},{7,4},{3,5},{6,6},{2,7},{13,8},{9,9},{12,1... | collective-permute-start | bytes 1769480 | tf_op jit(solution)/shard_map/ppermute | solution.py:999
  659.8 52.3 %collective-permute-start.75 = (bf16[2,128,1152]{2,1,0:T(8,128)(2,1)}, bf16[2,128,1152]{2,1,0:T(8,128)(2,1)S(1)}, u32[]{:S(2)}, u32[]{:S(2)}) collective-permute-start(bf16[2,128,1152]{2,1,0:T(8,128)(2,1)} %get-tuple-element.298), channel_id=1, source_target_pairs={{0,0},{4,1},{1,2},{5,3},{2,4},{6,5},{3,6},{7,7},{8,8},{12,9},{9,10... | collective-permute-start | bytes 1769480 | tf_op jit(solution)/shard_map/ppermute | solution.py:999
  666.9 10.0 %collective-permute-start.70 = (bf16[400,256]{1,0:T(8,128)(2,1)S(1)}, bf16[400,256]{1,0:T(8,128)(2,1)S(1)}, u32[]{:S(2)}, u32[]{:S(2)}) collective-permute-start(bf16[400,256]{1,0:T(8,128)(2,1)S(1)} %get-tuple-element.343), channel_id=1, source_target_pairs={{0,24},{4,28},{8,16},{12,20},{16,8},{20,12},{24,0},{28,4},{1,25},{... | collective-permute-start | bytes 614408 | tf_op jit(solution)/shard_map/ppermute | solution.py:852
  678.1 9.6 %collective-permute-start.72 = (bf16[400,256]{1,0:T(8,128)(2,1)S(1)}, bf16[400,256]{1,0:T(8,128)(2,1)S(1)}, u32[]{:S(2)}, u32[]{:S(2)}) collective-permute-start(bf16[400,256]{1,0:T(8,128)(2,1)S(1)} %fusion.31.refs_0_), channel_id=1, source_target_pairs={{0,16},{4,20},{8,24},{12,28},{16,0},{20,4},{24,8},{28,12},{1,17},{... | collective-permute-start | bytes 614408 | tf_op jit(solution)/shard_map/ppermute | solution.py:852
  679.3 10.8 %collective-permute-start.71 = (bf16[400,256]{1,0:T(8,128)(2,1)S(1)}, bf16[400,256]{1,0:T(8,128)(2,1)S(1)}, u32[]{:S(2)}, u32[]{:S(2)}) collective-permute-start(bf16[400,256]{1,0:T(8,128)(2,1)S(1)} %fusion.31.refs_0_), channel_id=1, source_target_pairs={{0,8},{4,12},{8,0},{12,4},{16,24},{20,28},{24,16},{28,20},{1,9},{5... | collective-permute-start | bytes 614408 | tf_op jit(solution)/shard_map/ppermute | solution.py:852
  682.7 31.8 %collective-permute-start.76 = (bf16[2,128,1152]{2,1,0:T(8,128)(2,1)}, bf16[2,128,1152]{2,1,0:T(8,128)(2,1)S(1)}, u32[]{:S(2)}, u32[]{:S(2)}) collective-permute-start(bf16[2,128,1152]{2,1,0:T(8,128)(2,1)} %get-tuple-element.299), channel_id=1, source_target_pairs={{4,0},{0,1},{5,2},{1,3},{6,4},{2,5},{7,6},{3,7},{12,8},{8,9},{13,1... | collective-permute-start | bytes 1769480 | tf_op jit(solution)/shard_map/ppermute | solution.py:999
  687.7 26.8 %collective-permute-start.77 = (bf16[2,128,1152]{2,1,0:T(8,128)(2,1)S(1)}, bf16[2,128,1152]{2,1,0:T(8,128)(2,1)S(1)}, u32[]{:S(2)}, u32[]{:S(2)}) collective-permute-start(bf16[2,128,1152]{2,1,0:T(8,128)(2,1)S(1)} %get-tuple-element.300), channel_id=1, source_target_pairs={{1,0},{5,1},{0,2},{4,3},{3,4},{7,5},{2,6},{6,7},{9,8},{13,9},{8,10... | collective-permute-start | bytes 1769480 | tf_op jit(solution)/shard_map/ppermute | solution.py:999
  720.5 9.8 %collective-permute-start.81 = (bf16[144,1152]{1,0:T(8,128)(2,1)S(1)}, bf16[144,1152]{1,0:T(8,128)(2,1)S(1)}, u32[]{:S(2)}, u32[]{:S(2)}) collective-permute-start(bf16[144,1152]{1,0:T(8,128)(2,1)S(1)} %get-tuple-element.306), channel_id=1, source_target_pairs={{0,1},{1,2},{2,3},{3,0},{4,5},{5,6},{6,7},{7,4},{8,9},{9,10},{10,1... | collective-permute-start | bytes 995336 | tf_op jit(solution)/shard_map/ppermute | solution.py:846
  720.6 27.7 %collective-permute-start.80 = (bf16[144,1152]{1,0:T(8,128)(2,1)S(1)}, bf16[144,1152]{1,0:T(8,128)(2,1)S(1)}, u32[]{:S(2)}, u32[]{:S(2)}) collective-permute-start(bf16[144,1152]{1,0:T(8,128)(2,1)S(1)} %get-tuple-element.307), channel_id=1, source_target_pairs={{0,2},{1,3},{2,0},{3,1},{4,6},{5,7},{6,4},{7,5},{8,10},{9,11},{10,... | collective-permute-start | bytes 995336 | tf_op jit(solution)/shard_map/ppermute | solution.py:846
  723.7 28.9 %collective-permute-start.79 = (bf16[144,1152]{1,0:T(8,128)(2,1)S(1)}, bf16[144,1152]{1,0:T(8,128)(2,1)S(1)}, u32[]{:S(2)}, u32[]{:S(2)}) collective-permute-start(bf16[144,1152]{1,0:T(8,128)(2,1)S(1)} %get-tuple-element.308), channel_id=1, source_target_pairs={{0,3},{1,0},{2,1},{3,2},{4,7},{5,4},{6,5},{7,6},{8,11},{9,8},{10,9... | collective-permute-start | bytes 995336 | tf_op jit(solution)/shard_map/ppermute | solution.py:846
  (161 other events, 1611.4 us)
Sparse Core Ops, SparseCore 0:
  56.9 168.4 all-gather.3
